TPU v7x, 256 devices: a whole 4x4x8 slice. The times are simulated.
256 devices in a mesh: dp: 32 (over z, x_lo, core), tensor: 8 (over x_hi, y).
Axes of the slice: x: 4 (x_hi: 2, x_lo: 2; x = x_hi * 2 + x_lo), y: 4, z: 8, core: 2. Of those that a mesh axis runs over, the one named last changes fastest.
Arguments:
- tile_rows: bfloat16 [96, 256, 6144], P('dp', 'tensor'), may hold values from -6 to 6
- queries: bfloat16 [96, 256, 3072], P('dp', None, 'tensor'), may hold values from -6 to 6
- keys: bfloat16 [96, 256, 3072], P('dp', None, 'tensor'), may hold values from -6 to 6
- w_value: bfloat16 [6144, 3072], P(None, 'tensor'), may hold values from -0.078125 to 0.078125
- ctx_grad: bfloat16 [64, 256, 3072], P('dp', None, 'tensor'), may hold values from -6 to 6
- move: int32 [32, 3], replicated, may hold values from -1 to 63, as said below
- blocks: int32 [64, 256], P('dp'), may hold values from 0 to 3, never falling along the last dimension, each value on 1 to 128 neighbouring positions
Outputs:
- attended: bfloat16 [64, 256, 3072], P('dp', None, 'tensor')
- tile_grad: bfloat16 [96, 256, 6144], P('dp', 'tensor')
- query_grad: bfloat16 [96, 256, 3072], P('dp', None, 'tensor')
- key_grad: bfloat16 [96, 256, 3072], P('dp', None, 'tensor')
- weight_grad: float32 [6144, 3072], P('dp', 'tensor')
Inputs may be any that keep to these rules, and one draw needn't show every extreme that they name: move[r, j] is the balanced slot r2 * 2 + i of home tile row j of data rank r, or -1 for an empty row. A live row j below 2 keeps slot j on its own rank; a live row from 2 on goes to the data rank 32/2 away; no balanced slot takes two rows.
All inputs are finite; a program needn't handle non-finite values.
Results may differ from a plain program's by a relative error of at most 0.029.
Values may be sent and summed in bfloat16 or wider, within the bound.
No kernel may reach another device: no remote copies, remote signals or barrier semaphores. Data moves between devices by JAX's collectives and lax.ppermute only.
A program may use at most 128 MiB of HBM per device.

v0:
```python
import math

import jax
import jax.numpy as jnp
from jax import lax
from jax.sharding import PartitionSpec as P

HD = 128


masked_score = -1e30


def from_behind(x, axis, by):
    size = lax.axis_size(axis)
    return lax.ppermute(x, axis, [(i, (i + by) % size) for i in range(size)])


def place_rows(own_rows, own_live, arrived, pick_matrix):
    kept = jnp.where(own_live[:, None, None], own_rows, jnp.zeros_like(own_rows))
    landed = jnp.einsum(
        "sj,jtc->stc",
        pick_matrix.astype(own_rows.dtype),
        arrived,
        preferred_element_type=jnp.float32,
    )
    return (kept.astype(jnp.float32) + landed).astype(own_rows.dtype)


def pick_rows(balanced, pick_matrix):
    chosen = jnp.einsum(
        "sj,stc->jtc",
        pick_matrix.astype(balanced.dtype),
        balanced,
        preferred_element_type=jnp.float32,
    )
    return chosen.astype(balanced.dtype)


def home_rows(own_rows, own_live, returned, leaving):
    kept = jnp.where(own_live[:, None, None], own_rows, jnp.zeros_like(own_rows))
    back_part = jnp.where(leaving[:, None, None], returned, jnp.zeros_like(returned))
    return jnp.concatenate([kept, back_part], axis=0)


def shards(tile_rows, queries, keys, w_value, ctx_grad, move, blocks):
    rank_count = lax.axis_size("dp")
    half_ranks = rank_count // 2
    my_rank = lax.axis_index("dp")
    partner = (my_rank + half_ranks) % rank_count
    work_slots = ctx_grad.shape[0]
    tile_len = ctx_grad.shape[1]
    slot_ids = jnp.arange(work_slots, dtype=jnp.int32)
    own_dest = move[my_rank]
    own_live = own_dest[:work_slots] == my_rank * work_slots + slot_ids
    leaving = (own_dest[work_slots:] >= 0) & (own_dest[work_slots:] // work_slots == partner)
    sender_dest = move[partner][work_slots:]
    arriving = (sender_dest >= 0) & (sender_dest // work_slots == my_rank)
    pick_matrix = arriving[None, :] & (
        sender_dest[None, :] - my_rank * work_slots == slot_ids[:, None]
    )

    def outgoing(home_array):
        extra_rows = home_array[work_slots:]
        return jnp.where(leaving[:, None, None], extra_rows, jnp.zeros_like(extra_rows))

    got_rows, got_queries, got_keys = from_behind(
        (outgoing(tile_rows), outgoing(queries), outgoing(keys)), "dp", half_ranks
    )
    rows_bal = place_rows(tile_rows[:work_slots], own_live, got_rows, pick_matrix)
    queries_bal = place_rows(queries[:work_slots], own_live, got_queries, pick_matrix)
    keys_bal = place_rows(keys[:work_slots], own_live, got_keys, pick_matrix)
    heads_local = w_value.shape[1] // HD
    score_scale = 1.0 / math.sqrt(HD)
    values_bal = jnp.einsum(
        "wtd,dc->wtc",
        lax.all_gather(rows_bal, "tensor", axis=1, tiled=True),
        w_value,
        preferred_element_type=jnp.float32,
    ).astype(jnp.bfloat16)
    head_shape = (work_slots, tile_len, heads_local, HD)
    query_heads = queries_bal.reshape(head_shape)
    key_heads = keys_bal.reshape(head_shape)
    value_heads = values_bal.reshape(head_shape)
    grad_heads = ctx_grad.reshape(head_shape)
    scores = (
        jnp.einsum("wqhd,wkhd->whqk", query_heads, key_heads, preferred_element_type=jnp.float32)
        * score_scale
    )
    same_block = blocks[:, None, :, None] == blocks[:, None, None, :]
    scores = jnp.where(same_block, scores, masked_score)
    row_max = jnp.max(scores, axis=-1, keepdims=True)
    raised = jnp.exp(scores - row_max)
    probs = raised / jnp.sum(raised, axis=-1, keepdims=True)
    probs_low = probs.astype(jnp.bfloat16)
    attended = jnp.einsum(
        "whqk,wkhd->wqhd", probs_low, value_heads, preferred_element_type=jnp.float32
    )
    attended = attended.astype(jnp.bfloat16).reshape(work_slots, tile_len, heads_local * HD)
    prob_grad = jnp.einsum(
        "wqhd,wkhd->whqk", grad_heads, value_heads, preferred_element_type=jnp.float32
    )
    value_grad = jnp.einsum(
        "whqk,wqhd->wkhd", probs_low, grad_heads, preferred_element_type=jnp.float32
    )
    value_grad = value_grad.astype(jnp.bfloat16).reshape(work_slots, tile_len, heads_local * HD)
    inner_sum = jnp.sum(prob_grad * probs, axis=-1, keepdims=True)
    score_grad = (probs * (prob_grad - inner_sum) * score_scale).astype(jnp.bfloat16)
    query_bal_grad = jnp.einsum(
        "whqk,wkhd->wqhd", score_grad, key_heads, preferred_element_type=jnp.float32
    )
    query_bal_grad = query_bal_grad.astype(jnp.bfloat16).reshape(
        work_slots, tile_len, heads_local * HD
    )
    key_bal_grad = jnp.einsum(
        "whqk,wqhd->wkhd", score_grad, query_heads, preferred_element_type=jnp.float32
    )
    key_bal_grad = key_bal_grad.astype(jnp.bfloat16).reshape(work_slots, tile_len, heads_local * HD)
    row_terms = jnp.einsum("wtc,dc->wtd", value_grad, w_value, preferred_element_type=jnp.float32)
    rows_grad_bal = lax.psum_scatter(
        row_terms.astype(jnp.bfloat16), "tensor", scatter_dimension=1, tiled=True
    )
    full_rows = lax.all_gather(rows_bal, "tensor", axis=1, tiled=True)
    weight_term = jnp.einsum(
        "wtd,wtc->dc", full_rows, value_grad, preferred_element_type=jnp.float32
    )
    weight_grad = lax.psum_scatter(
        weight_term.astype(jnp.bfloat16), "dp", scatter_dimension=0, tiled=True
    ).astype(jnp.float32)
    back_rows, back_queries, back_keys = from_behind(
        (
            pick_rows(rows_grad_bal, pick_matrix),
            pick_rows(query_bal_grad, pick_matrix),
            pick_rows(key_bal_grad, pick_matrix),
        ),
        "dp",
        half_ranks,
    )
    tile_grad = home_rows(rows_grad_bal, own_live, back_rows, leaving)
    query_grad = home_rows(query_bal_grad, own_live, back_queries, leaving)
    key_grad = home_rows(key_bal_grad, own_live, back_keys, leaving)
    return (attended, tile_grad, query_grad, key_grad, weight_grad)


def solution(mesh):
    placed = (
        P("dp", "tensor", None),
        P("dp", None, "tensor"),
        P("dp", None, "tensor"),
        P(None, "tensor"),
        P("dp", None, "tensor"),
        P(),
        P("dp", None),
    )
    return jax.shard_map(
        shards,
        mesh=mesh,
        in_specs=placed,
        out_specs=(
            P("dp", None, "tensor"),
            P("dp", "tensor", None),
            P("dp", None, "tensor"),
            P("dp", None, "tensor"),
            P("dp", "tensor"),
        ),
        check_vma=False,
    )
```

profile of v0, /device:TPU:1, one launch (start us, length us, event | category | flops | bytes accessed | tf_op | source)
XLA Modules:
  0.0 374.9 jit_solution(7478518751164447113)
XLA Ops:
  7.2 0.9 constant_dynamic-slice_fusion
  8.1 0.5 slice.42
  11.9 1.0 slice_select_fusion
  12.9 7.8 %collective-permute-start = (bf16[1,32,6144]{2,1,0:T(8,128)(2,1)S(1)}, bf16[1,32,6144]{2,1,0:T(8,128)(2,1)S(1)}, u32[]{:S(2)}, u32[]{:S(2)}) collective-permute-start(bf16[1,32,6144]{2,1,0:T(8,128)(2,1)S(1)} %slice_select_fusion), channel_id=1, source_target_pairs={{0,128},{8,136},{16,144},{24,152},{32,160},{40,168},{48,176},{56,1... | collective-permute-start | bytes 1179656 | tf_op jit(solution)/shard_map/ppermute | solution.py:16
  20.7 0.5 slice.40
  25.3 4.8 %collective-permute-done = bf16[1,32,6144]{2,1,0:T(8,128)(2,1)S(1)} collective-permute-done((bf16[1,32,6144]{2,1,0:T(8,128)(2,1)S(1)}, bf16[1,32,6144]{2,1,0:T(8,128)(2,1)S(1)}, u32[]{:S(2)}, u32[]{:S(2)}) %collective-permute-start) | collective-permute-done | bytes 393248 | tf_op jit(solution)/shard_map/ppermute | solution.py:16
  30.1 1.2 add_convert_fusion
  31.4 0.1 copy.69
  31.6 5.7 %collective-permute-start.2 = (bf16[1,256,384]{1,2,0:T(8,128)(2,1)S(1)}, bf16[1,256,384]{1,2,0:T(8,128)(2,1)S(1)}, u32[]{:S(2)}, u32[]{:S(2)}) collective-permute-start(bf16[1,256,384]{1,2,0:T(8,128)(2,1)S(1)} %broadcast_select_fusion.4), channel_id=1, source_target_pairs={{0,128},{8,136},{16,144},{24,152},{32,160},{40,168},{48,176},{56,1... | collective-permute-start | bytes 589832 | tf_op jit(solution)/shard_map/ppermute | solution.py:16
  37.3 0.1 copy.67
  37.5 0.6 collective-permute-start.1
  38.2 0.2 copy.37
  38.4 0.2 copy.66
  38.5 0.2 copy.68
  38.7 0.2 copy-done.3
  38.9 0.1 broadcast_compare_fusion
  39.0 5.7 %collective-permute-done.2 = bf16[1,256,384]{1,2,0:T(8,128)(2,1)S(1)} collective-permute-done((bf16[1,256,384]{1,2,0:T(8,128)(2,1)S(1)}, bf16[1,256,384]{1,2,0:T(8,128)(2,1)S(1)}, u32[]{:S(2)}, u32[]{:S(2)}) %collective-permute-start.2) | collective-permute-done | bytes 196640 | tf_op jit(solution)/shard_map/ppermute | solution.py:16
  44.8 2.4 collective-permute-done.1
  47.2 0.3 add_convert_fusion.1
  47.5 1.9 fusion.32
  49.5 1.8 convolution_convert_fusion.3
  51.3 8.0 %convolution_convert_fusion = bf16[2,256,6144]{2,1,0:T(8,128)(2,1)} fusion(bf16[2,256,384]{1,2,0:T(8,128)(2,1)S(1)} %bitcast.107, bf16[6144,384]{1,0:T(8,128)(2,1)} %param.10), kind=kOutput, calls=%fused_computation.3 | convolution fusion | flops 2419064832 | bytes 11403264 | tf_op jit(solution)/shard_map/wtc,dc->wtd/dot_general | solution.py:119
  59.2 0.2 reduce-scatter.5.cloned.1.call-start
  59.5 75.0 %all-gather.2.cloned.1.call-done = bf16[2,256,6144]{2,1,0:T(8,128)(2,1)} async-done(((bf16[2,32,6144]{2,1,0:T(8,128)(2,1)}), bf16[2,256,6144]{2,1,0:T(8,128)(2,1)}) %all-gather.2.cloned.1.call-update) | async-done | bytes 6291472 | tf_op jit(solution)/shard_map/all_gather | solution.py:77
  134.5 8.4 %bitcast_convert_fusion = bf16[6144,384]{1,0:T(8,128)(2,1)} fusion(bf16[2,256,6144]{2,1,0:T(8,128)(2,1)} %all-gather.2.cloned.1.call-done, bf16[2,256,384]{1,2,0:T(8,128)(2,1)S(1)} %bitcast.108), kind=kOutput, calls=%fused_computation.2 | convolution fusion | flops 2418278400 | bytes 11403264 | tf_op jit(solution)/shard_map/wtd,wtc->dc/dot_general | solution.py:124
  142.9 7.6 %fusion.10 = bf16[2,256,384]{2,1,0:T(8,128)(2,1)S(1)} fusion(bf16[2,256,6144]{2,1,0:T(8,128)(2,1)} %all-gather.2.cloned.1.call-done, bf16[6144,384]{1,0:T(8,128)(2,1)} %param.10), kind=kOutput, calls=%fused_computation.20 | convolution fusion | flops 2416115712 | bytes 11403264 | tf_op jit(solution)/shard_map/wtd,dc->wtc/dot_general | solution.py:75
  150.4 0.2 copy.29
  150.6 1.7 convolution_convert_fusion.4
  152.3 0.9 copy.45
  153.2 0.4 fusion.33
  153.7 2.6 convolution_convert_fusion.2
  156.2 2.6 convolution_convert_fusion.1
  158.8 0.3 multiply_reduce_fusion
  159.1 5.6 %collective-permute-start.4 = (bf16[1,256,384]{1,2,0:T(8,128)(2,1)S(1)}, bf16[1,256,384]{1,2,0:T(8,128)(2,1)S(1)}, u32[]{:S(2)}, u32[]{:S(2)}) collective-permute-start(bf16[1,256,384]{1,2,0:T(8,128)(2,1)S(1)} %bitcast.106), channel_id=1, source_target_pairs={{0,128},{8,136},{16,144},{24,152},{32,160},{40,168},{48,176},{56,1... | collective-permute-start | bytes 589832 | tf_op jit(solution)/shard_map/ppermute | solution.py:16
  164.8 0.1 bitcast_select_fusion
  164.9 3.7 collective-permute-done.4
  168.6 8.0 %collective-permute-done.5 = bf16[1,256,384]{1,2,0:T(8,128)(2,1)S(1)} collective-permute-done((bf16[1,256,384]{1,2,0:T(8,128)(2,1)S(1)}, bf16[1,256,384]{1,2,0:T(8,128)(2,1)S(1)}, u32[]{:S(2)}, u32[]{:S(2)}) %collective-permute-start.5) | collective-permute-done | bytes 196640 | tf_op jit(solution)/shard_map/ppermute | solution.py:16
  176.7 1.1 copy.47
  177.8 1.1 copy.46
  178.9 60.8 %reduce-scatter.3.cloned.1.call-done = bf16[2,32,6144]{2,1,0:T(8,128)(2,1)} async-done(((bf16[2,256,6144]{2,1,0:T(8,128)(2,1)}), bf16[2,32,6144]{2,1,0:T(8,128)(2,1)}) %reduce-scatter.3.cloned.1.call-update) | async-done | bytes 786448 | tf_op jit(solution)/shard_map/reduce_scatter | solution.py:120
  239.7 2.2 fusion.16
  241.9 0.2 copy.75
  242.1 5.5 %collective-permute-start.3 = (bf16[1,32,6144]{2,1,0:T(8,128)(2,1)S(1)}, bf16[1,32,6144]{2,1,0:T(8,128)(2,1)S(1)}, u32[]{:S(2)}, u32[]{:S(2)}) collective-permute-start(bf16[1,32,6144]{2,1,0:T(8,128)(2,1)S(1)} %copy.75), channel_id=1, source_target_pairs={{0,128},{8,136},{16,144},{24,152},{32,160},{40,168},{48,176},{56,1... | collective-permute-start | bytes 1179656 | tf_op jit(solution)/shard_map/ppermute | solution.py:16
  247.7 0.1 broadcast_select_fusion
  247.8 9.5 %collective-permute-done.3 = bf16[1,32,6144]{2,1,0:T(8,128)(2,1)S(1)} collective-permute-done((bf16[1,32,6144]{2,1,0:T(8,128)(2,1)S(1)}, bf16[1,32,6144]{2,1,0:T(8,128)(2,1)S(1)}, u32[]{:S(2)}, u32[]{:S(2)}) %collective-permute-start.3) | collective-permute-done | bytes 393248 | tf_op jit(solution)/shard_map/ppermute | solution.py:16
  257.4 1.1 pad_maximum_fusion
  258.5 108.3 %reduce-scatter.5.cloned.1.call-done = bf16[192,384]{1,0:T(8,128)(2,1)} async-done(((bf16[6144,384]{1,0:T(8,128)(2,1)}), bf16[192,384]{1,0:T(8,128)(2,1)}) %reduce-scatter.5.cloned.1.call-update) | async-done | bytes 147472 | tf_op jit(solution)/shard_map/reduce_scatter | solution.py:127
  366.8 1.6 convert_element_type.109
  (33 shorter events, 0.7 us)
Async XLA Ops:
  7.2 22.9 %copy-start = (bf16[3,32,6144]{2,1,0:T(8,128)(2,1)S(1)}, bf16[3,32,6144]{2,1,0:T(8,128)(2,1)}, u32[]{:S(2)}) copy-start(bf16[3,32,6144]{2,1,0:T(8,128)(2,1)} %param.7) | copy-start | bytes 3538948
  7.2 127.3 %all-gather.2.cloned.1.call-start = ((), (), s32[]{:S(2)}) async-start(), calls=%async_computation.2 | async-start | bytes 7077888 | tf_op jit(solution)/shard_map/all_gather | solution.py:77
  12.9 17.1 %collective-permute-start = (bf16[1,32,6144]{2,1,0:T(8,128)(2,1)S(1)}, bf16[1,32,6144]{2,1,0:T(8,128)(2,1)S(1)}, u32[]{:S(2)}, u32[]{:S(2)}) collective-permute-start(bf16[1,32,6144]{2,1,0:T(8,128)(2,1)S(1)} %slice_select_fusion), channel_id=1, source_target_pairs={{0,128},{8,136},{16,144},{24,152},{32,160},{40,168},{48,176},{56,1... | collective-permute-start | bytes 1179656 | tf_op jit(solution)/shard_map/ppermute | solution.py:16
  30.1 1.3 slice-start
  31.3 6.0 %slice-start.2 = ((bf16[3,256,384]{2,1,0:T(8,128)(2,1)}), bf16[1,256,384]{2,1,0:T(8,128)(2,1)S(1)}, s32[]{:S(2)}) async-start(bf16[3,256,384]{2,1,0:T(8,128)(2,1)} %param.8), calls=%async_computation.7 | async-start | bytes 393216 | tf_op jit(solution)/shard_map/slice | solution.py:64
  31.3 208.4 %reduce-scatter.3.cloned.1.call-start = ((), (), s32[]{:S(2)}) async-start(), calls=%async_computation.3 | async-start | bytes 7077888 | tf_op jit(solution)/shard_map/reduce_scatter | solution.py:120
  31.6 6.6 %copy-start.2 = (bf16[2,256,384]{2,1,0:T(8,128)(2,1)S(1)}, bf16[2,256,384]{2,1,0:T(8,128)(2,1)}, u32[]{:S(2)}) copy-start(bf16[2,256,384]{2,1,0:T(8,128)(2,1)} %param.11) | copy-start | bytes 1179652
  31.6 13.1 %collective-permute-start.2 = (bf16[1,256,384]{1,2,0:T(8,128)(2,1)S(1)}, bf16[1,256,384]{1,2,0:T(8,128)(2,1)S(1)}, u32[]{:S(2)}, u32[]{:S(2)}) collective-permute-start(bf16[1,256,384]{1,2,0:T(8,128)(2,1)S(1)} %broadcast_select_fusion.4), channel_id=1, source_target_pairs={{0,128},{8,136},{16,144},{24,152},{32,160},{40,168},{48,176},{56,1... | collective-permute-start | bytes 589832 | tf_op jit(solution)/shard_map/ppermute | solution.py:16
  37.3 1.0 slice-start.3
  37.5 1.0 slice-start.1
  37.5 9.7 %collective-permute-start.1 = (bf16[1,256,384]{1,2,0:T(8,128)(2,1)S(1)}, bf16[1,256,384]{1,2,0:T(8,128)(2,1)S(1)}, u32[]{:S(2)}, u32[]{:S(2)}) collective-permute-start(bf16[1,256,384]{1,2,0:T(8,128)(2,1)S(1)} %broadcast_select_fusion.5), channel_id=1, source_target_pairs={{0,128},{8,136},{16,144},{24,152},{32,160},{40,168},{48,176},{56,1... | collective-permute-start | bytes 589832 | tf_op jit(solution)/shard_map/ppermute | solution.py:16
  38.2 0.7 copy-start.3
  59.2 307.5 %reduce-scatter.5.cloned.1.call-start = ((), (), s32[]{:S(2)}) async-start(), calls=%async_computation.4 | async-start | bytes 4866048 | tf_op jit(solution)/shard_map/reduce_scatter | solution.py:127
  159.1 9.5 %collective-permute-start.4 = (bf16[1,256,384]{1,2,0:T(8,128)(2,1)S(1)}, bf16[1,256,384]{1,2,0:T(8,128)(2,1)S(1)}, u32[]{:S(2)}, u32[]{:S(2)}) collective-permute-start(bf16[1,256,384]{1,2,0:T(8,128)(2,1)S(1)} %bitcast.106), channel_id=1, source_target_pairs={{0,128},{8,136},{16,144},{24,152},{32,160},{40,168},{48,176},{56,1... | collective-permute-start | bytes 589832 | tf_op jit(solution)/shard_map/ppermute | solution.py:16
  164.7 11.9 %collective-permute-start.5 = (bf16[1,256,384]{1,2,0:T(8,128)(2,1)S(1)}, bf16[1,256,384]{1,2,0:T(8,128)(2,1)S(1)}, u32[]{:S(2)}, u32[]{:S(2)}) collective-permute-start(bf16[1,256,384]{1,2,0:T(8,128)(2,1)S(1)} %bitcast.105), channel_id=1, source_target_pairs={{0,128},{8,136},{16,144},{24,152},{32,160},{40,168},{48,176},{56,1... | collective-permute-start | bytes 589832 | tf_op jit(solution)/shard_map/ppermute | solution.py:16
  239.7 8.0 %copy-start.1 = (bf16[2,32,6144]{2,1,0:T(8,128)(2,1)S(1)}, bf16[2,32,6144]{2,1,0:T(8,128)(2,1)}, u32[]{:S(2)}) copy-start(bf16[2,32,6144]{2,1,0:T(8,128)(2,1)} %reduce-scatter.3.cloned.1.call-done) | copy-start | bytes 2359300
  242.1 15.2 %collective-permute-start.3 = (bf16[1,32,6144]{2,1,0:T(8,128)(2,1)S(1)}, bf16[1,32,6144]{2,1,0:T(8,128)(2,1)S(1)}, u32[]{:S(2)}, u32[]{:S(2)}) collective-permute-start(bf16[1,32,6144]{2,1,0:T(8,128)(2,1)S(1)} %copy.75), channel_id=1, source_target_pairs={{0,128},{8,136},{16,144},{24,152},{32,160},{40,168},{48,176},{56,1... | collective-permute-start | bytes 1179656 | tf_op jit(solution)/shard_map/ppermute | solution.py:16
Sparse Core Ops, SparseCore 0:
  31.5 102.9 all-gather.1
  138.6 101.0 reduce-scatter.2
  242.2 124.4 reduce-scatter.4
where the time goes:
time: 379 us; the launch traced here: 375 us
  waiting for transfers between devices  278 us (73%)
  matrix products  37 us (10%)
  starting transfers between devices  25.7 us (7%)
  between operations  21.2 us (6%)
  local copies, waits for them, and re-layouts  6.47 us (2%)
  other arithmetic  6.26 us (2%)
    reduce_scatter x1, waiting for transfers between devices, shards(): lax.psum_scatter(weight_term.astype(jnp.bfloat16), 'dp', scatter_dimensio...  108 us
    all_gather x1, waiting for transfers between devices, shards(): lax.all_gather(rows_bal, 'tensor', axis=1, tiled=True)  75 us
    reduce_scatter x1, waiting for transfers between devices, shards(): lax.psum_scatter(row_terms.astype(jnp.bfloat16), 'tensor', scatter_dimens...  60.8 us
    ppermute x6, waiting for transfers between devices, from_behind(): return lax.ppermute(x, axis, [(i, (i + by) % size) for i in range(size)])  34.2 us
    ppermute x6, starting transfers between devices, from_behind(): return lax.ppermute(x, axis, [(i, (i + by) % size) for i in range(size)])  25.4 us
    dot_general x1, matrix products, shards(): jnp.einsum('wtd,wtc->dc', full_rows, value_grad, preferred_element_type=j...  8.35 us
    dot_general x1, matrix products, shards(): jnp.einsum('wtc,dc->wtd', value_grad, w_value, preferred_element_type=jnp...  7.95 us
  transfers between devices with their start and end apart: 9, of which 9 were waited for; matrix products, arithmetic and copies ran while one was open for 12% of the time, Pallas kernels for 0%

commit v1 on v0

v1 whole, which is shorter than its diff:
```python
import functools
import math

import jax
import jax.numpy as jnp
from jax import lax
from jax.experimental import pallas as pl
from jax.experimental.pallas import tpu as pltpu
from jax.sharding import PartitionSpec as P

HD = 128
N_TENSOR = 8
N_Z = 8
masked_score = -1e30
BF = jnp.bfloat16
F32 = jnp.float32
VMEM_LIMIT = 48 * 1024 * 1024


def swap(x, d):
    return lax.ppermute(x, "tensor", [(i, i ^ d) for i in range(N_TENSOR)])


def dp_perm(x, move):
    pairs = []
    for z in range(N_Z):
        for xl in range(2):
            for c in range(2):
                z2, xl2, c2 = move(z, xl, c)
                pairs.append(((z * 2 + xl) * 2 + c, ((z2 % N_Z) * 2 + xl2 % 2) * 2 + c2 % 2))
    return lax.ppermute(x, "dp", pairs)


def to_partner(x):
    return dp_perm(x, lambda z, xl, c: (z + N_Z // 2, xl, c))


def along_z(x, by):
    return dp_perm(x, lambda z, xl, c: (z + by, xl, c))


def other_core(x):
    return dp_perm(x, lambda z, xl, c: (z, xl, c + 1))


def other_xl(x):
    return dp_perm(x, lambda z, xl, c: (z, xl + 1, c))


def gather_chunks(own, a, b):
    c = [None] * N_TENSOR
    c[0] = own
    c[4] = swap(own, 4)
    c[a] = swap(own, a)
    c[b] = swap(own, b)
    c[4 ^ b] = swap(c[b], 4)
    c[2] = swap(c[a], b)
    c[4 ^ a] = swap(c[4], a)
    c[6] = swap(c[4 ^ b], a)
    return c


def scatter_chunks(t, a, b):
    u4b = t[4 ^ b] + swap(t[6], a)
    ua = t[a] + swap(t[2], b)
    u4 = t[4] + swap(t[4 ^ a], a)
    ub = t[b] + swap(u4b, 4)
    parts = (t[0], swap(u4, 4), swap(ua, a), swap(ub, b))
    return sum(p.astype(F32) for p in parts).astype(BF)


def value_kernel(*refs):
    chunks, w_ref, out_ref, acc = refs[:8], refs[8], refs[9], refs[10]
    step = pl.program_id(0)
    rows = jnp.concatenate([c[...] for c in chunks], axis=0)
    part = jnp.dot(rows, w_ref[...], preferred_element_type=F32)

    @pl.when(step == 0)
    def _():
        acc[...] = part

    @pl.when(step > 0)
    def _():
        acc[...] += part

    @pl.when(step == pl.num_programs(0) - 1)
    def _():
        out_ref[...] = acc[...].astype(BF)


def project_values(chunks, w):
    n, d = chunks[0].shape
    cols = w.shape[1]
    blk = 1024
    return pl.pallas_call(
        value_kernel,
        grid=(d // blk,),
        in_specs=[pl.BlockSpec((n, blk), lambda i: (0, i))] * 8
        + [pl.BlockSpec((blk, cols), lambda i: (i, 0))],
        out_specs=pl.BlockSpec((8 * n, cols), lambda i: (0, 0)),
        out_shape=jax.ShapeDtypeStruct((8 * n, cols), BF),
        scratch_shapes=[pltpu.VMEM((8 * n, cols), F32)],
        compiler_params=pltpu.CompilerParams(vmem_limit_bytes=VMEM_LIMIT),
        cost_estimate=pl.CostEstimate(
            flops=2 * 8 * n * d * cols, bytes_accessed=2 * d * (8 * n + cols), transcendentals=0
        ),
        name="project_values",
    )(*chunks, w)


def attend_kernel(me_ref, q_ref, k_ref, v_ref, g_ref, bq_ref, bk_ref,
                  att_ref, vg_ref, dq_ref, dk_ref, v_abs, vg_abs):
    me = me_ref[0]
    n = q_ref.shape[0] // N_TENSOR
    scale = 1.0 / math.sqrt(HD)
    for d in range(N_TENSOR):
        at = pl.multiple_of((me ^ d) * n, n)
        v_abs[pl.ds(at, n), :] = v_ref[d * n:(d + 1) * n, :]
    q, k, g, v = q_ref[...], k_ref[...], g_ref[...], v_abs[...]
    nt = (((1,), (1,)), ((), ()))
    tn = (((0,), (0,)), ((), ()))
    s = lax.dot_general(q, k, nt, preferred_element_type=F32) * scale
    s = jnp.where(bq_ref[...] == bk_ref[...], s, masked_score)
    e = jnp.exp(s - jnp.max(s, axis=-1, keepdims=True))
    p = e / jnp.sum(e, axis=-1, keepdims=True)
    low = p.astype(BF)
    att_ref[...] = jnp.dot(low, v, preferred_element_type=F32).astype(BF)
    pg = lax.dot_general(g, v, nt, preferred_element_type=F32)
    vg_abs[...] = lax.dot_general(low, g, tn, preferred_element_type=F32).astype(BF)
    inner = jnp.sum(pg * p, axis=-1, keepdims=True)
    sg = (p * (pg - inner) * scale).astype(BF)
    dq_ref[...] = jnp.dot(sg, k, preferred_element_type=F32).astype(BF)
    dk_ref[...] = lax.dot_general(sg, q, tn, preferred_element_type=F32).astype(BF)
    for d in range(N_TENSOR):
        at = pl.multiple_of((me ^ d) * n, n)
        vg_ref[d * n:(d + 1) * n, :] = vg_abs[pl.ds(at, n), :]


def attend(me, q, k, v_rel, g, block_ids):
    t, cols = q.shape
    head = pl.BlockSpec((t, HD), lambda h, m: (0, h))
    return pl.pallas_call(
        attend_kernel,
        grid_spec=pltpu.PrefetchScalarGridSpec(
            num_scalar_prefetch=1,
            grid=(cols // HD,),
            in_specs=[head] * 4
            + [
                pl.BlockSpec((t, 1), lambda h, m: (0, 0)),
                pl.BlockSpec((1, t), lambda h, m: (0, 0)),
            ],
            out_specs=[head] * 4,
            scratch_shapes=[pltpu.VMEM((t, HD), BF)] * 2,
        ),
        out_shape=[jax.ShapeDtypeStruct((t, cols), BF)] * 4,
        compiler_params=pltpu.CompilerParams(vmem_limit_bytes=VMEM_LIMIT),
        cost_estimate=pl.CostEstimate(
            flops=12 * t * t * cols, bytes_accessed=16 * t * cols, transcendentals=3 * t * t
        ),
        name="attend",
    )(me, q, k, v_rel, g, block_ids.reshape(t, 1), block_ids.reshape(1, t))


def terms_kernel(vg_ref, w_ref, *outs):
    n = outs[0].shape[0]
    part = lax.dot_general(
        vg_ref[...], w_ref[...], (((1,), (1,)), ((), ())), preferred_element_type=F32
    ).astype(BF)
    for d in range(N_TENSOR):
        outs[d][...] = part[d * n:(d + 1) * n]


def row_terms(vg_rel, w):
    t, cols = vg_rel.shape
    d = w.shape[0]
    n = t // N_TENSOR
    blk = 1024
    return pl.pallas_call(
        terms_kernel,
        grid=(d // blk,),
        in_specs=[
            pl.BlockSpec((t, cols), lambda i: (0, 0)),
            pl.BlockSpec((blk, cols), lambda i: (i, 0)),
        ],
        out_specs=[pl.BlockSpec((n, blk), lambda i: (0, i))] * N_TENSOR,
        out_shape=[jax.ShapeDtypeStruct((n, d), BF)] * N_TENSOR,
        compiler_params=pltpu.CompilerParams(vmem_limit_bytes=VMEM_LIMIT),
        cost_estimate=pl.CostEstimate(
            flops=2 * t * d * cols, bytes_accessed=2 * d * (t + cols), transcendentals=0
        ),
        name="row_terms",
    )(vg_rel, w)


def weight_kernel(where_ref, *refs):
    chunks, vga_ref, vgb_ref, keep_ref, send_ref = refs[:16], refs[16], refs[17], refs[18], refs[19]
    rows = jnp.concatenate([c[...] for c in chunks], axis=0)
    vg = jnp.concatenate([vga_ref[...], vgb_ref[...]], axis=0)
    part = lax.dot_general(rows, vg, (((0,), (0,)), ((), ())), preferred_element_type=F32)
    part = part.astype(BF)
    half = part.shape[0] // 2
    mine = where_ref[1] == 0
    keep_ref[0] = jnp.where(mine, part[:half], part[half:])
    send_ref[0] = jnp.where(mine, part[half:], part[:half])


def weight_terms(where, chunks, vg_a, vg_b):
    n, d = chunks[0].shape
    t, cols = vg_a.shape
    blk = d // 16
    full = pl.BlockSpec((t, cols), lambda i, wh: (0, 0))
    out = pl.BlockSpec((1, blk // 2, cols), lambda i, wh: (i, 0, 0))
    return pl.pallas_call(
        weight_kernel,
        grid_spec=pltpu.PrefetchScalarGridSpec(
            num_scalar_prefetch=1,
            grid=(16,),
            in_specs=[
                pl.BlockSpec((n, blk), lambda i, wh: (0, lax.rem(wh[0] * 2 + i, 16)))
            ] * 16 + [full, full],
            out_specs=[out, out],
        ),
        out_shape=[jax.ShapeDtypeStruct((16, blk // 2, cols), BF)] * 2,
        compiler_params=pltpu.CompilerParams(vmem_limit_bytes=VMEM_LIMIT),
        cost_estimate=pl.CostEstimate(
            flops=2 * 2 * t * d * cols, bytes_accessed=2 * d * (2 * t + cols), transcendentals=0
        ),
        name="weight_terms",
    )(where, *chunks, vg_a, vg_b)


def weight_sum(keep, sent, xl):
    got = other_core(sent)
    u = keep + got
    u = [u[2 * i:2 * i + 2] for i in range(N_Z)]
    up = along_z(u[4][:1], 1)
    down = along_z(u[4][1:], -1)
    up = along_z(jnp.concatenate([u[3][:1] + up, u[3][1:]], axis=0), 1)
    down = along_z(jnp.concatenate([u[5][:1], u[5][1:] + down], axis=0), -1)
    up = along_z(u[2] + up, 1)
    down = along_z(u[6] + down, -1)
    up = along_z(u[1] + up, 1)
    down = along_z(u[7] + down, -1)
    total = u[0].astype(F32) + up.astype(F32) + down.astype(F32)
    mine = lax.dynamic_index_in_dim(total, xl, 0, keepdims=False)
    theirs = lax.dynamic_index_in_dim(total, 1 - xl, 0, keepdims=False)
    return mine + other_xl(theirs.astype(BF)).astype(F32)


def shards(tile_rows, queries, keys, w_value, ctx_grad, move, blocks):
    rank_count = lax.axis_size("dp")
    half_ranks = rank_count // 2
    my_rank = lax.axis_index("dp")
    partner = (my_rank + half_ranks) % rank_count
    me = lax.axis_index("tensor").astype(jnp.int32).reshape(1)
    z, xl, core = my_rank // 4, (my_rank // 2) % 2, my_rank % 2
    where = jnp.stack([z, core]).astype(jnp.int32)

    own_dest = move[my_rank]
    live = own_dest[:2] == my_rank * 2 + jnp.arange(2, dtype=jnp.int32)
    leaving = (own_dest[2] >= 0) & (own_dest[2] // 2 == partner)
    sender_dest = move[partner, 2]
    arriving = (sender_dest >= 0) & (sender_dest // 2 == my_rank)
    slot_b = jnp.where(arriving, sender_dest % 2, jnp.where(live[0], 1, 0)).astype(jnp.int32)
    slot_a = 1 - slot_b
    live_a, live_b = live[slot_a], live[slot_b]

    def own(home, slot):
        return lax.dynamic_index_in_dim(home, slot, 0, keepdims=False)

    def kept(home):
        row = own(home, slot_a)
        return jnp.where(live_a, row, jnp.zeros_like(row))

    def second(home, got):
        row = own(home, slot_b)
        return jnp.where(arriving, got, jnp.where(live_b, row, jnp.zeros_like(row)))

    got_rows = to_partner(tile_rows[2])
    rows_a = gather_chunks(kept(tile_rows), 1, 3)
    rows_b = gather_chunks(second(tile_rows, got_rows), 3, 1)
    late_q, late_k, _ = lax.optimization_barrier((queries[2], keys[2], got_rows))
    q_b, k_b = second(queries, to_partner(late_q)), second(keys, to_partner(late_k))
    q_a, k_a = kept(queries), kept(keys)

    values_a = project_values(rows_a, w_value)
    att_a, vg_a, dq_a, dk_a = attend(
        me, q_a, k_a, values_a, own(ctx_grad, slot_a), own(blocks, slot_a))
    values_b = project_values(rows_b, w_value)
    att_b, vg_b, dq_b, dk_b = attend(
        me, q_b, k_b, values_b, own(ctx_grad, slot_b), own(blocks, slot_b))

    grad_b = scatter_chunks(row_terms(vg_b, w_value), 3, 1)
    grad_a = scatter_chunks(row_terms(vg_a, w_value), 1, 3)
    keep, sent = weight_terms(where, rows_a + rows_b, vg_a, vg_b)
    weight_grad = weight_sum(keep, sent, xl)

    def by_slot(of_a, of_b):
        first = slot_a == 0
        return [jnp.where(first, of_a, of_b), jnp.where(first, of_b, of_a)]

    def home(of_a, of_b):
        back = to_partner(of_b)
        here = by_slot(of_a, of_b)
        rows = [jnp.where(live[0], here[0], 0), jnp.where(live[1], here[1], 0),
                jnp.where(leaving, back, 0)]
        return jnp.stack(rows).astype(BF)

    attended = jnp.stack(by_slot(att_a, att_b))
    return (attended, home(grad_a, grad_b), home(dq_a, dq_b), home(dk_a, dk_b), weight_grad)


def solution(mesh):
    placed = (
        P("dp", "tensor", None),
        P("dp", None, "tensor"),
        P("dp", None, "tensor"),
        P(None, "tensor"),
        P("dp", None, "tensor"),
        P(),
        P("dp", None),
    )
    return jax.shard_map(
        shards,
        mesh=mesh,
        in_specs=placed,
        out_specs=(
            P("dp", None, "tensor"),
            P("dp", "tensor", None),
            P("dp", None, "tensor"),
            P("dp", None, "tensor"),
            P("dp", "tensor"),
        ),
        check_vma=False,
    )
```

time: 379 us -> 252 us (0.66)
  the two profiles are of different devices: /device:TPU:1 before, /device:TPU:96 now
where the time goes in v1:
time: 252 us; the launch traced here: 250 us
  starting transfers between devices  87.6 us (35%)
  waiting for transfers between devices  78.8 us (31%)
  Pallas kernels  43.8 us (17%)
  other arithmetic  22 us (9%)
  local copies, waits for them, and re-layouts  10.2 us (4%)
  between operations  7.82 us (3%)
    ppermute x16, waiting for transfers between devices, dp_perm(): return lax.ppermute(x, 'dp', pairs)  54.8 us
    ppermute x16, starting transfers between devices, dp_perm(): return lax.ppermute(x, 'dp', pairs)  47.3 us
    ppermute x28, starting transfers between devices, swap(): return lax.ppermute(x, 'tensor', [(i, i ^ d) for i in range(N_TENSOR)])  40.3 us
    ppermute x28, waiting for transfers between devices, swap(): return lax.ppermute(x, 'tensor', [(i, i ^ d) for i in range(N_TENSOR)])  23.9 us
    pallas_call x1, Pallas kernels, weight_terms(): pl.pallas_call(weight_kernel, grid_spec=pltpu.PrefetchScalarGridSpec(num_...  13.6 us
    pallas_call x2, Pallas kernels, row_terms(): pl.pallas_call(terms_kernel, grid=(d // blk,), in_specs=[pl.BlockSpec((t,...  12.1 us
    pallas_call x2, Pallas kernels, project_values(): pl.pallas_call(value_kernel, grid=(d // blk,), in_specs=[pl.BlockSpec((n,...  11.8 us
    pallas_call x2, Pallas kernels, attend(): pl.pallas_call(attend_kernel, grid_spec=pltpu.PrefetchScalarGridSpec(num_...  6.29 us
  transfers between devices with their start and end apart: 44, of which 15 were waited for; matrix products, arithmetic and copies ran while one was open for 10% of the time, Pallas kernels for 8%

profile of v1, /device:TPU:96, one launch (start us, length us, event | category | flops | bytes accessed | tf_op | source)
XLA Modules:
  0.0 250.3 jit_solution(16904081808981460159)
XLA Ops:
  6.7 1.8 select_bitcast_fusion.3
  8.5 4.6 %collective-permute-start.7 = (bf16[32,6144]{1,0:T(8,128)(2,1)S(1)}, bf16[32,6144]{1,0:T(8,128)(2,1)S(1)}, u32[]{:S(2)}, u32[]{:S(2)}) collective-permute-start(bf16[32,6144]{1,0:T(8,128)(2,1)S(1)} %get-tuple-element.71), channel_id=1, source_target_pairs={{0,128},{8,136},{16,144},{24,152},{32,160},{40,168},{48,176},{56,1... | collective-permute-start | bytes 1179656 | tf_op jit(solution)/shard_map/ppermute | solution.py:31
  13.1 3.0 %collective-permute-start.2 = (bf16[32,6144]{1,0:T(8,128)(2,1)S(1)}, bf16[32,6144]{1,0:T(8,128)(2,1)S(1)}, u32[]{:S(2)}, u32[]{:S(2)}) collective-permute-start(bf16[32,6144]{1,0:T(8,128)(2,1)S(1)} %get-tuple-element.70.refs_0_), channel_id=1, source_target_pairs={{0,3},{1,2},{2,1},{3,0},{4,7},{5,6},{6,5},{7,4},{8,11},{9,10},{10,... | collective-permute-start | bytes 1179656 | tf_op jit(solution)/shard_map/ppermute | solution.py:21
  16.2 3.0 %collective-permute-start.3 = (bf16[32,6144]{1,0:T(8,128)(2,1)S(1)}, bf16[32,6144]{1,0:T(8,128)(2,1)S(1)}, u32[]{:S(2)}, u32[]{:S(2)}) collective-permute-start(bf16[32,6144]{1,0:T(8,128)(2,1)S(1)} %get-tuple-element.70.refs_0_), channel_id=1, source_target_pairs={{0,4},{1,5},{2,6},{3,7},{4,0},{5,1},{6,2},{7,3},{8,12},{9,13},{10,... | collective-permute-start | bytes 1179656 | tf_op jit(solution)/shard_map/ppermute | solution.py:21
  19.3 2.4 select_bitcast_fusion.12
  21.6 5.8 %collective-permute-done.7 = bf16[32,6144]{1,0:T(8,128)(2,1)S(1)} collective-permute-done((bf16[32,6144]{1,0:T(8,128)(2,1)S(1)}, bf16[32,6144]{1,0:T(8,128)(2,1)S(1)}, u32[]{:S(2)}, u32[]{:S(2)}) %collective-permute-start.7) | collective-permute-done | bytes 393248 | tf_op jit(solution)/shard_map/ppermute | solution.py:31
  27.5 1.7 bitcast_select_fusion.refs_0_.refs_8_
  29.2 1.7 collective-permute-start.10
  30.8 1.4 select_bitcast_fusion.13
  32.2 5.5 %collective-permute-start.9 = (bf16[256,384]{1,0:T(8,128)(2,1)S(1)}, bf16[256,384]{1,0:T(8,128)(2,1)S(1)}, u32[]{:S(2)}, u32[]{:S(2)}) collective-permute-start(bf16[256,384]{1,0:T(8,128)(2,1)S(1)} %get-tuple-element.35), channel_id=1, source_target_pairs={{0,128},{8,136},{16,144},{24,152},{32,160},{40,168},{48,176},{56,1... | collective-permute-start | bytes 589832 | tf_op jit(solution)/shard_map/ppermute | solution.py:31
  38.1 2.2 collective-permute-start.11
  40.3 3.0 %collective-permute-start.13 = (bf16[32,6144]{1,0:T(8,128)(2,1)S(1)}, bf16[32,6144]{1,0:T(8,128)(2,1)S(1)}, u32[]{:S(2)}, u32[]{:S(2)}) collective-permute-start(bf16[32,6144]{1,0:T(8,128)(2,1)S(1)} %bitcast_select_fusion.refs_0_.refs_8_), channel_id=1, source_target_pairs={{0,4},{1,5},{2,6},{3,7},{4,0},{5,1},{6,2},{7,3},{8,12},{9,13},{10,... | collective-permute-start | bytes 1179656 | tf_op jit(solution)/shard_map/ppermute | solution.py:21
  44.3 3.0 %collective-permute-start.5 = (bf16[32,6144]{1,0:T(8,128)(2,1)S(1)}, bf16[32,6144]{1,0:T(8,128)(2,1)S(1)}, u32[]{:S(2)}, u32[]{:S(2)}) collective-permute-start(bf16[32,6144]{1,0:T(8,128)(2,1)S(1)} %collective-permute-done.2.refs_3_), channel_id=1, source_target_pairs={{0,4},{1,5},{2,6},{3,7},{4,0},{5,1},{6,2},{7,3},{8,12},{9,13},{10,... | collective-permute-start | bytes 1179656 | tf_op jit(solution)/shard_map/ppermute | solution.py:21
  47.3 7.0 %collective-permute-done.8 = bf16[256,384]{1,0:T(8,128)(2,1)S(1)} collective-permute-done((bf16[256,384]{1,0:T(8,128)(2,1)S(1)}, bf16[256,384]{1,0:T(8,128)(2,1)S(1)}, u32[]{:S(2)}, u32[]{:S(2)}) %collective-permute-start.8) | collective-permute-done | bytes 196640 | tf_op jit(solution)/shard_map/ppermute | solution.py:31
  54.3 2.2 collective-permute-start.1
  56.5 3.1 %collective-permute-start.14 = (bf16[32,6144]{1,0:T(8,128)(2,1)S(1)}, bf16[32,6144]{1,0:T(8,128)(2,1)}, u32[]{:S(2)}, u32[]{:S(2)}) collective-permute-start(bf16[32,6144]{1,0:T(8,128)(2,1)S(1)} %collective-permute-done.10.refs_1_.refs_9_), channel_id=1, source_target_pairs={{0,4},{1,5},{2,6},{3,7},{4,0},{5,1},{6,2},{7,3},{8,12},{9,13},{10,... | collective-permute-start | bytes 1179656 | tf_op jit(solution)/shard_map/ppermute | solution.py:21
  63.9 1.3 collective-permute-start.12
  66.5 2.0 collective-permute-done.14.refs_5_.refs_13_
  69.5 1.7 bitcast_select_fusion.1.k_ref
  71.2 1.7 bitcast_select_fusion.2.q_ref
  74.0 8.4 %collective-permute-done.6.refs_6_ = bf16[32,6144]{1,0:T(8,128)(2,1)S(1)} collective-permute-done((bf16[32,6144]{1,0:T(8,128)(2,1)S(1)}, bf16[32,6144]{1,0:T(8,128)(2,1)S(1)}, u32[]{:S(2)}, u32[]{:S(2)}) %collective-permute-start.6) | collective-permute-done | bytes 393248 | tf_op jit(solution)/shard_map/ppermute | solution.py:21
  82.5 5.7 %project_values.2.v_ref = bf16[256,384]{1,0:T(8,128)(2,1)S(1)} custom-call(bf16[32,6144]{1,0:T(8,128)(2,1)S(1)} %get-tuple-element.70.refs_0_, bf16[32,6144]{1,0:T(8,128)(2,1)S(1)} %collective-permute-done.refs_1_, bf16[32,6144]{1,0:T(8,128)(2,1)} %collective-permute-done.1.refs_2_, bf16[32,6144]{1,0:T(8,128)(2,1)S(1)} %collective-permute-done.2.refs_3_, ...), custom_call_target="tpu_custom_call" | custom-call | flops 1207959552 | bytes 7864320 | tf_op jit(solution)/shard_map/project_values/pallas_call | solution.py:95
  88.2 3.1 %attend.2 = (bf16[256,384]{1,0:T(8,128)(2,1)S(1)}, bf16[256,384]{1,0:T(8,128)(2,1)S(1)}, bf16[256,384]{1,0:T(8,128)(2,1)S(1)}, bf16[256,384]{1,0:T(8,128)(2,1)S(1)}) custom-call(s32[1]{0:T(128)} %bitcast.2.me_ref, bf16[256,384]{1,0:T(8,128)(2,1)S(1)} %copy-done.18, bf16[256,384]{1,0:T(8,128)(2,1)S(1)} %copy-done.17, ...), custom_call_target="tpu_custom_call" | custom-call | flops 301989888 | bytes 1572864 | tf_op jit(solution)/shard_map/attend/pallas_call | solution.py:142
  92.1 6.1 %project_values.3.v_ref = bf16[256,384]{1,0:T(8,128)(2,1)S(1)} custom-call(bf16[32,6144]{1,0:T(8,128)(2,1)S(1)} %bitcast_select_fusion.refs_0_.refs_8_, bf16[32,6144]{1,0:T(8,128)(2,1)S(1)} %collective-permute-done.10.refs_1_.refs_9_, bf16[32,6144]{1,0:T(8,128)(2,1)S(1)} %collective-permute-done.12.refs_2_.refs_10_, ...), custom_call_target="tpu_custom_call" | custom-call | flops 1207959552 | bytes 7864320 | tf_op jit(solution)/shard_map/project_values/pallas_call | solution.py:95
  98.2 3.1 %attend.3 = (bf16[256,384]{1,0:T(8,128)(2,1)S(1)}, bf16[256,384]{1,0:T(8,128)(2,1)S(1)}, bf16[256,384]{1,0:T(8,128)(2,1)S(1)}, bf16[256,384]{1,0:T(8,128)(2,1)S(1)}) custom-call(s32[1]{0:T(128)} %bitcast.2.me_ref, bf16[256,384]{1,0:T(8,128)(2,1)S(1)} %bitcast_select_fusion.2.q_ref, bf16[256,384]{1,0:T(8,128)(2,1)S(1)} %bitcast_select_fusion.1.k_ref, ...), custom_call_target="tpu_custom_call" | custom-call | flops 301989888 | bytes 1572864 | tf_op jit(solution)/shard_map/attend/pallas_call | solution.py:142
  102.8 13.6 %weight_terms.1 = (bf16[16,192,384]{2,1,0:T(8,128)(2,1)}, bf16[16,192,384]{2,1,0:T(8,128)(2,1)}) custom-call(s32[2]{0:T(128)S(1)} %pad_add_fusion.where_ref, bf16[32,6144]{1,0:T(8,128)(2,1)S(1)} %get-tuple-element.70.refs_0_, bf16[32,6144]{1,0:T(8,128)(2,1)S(1)} %collective-permute-done.refs_1_, bf16[32,6144]{1,0:T(8,128)(2,1)} %collective-permute-done.1.refs_2_, ...), custom_call_target="tpu_custom_call" | custom-call | flops 2415919104 | bytes 11010048 | tf_op jit(solution)/shard_map/weight_terms/pallas_call | solution.py:213
  116.5 6.5 %row_terms.2 = (bf16[32,6144]{1,0:T(8,128)(2,1)S(1)}, bf16[32,6144]{1,0:T(8,128)(2,1)S(1)}, bf16[32,6144]{1,0:T(8,128)(2,1)S(1)}, bf16[32,6144]{1,0:T(8,128)(2,1...) custom-call(bf16[256,384]{1,0:T(8,128)(2,1)S(1)} %get-tuple-element., ...), custom_call_target="tpu_custom_call" | custom-call | flops 1207959552 | bytes 7864320 | tf_op jit(solution)/shard_map/row_terms/pallas_call | solution.py:178
  128.9 1.5 collective-permute-start.19
  130.8 6.0 %collective-permute-start.33 = (bf16[256,384]{1,0:T(8,128)(2,1)S(1)}, bf16[256,384]{1,0:T(8,128)(2,1)S(1)}, u32[]{:S(2)}, u32[]{:S(2)}) collective-permute-start(bf16[256,384]{1,0:T(8,128)(2,1)S(1)} %copy-done.8), channel_id=1, source_target_pairs={{0,128},{8,136},{16,144},{24,152},{32,160},{40,168},{48,176},{56,1... | collective-permute-start | bytes 589832 | tf_op jit(solution)/shard_map/ppermute | solution.py:31
  137.5 5.6 %row_terms.3 = (bf16[32,6144]{1,0:T(8,128)(2,1)S(1)}, bf16[32,6144]{1,0:T(8,128)(2,1)S(1)}, bf16[32,6144]{1,0:T(8,128)(2,1)S(1)}, bf16[32,6144]{1,0:T(8,128)(2,1...) custom-call(bf16[256,384]{1,0:T(8,128)(2,1)S(1)} %copy-done.4, ...), custom_call_target="tpu_custom_call" | custom-call | flops 1207959552 | bytes 7864320 | tf_op jit(solution)/shard_map/row_terms/pallas_call | solution.py:178
  143.2 2.3 collective-permute-start.28
  146.8 1.3 collective-permute-start.32
  150.0 2.5 add.164
  152.6 3.9 %collective-permute-done.28 = bf16[32,6144]{1,0:T(8,128)(2,1)S(1)} collective-permute-done((bf16[32,6144]{1,0:T(8,128)(2,1)S(1)}, bf16[32,6144]{1,0:T(8,128)(2,1)S(1)}, u32[]{:S(2)}, u32[]{:S(2)}) %collective-permute-start.28) | collective-permute-done | bytes 393248 | tf_op jit(solution)/shard_map/ppermute | solution.py:21
  157.1 5.0 %collective-permute-done.35 = bf16[1,192,384]{2,1,0:T(8,128)(2,1)S(1)} collective-permute-done((bf16[1,192,384]{2,1,0:T(8,128)(2,1)S(1)}, bf16[1,192,384]{2,1,0:T(8,128)(2,1)S(1)}, u32[]{:S(2)}, u32[]{:S(2)}) %collective-permute-start.35) | collective-permute-done | bytes 147488 | tf_op jit(solution)/shard_map/ppermute | solution.py:31
  162.8 3.1 %collective-permute-start.29 = (bf16[32,6144]{1,0:T(8,128)(2,1)S(1)}, bf16[32,6144]{1,0:T(8,128)(2,1)S(1)}, u32[]{:S(2)}, u32[]{:S(2)}) collective-permute-start(bf16[32,6144]{1,0:T(8,128)(2,1)S(1)} %add.160), channel_id=1, source_target_pairs={{0,4},{1,5},{2,6},{3,7},{4,0},{5,1},{6,2},{7,3},{8,12},{9,13},{10,... | collective-permute-start | bytes 1179656 | tf_op jit(solution)/shard_map/ppermute | solution.py:21
  165.9 7.4 %collective-permute-start.36 = (bf16[2,192,384]{2,1,0:T(8,128)(2,1)S(1)}, bf16[2,192,384]{2,1,0:T(8,128)(2,1)S(1)}, u32[]{:S(2)}, u32[]{:S(2)}) collective-permute-start(bf16[2,192,384]{2,1,0:T(8,128)(2,1)S(1)} %pad_maximum_fusion.4), channel_id=1, source_target_pairs={{0,32},{8,40},{16,48},{24,56},{32,64},{40,72},{48,80},{56,88},{64,... | collective-permute-start | bytes 884744 | tf_op jit(solution)/shard_map/ppermute | solution.py:31
  177.3 5.3 %collective-permute-done.29 = bf16[32,6144]{1,0:T(8,128)(2,1)S(1)} collective-permute-done((bf16[32,6144]{1,0:T(8,128)(2,1)S(1)}, bf16[32,6144]{1,0:T(8,128)(2,1)S(1)}, u32[]{:S(2)}, u32[]{:S(2)}) %collective-permute-start.29) | collective-permute-done | bytes 393248 | tf_op jit(solution)/shard_map/ppermute | solution.py:21
  183.3 2.3 collective-permute-start.27
  186.8 4.3 %collective-permute-start.40 = (bf16[2,192,384]{2,1,0:T(8,128)(2,1)S(1)}, bf16[2,192,384]{2,1,0:T(8,128)(2,1)S(1)}, u32[]{:S(2)}, u32[]{:S(2)}) collective-permute-start(bf16[2,192,384]{2,1,0:T(8,128)(2,1)S(1)} %pad_maximum_fusion.5), channel_id=1, source_target_pairs={{0,224},{8,232},{16,240},{24,248},{32,0},{40,8},{48,16},{56,24},{6... | collective-permute-start | bytes 884744 | tf_op jit(solution)/shard_map/ppermute | solution.py:31
  191.1 2.2 collective-permute-done.25
  193.3 10.3 %collective-permute-start.37 = (bf16[2,192,384]{2,1,0:T(8,128)(2,1)S(1)}, bf16[2,192,384]{2,1,0:T(8,128)(2,1)S(1)}, u32[]{:S(2)}, u32[]{:S(2)}) collective-permute-start(bf16[2,192,384]{2,1,0:T(8,128)(2,1)S(1)} %slice_add_fusion.2), channel_id=1, source_target_pairs={{0,32},{8,40},{16,48},{24,56},{32,64},{40,72},{48,80},{56,88},{64,... | collective-permute-start | bytes 884744 | tf_op jit(solution)/shard_map/ppermute | solution.py:31
  204.1 1.6 collective-permute-start.31
  205.6 18.5 %collective-permute-done.37 = bf16[2,192,384]{2,1,0:T(8,128)(2,1)S(1)} collective-permute-done((bf16[2,192,384]{2,1,0:T(8,128)(2,1)S(1)}, bf16[2,192,384]{2,1,0:T(8,128)(2,1)S(1)}, u32[]{:S(2)}, u32[]{:S(2)}) %collective-permute-start.37) | collective-permute-done | bytes 294944 | tf_op jit(solution)/shard_map/ppermute | solution.py:31
  224.9 4.2 %collective-permute-start.38 = (bf16[2,192,384]{2,1,0:T(8,128)(2,1)S(1)}, bf16[2,192,384]{2,1,0:T(8,128)(2,1)S(1)}, u32[]{:S(2)}, u32[]{:S(2)}) collective-permute-start(bf16[2,192,384]{2,1,0:T(8,128)(2,1)S(1)} %get-tuple-element.64), channel_id=1, source_target_pairs={{0,32},{8,40},{16,48},{24,56},{32,64},{40,72},{48,80},{56,88},{64,... | collective-permute-start | bytes 884744 | tf_op jit(solution)/shard_map/ppermute | solution.py:31
  229.1 6.9 %collective-permute-done.41 = bf16[2,192,384]{2,1,0:T(8,128)(2,1)S(1)} collective-permute-done((bf16[2,192,384]{2,1,0:T(8,128)(2,1)S(1)}, bf16[2,192,384]{2,1,0:T(8,128)(2,1)S(1)}, u32[]{:S(2)}, u32[]{:S(2)}) %collective-permute-start.41) | collective-permute-done | bytes 294944 | tf_op jit(solution)/shard_map/ppermute | solution.py:31
  236.3 7.9 %collective-permute-done.42 = bf16[2,192,384]{2,1,0:T(8,128)(2,1)S(1)} collective-permute-done((bf16[2,192,384]{2,1,0:T(8,128)(2,1)S(1)}, bf16[2,192,384]{2,1,0:T(8,128)(2,1)S(1)}, u32[]{:S(2)}, u32[]{:S(2)}) %collective-permute-start.42) | collective-permute-done | bytes 294944 | tf_op jit(solution)/shard_map/ppermute | solution.py:31
  246.7 2.8 %collective-permute-done.43 = bf16[192,384]{1,0:T(8,128)(2,1)S(1)} collective-permute-done((bf16[192,384]{1,0:T(8,128)(2,1)S(1)}, bf16[192,384]{1,0:T(8,128)(2,1)S(1)}, u32[]{:S(2)}, u32[]{:S(2)}) %collective-permute-start.43) | collective-permute-done | bytes 147488 | tf_op jit(solution)/shard_map/ppermute | solution.py:31
  (149 shorter events, 32.9 us)
Async XLA Ops:
  0.6 30.2 %copy-start.23 = (bf16[3,256,384]{2,1,0:T(8,128)(2,1)S(1)}, bf16[3,256,384]{2,1,0:T(8,128)(2,1)}, u32[]{:S(2)}) copy-start(bf16[3,256,384]{2,1,0:T(8,128)(2,1)} %param.8) | copy-start | bytes 1769476
  8.5 19.0 %collective-permute-start.7 = (bf16[32,6144]{1,0:T(8,128)(2,1)S(1)}, bf16[32,6144]{1,0:T(8,128)(2,1)S(1)}, u32[]{:S(2)}, u32[]{:S(2)}) collective-permute-start(bf16[32,6144]{1,0:T(8,128)(2,1)S(1)} %get-tuple-element.71), channel_id=1, source_target_pairs={{0,128},{8,136},{16,144},{24,152},{32,160},{40,168},{48,176},{56,1... | collective-permute-start | bytes 1179656 | tf_op jit(solution)/shard_map/ppermute | solution.py:31
  13.1 24.6 %collective-permute-start.2 = (bf16[32,6144]{1,0:T(8,128)(2,1)S(1)}, bf16[32,6144]{1,0:T(8,128)(2,1)S(1)}, u32[]{:S(2)}, u32[]{:S(2)}) collective-permute-start(bf16[32,6144]{1,0:T(8,128)(2,1)S(1)} %get-tuple-element.70.refs_0_), channel_id=1, source_target_pairs={{0,3},{1,2},{2,1},{3,0},{4,7},{5,6},{6,5},{7,4},{8,11},{9,10},{10,... | collective-permute-start | bytes 1179656 | tf_op jit(solution)/shard_map/ppermute | solution.py:21
  16.1 22.0 %collective-permute-start = (bf16[32,6144]{1,0:T(8,128)(2,1)S(1)}, bf16[32,6144]{1,0:T(8,128)(2,1)S(1)}, u32[]{:S(2)}, u32[]{:S(2)}) collective-permute-start(bf16[32,6144]{1,0:T(8,128)(2,1)S(1)} %get-tuple-element.70.refs_0_), channel_id=1, source_target_pairs={{0,1},{1,0},{2,3},{3,2},{4,5},{5,4},{6,7},{7,6},{8,9},{9,8},{10,11... | collective-permute-start | bytes 1179656 | tf_op jit(solution)/shard_map/ppermute | solution.py:21
  16.2 24.1 %collective-permute-start.3 = (bf16[32,6144]{1,0:T(8,128)(2,1)S(1)}, bf16[32,6144]{1,0:T(8,128)(2,1)S(1)}, u32[]{:S(2)}, u32[]{:S(2)}) collective-permute-start(bf16[32,6144]{1,0:T(8,128)(2,1)S(1)} %get-tuple-element.70.refs_0_), channel_id=1, source_target_pairs={{0,4},{1,5},{2,6},{3,7},{4,0},{5,1},{6,2},{7,3},{8,12},{9,13},{10,... | collective-permute-start | bytes 1179656 | tf_op jit(solution)/shard_map/ppermute | solution.py:21
  29.2 27.3 %collective-permute-start.10 = (bf16[32,6144]{1,0:T(8,128)(2,1)S(1)}, bf16[32,6144]{1,0:T(8,128)(2,1)S(1)}, u32[]{:S(2)}, u32[]{:S(2)}) collective-permute-start(bf16[32,6144]{1,0:T(8,128)(2,1)S(1)} %bitcast_select_fusion.refs_0_.refs_8_), channel_id=1, source_target_pairs={{0,1},{1,0},{2,3},{3,2},{4,5},{5,4},{6,7},{7,6},{8,9},{9,8},{10,11... | collective-permute-start | bytes 1179656 | tf_op jit(solution)/shard_map/ppermute | solution.py:21
  32.2 12.1 %collective-permute-start.9 = (bf16[256,384]{1,0:T(8,128)(2,1)S(1)}, bf16[256,384]{1,0:T(8,128)(2,1)S(1)}, u32[]{:S(2)}, u32[]{:S(2)}) collective-permute-start(bf16[256,384]{1,0:T(8,128)(2,1)S(1)} %get-tuple-element.35), channel_id=1, source_target_pairs={{0,128},{8,136},{16,144},{24,152},{32,160},{40,168},{48,176},{56,1... | collective-permute-start | bytes 589832 | tf_op jit(solution)/shard_map/ppermute | solution.py:31
  37.7 16.6 %collective-permute-start.8 = (bf16[256,384]{1,0:T(8,128)(2,1)S(1)}, bf16[256,384]{1,0:T(8,128)(2,1)S(1)}, u32[]{:S(2)}, u32[]{:S(2)}) collective-permute-start(bf16[256,384]{1,0:T(8,128)(2,1)S(1)} %get-tuple-element.34), channel_id=1, source_target_pairs={{0,128},{8,136},{16,144},{24,152},{32,160},{40,168},{48,176},{56,1... | collective-permute-start | bytes 589832 | tf_op jit(solution)/shard_map/ppermute | solution.py:31
  38.1 24.9 %collective-permute-start.11 = (bf16[32,6144]{1,0:T(8,128)(2,1)S(1)}, bf16[32,6144]{1,0:T(8,128)(2,1)S(1)}, u32[]{:S(2)}, u32[]{:S(2)}) collective-permute-start(bf16[32,6144]{1,0:T(8,128)(2,1)S(1)} %bitcast_select_fusion.refs_0_.refs_8_), channel_id=1, source_target_pairs={{0,3},{1,2},{2,1},{3,0},{4,7},{5,6},{6,5},{7,4},{8,11},{9,10},{10,... | collective-permute-start | bytes 1179656 | tf_op jit(solution)/shard_map/ppermute | solution.py:21
  40.3 23.5 %collective-permute-start.13 = (bf16[32,6144]{1,0:T(8,128)(2,1)S(1)}, bf16[32,6144]{1,0:T(8,128)(2,1)S(1)}, u32[]{:S(2)}, u32[]{:S(2)}) collective-permute-start(bf16[32,6144]{1,0:T(8,128)(2,1)S(1)} %bitcast_select_fusion.refs_0_.refs_8_), channel_id=1, source_target_pairs={{0,4},{1,5},{2,6},{3,7},{4,0},{5,1},{6,2},{7,3},{8,12},{9,13},{10,... | collective-permute-start | bytes 1179656 | tf_op jit(solution)/shard_map/ppermute | solution.py:21
  44.3 20.9 %collective-permute-start.5 = (bf16[32,6144]{1,0:T(8,128)(2,1)S(1)}, bf16[32,6144]{1,0:T(8,128)(2,1)S(1)}, u32[]{:S(2)}, u32[]{:S(2)}) collective-permute-start(bf16[32,6144]{1,0:T(8,128)(2,1)S(1)} %collective-permute-done.2.refs_3_), channel_id=1, source_target_pairs={{0,4},{1,5},{2,6},{3,7},{4,0},{5,1},{6,2},{7,3},{8,12},{9,13},{10,... | collective-permute-start | bytes 1179656 | tf_op jit(solution)/shard_map/ppermute | solution.py:21
  54.3 12.0 %collective-permute-start.1 = (bf16[32,6144]{1,0:T(8,128)(2,1)S(1)}, bf16[32,6144]{1,0:T(8,128)(2,1)}, u32[]{:S(2)}, u32[]{:S(2)}) collective-permute-start(bf16[32,6144]{1,0:T(8,128)(2,1)S(1)} %collective-permute-done.refs_1_), channel_id=1, source_target_pairs={{0,3},{1,2},{2,1},{3,0},{4,7},{5,6},{6,5},{7,4},{8,11},{9,10},{10,... | collective-permute-start | bytes 1179656 | tf_op jit(solution)/shard_map/ppermute | solution.py:21
  56.5 12.0 %collective-permute-start.14 = (bf16[32,6144]{1,0:T(8,128)(2,1)S(1)}, bf16[32,6144]{1,0:T(8,128)(2,1)}, u32[]{:S(2)}, u32[]{:S(2)}) collective-permute-start(bf16[32,6144]{1,0:T(8,128)(2,1)S(1)} %collective-permute-done.10.refs_1_.refs_9_), channel_id=1, source_target_pairs={{0,4},{1,5},{2,6},{3,7},{4,0},{5,1},{6,2},{7,3},{8,12},{9,13},{10,... | collective-permute-start | bytes 1179656 | tf_op jit(solution)/shard_map/ppermute | solution.py:21
  63.1 10.9 %collective-permute-start.4 = (bf16[32,6144]{1,0:T(8,128)(2,1)S(1)}, bf16[32,6144]{1,0:T(8,128)(2,1)S(1)}, u32[]{:S(2)}, u32[]{:S(2)}) collective-permute-start(bf16[32,6144]{1,0:T(8,128)(2,1)S(1)} %collective-permute-done.3.refs_4_), channel_id=1, source_target_pairs={{0,1},{1,0},{2,3},{3,2},{4,5},{5,4},{6,7},{7,6},{8,9},{9,8},{10,11... | collective-permute-start | bytes 1179656 | tf_op jit(solution)/shard_map/ppermute | solution.py:21
  63.9 28.2 %collective-permute-start.12 = (bf16[32,6144]{1,0:T(8,128)(2,1)S(1)}, bf16[32,6144]{1,0:T(8,128)(2,1)S(1)}, u32[]{:S(2)}, u32[]{:S(2)}) collective-permute-start(bf16[32,6144]{1,0:T(8,128)(2,1)S(1)} %collective-permute-done.11.refs_3_.refs_11_), channel_id=1, source_target_pairs={{0,1},{1,0},{2,3},{3,2},{4,5},{5,4},{6,7},{7,6},{8,9},{9,8},{10,11... | collective-permute-start | bytes 1179656 | tf_op jit(solution)/shard_map/ppermute | solution.py:21
  65.2 26.8 %collective-permute-start.16 = (bf16[32,6144]{1,0:T(8,128)(2,1)S(1)}, bf16[32,6144]{1,0:T(8,128)(2,1)S(1)}, u32[]{:S(2)}, u32[]{:S(2)}) collective-permute-start(bf16[32,6144]{1,0:T(8,128)(2,1)S(1)} %collective-permute-done.13.refs_4_.refs_12_), channel_id=1, source_target_pairs={{0,3},{1,2},{2,1},{3,0},{4,7},{5,6},{6,5},{7,4},{8,11},{9,10},{10,... | collective-permute-start | bytes 1179656 | tf_op jit(solution)/shard_map/ppermute | solution.py:21
  66.3 16.2 %collective-permute-start.6 = (bf16[32,6144]{1,0:T(8,128)(2,1)S(1)}, bf16[32,6144]{1,0:T(8,128)(2,1)S(1)}, u32[]{:S(2)}, u32[]{:S(2)}) collective-permute-start(bf16[32,6144]{1,0:T(8,128)(2,1)S(1)} %collective-permute-done.5.refs_7_), channel_id=1, source_target_pairs={{0,1},{1,0},{2,3},{3,2},{4,5},{5,4},{6,7},{7,6},{8,9},{9,8},{10,11... | collective-permute-start | bytes 1179656 | tf_op jit(solution)/shard_map/ppermute | solution.py:21
  68.5 23.6 %collective-permute-start.15 = (bf16[32,6144]{1,0:T(8,128)(2,1)}, bf16[32,6144]{1,0:T(8,128)(2,1)S(1)}, u32[]{:S(2)}, u32[]{:S(2)}) collective-permute-start(bf16[32,6144]{1,0:T(8,128)(2,1)} %collective-permute-done.14.refs_5_.refs_13_), channel_id=1, source_target_pairs={{0,3},{1,2},{2,1},{3,0},{4,7},{5,6},{6,5},{7,4},{8,11},{9,10},{10,... | collective-permute-start | bytes 1179656 | tf_op jit(solution)/shard_map/ppermute | solution.py:21
  116.4 20.4 %copy-start.6 = (bf16[256,384]{1,0:T(8,128)(2,1)S(1)}, bf16[256,384]{1,0:T(8,128)(2,1)}, u32[]{:S(2)}) copy-start(bf16[256,384]{1,0:T(8,128)(2,1)} %copy-done.5) | copy-start | bytes 589828
  116.4 20.3 %copy-start.10 = (bf16[256,384]{1,0:T(8,128)(2,1)S(1)}, bf16[256,384]{1,0:T(8,128)(2,1)}, u32[]{:S(2)}) copy-start(bf16[256,384]{1,0:T(8,128)(2,1)} %copy-done.9) | copy-start | bytes 589828
  116.4 21.1 %copy-start.4 = (bf16[256,384]{1,0:T(8,128)(2,1)S(1)}, bf16[256,384]{1,0:T(8,128)(2,1)}, u32[]{:S(2)}) copy-start(bf16[256,384]{1,0:T(8,128)(2,1)} %copy-done.3) | copy-start | bytes 589828
  116.4 33.5 %collective-permute-start.34 = (bf16[16,192,384]{2,1,0:T(8,128)(2,1)}, bf16[16,192,384]{2,1,0:T(8,128)(2,1)}, u32[]{:S(2)}, u32[]{:S(2)}) collective-permute-start(bf16[16,192,384]{2,1,0:T(8,128)(2,1)} %get-tuple-element.60), channel_id=1, source_target_pairs={{0,8},{8,0},{16,24},{24,16},{32,40},{40,32},{48,56},{56,48},{64,72... | collective-permute-start | bytes 7077896 | tf_op jit(solution)/shard_map/ppermute | solution.py:31
  123.8 19.4 %collective-permute-start.17 = (bf16[32,6144]{1,0:T(8,128)(2,1)}, bf16[32,6144]{1,0:T(8,128)(2,1)}, u32[]{:S(2)}, u32[]{:S(2)}) collective-permute-start(bf16[32,6144]{1,0:T(8,128)(2,1)} %get-tuple-element.40), channel_id=1, source_target_pairs={{0,1},{1,0},{2,3},{3,2},{4,5},{5,4},{6,7},{7,6},{8,9},{9,8},{10,11... | collective-permute-start | bytes 1179656 | tf_op jit(solution)/shard_map/ppermute | solution.py:21
  128.9 17.9 %collective-permute-start.19 = (bf16[32,6144]{1,0:T(8,128)(2,1)}, bf16[32,6144]{1,0:T(8,128)(2,1)S(1)}, u32[]{:S(2)}, u32[]{:S(2)}) collective-permute-start(bf16[32,6144]{1,0:T(8,128)(2,1)} %copy-done.21), channel_id=1, source_target_pairs={{0,3},{1,2},{2,1},{3,0},{4,7},{5,6},{6,5},{7,4},{8,11},{9,10},{10,... | collective-permute-start | bytes 1179656 | tf_op jit(solution)/shard_map/ppermute | solution.py:21
  130.4 17.8 %collective-permute-start.21 = (bf16[32,6144]{1,0:T(8,128)(2,1)S(1)}, bf16[32,6144]{1,0:T(8,128)(2,1)S(1)}, u32[]{:S(2)}, u32[]{:S(2)}) collective-permute-start(bf16[32,6144]{1,0:T(8,128)(2,1)S(1)} %get-tuple-element.45), channel_id=1, source_target_pairs={{0,1},{1,0},{2,3},{3,2},{4,5},{5,4},{6,7},{7,6},{8,9},{9,8},{10,11... | collective-permute-start | bytes 1179656 | tf_op jit(solution)/shard_map/ppermute | solution.py:21
  130.8 21.7 %collective-permute-start.33 = (bf16[256,384]{1,0:T(8,128)(2,1)S(1)}, bf16[256,384]{1,0:T(8,128)(2,1)S(1)}, u32[]{:S(2)}, u32[]{:S(2)}) collective-permute-start(bf16[256,384]{1,0:T(8,128)(2,1)S(1)} %copy-done.8), channel_id=1, source_target_pairs={{0,128},{8,136},{16,144},{24,152},{32,160},{40,168},{48,176},{56,1... | collective-permute-start | bytes 589832 | tf_op jit(solution)/shard_map/ppermute | solution.py:31
  143.2 13.4 %collective-permute-start.28 = (bf16[32,6144]{1,0:T(8,128)(2,1)S(1)}, bf16[32,6144]{1,0:T(8,128)(2,1)S(1)}, u32[]{:S(2)}, u32[]{:S(2)}) collective-permute-start(bf16[32,6144]{1,0:T(8,128)(2,1)S(1)} %get-tuple-element.54), channel_id=1, source_target_pairs={{0,3},{1,2},{2,1},{3,0},{4,7},{5,6},{6,5},{7,4},{8,11},{9,10},{10,... | collective-permute-start | bytes 1179656 | tf_op jit(solution)/shard_map/ppermute | solution.py:21
  146.8 15.9 %collective-permute-start.32 = (bf16[256,384]{1,0:T(8,128)(2,1)S(1)}, bf16[256,384]{1,0:T(8,128)(2,1)S(1)}, u32[]{:S(2)}, u32[]{:S(2)}) collective-permute-start(bf16[256,384]{1,0:T(8,128)(2,1)S(1)} %copy-done.6), channel_id=1, source_target_pairs={{0,128},{8,136},{16,144},{24,152},{32,160},{40,168},{48,176},{56,1... | collective-permute-start | bytes 589832 | tf_op jit(solution)/shard_map/ppermute | solution.py:31
  148.2 17.7 %collective-permute-start.24 = (bf16[32,6144]{1,0:T(8,128)(2,1)S(1)}, bf16[32,6144]{1,0:T(8,128)(2,1)S(1)}, u32[]{:S(2)}, u32[]{:S(2)}) collective-permute-start(bf16[32,6144]{1,0:T(8,128)(2,1)S(1)} %get-tuple-element.49), channel_id=1, source_target_pairs={{0,3},{1,2},{2,1},{3,0},{4,7},{5,6},{6,5},{7,4},{8,11},{9,10},{10,... | collective-permute-start | bytes 1179656 | tf_op jit(solution)/shard_map/ppermute | solution.py:21
  149.9 23.4 %collective-permute-start.26 = (bf16[32,6144]{1,0:T(8,128)(2,1)S(1)}, bf16[32,6144]{1,0:T(8,128)(2,1)S(1)}, u32[]{:S(2)}, u32[]{:S(2)}) collective-permute-start(bf16[32,6144]{1,0:T(8,128)(2,1)S(1)} %get-tuple-element.51), channel_id=1, source_target_pairs={{0,1},{1,0},{2,3},{3,2},{4,5},{5,4},{6,7},{7,6},{8,9},{9,8},{10,11... | collective-permute-start | bytes 1179656 | tf_op jit(solution)/shard_map/ppermute | solution.py:21
  152.5 9.7 %collective-permute-start.35 = (bf16[1,192,384]{2,1,0:T(8,128)(2,1)S(1)}, bf16[1,192,384]{2,1,0:T(8,128)(2,1)S(1)}, u32[]{:S(2)}, u32[]{:S(2)}) collective-permute-start(bf16[1,192,384]{2,1,0:T(8,128)(2,1)S(1)} %slice.96), channel_id=1, source_target_pairs={{0,32},{8,40},{16,48},{24,56},{32,64},{40,72},{48,80},{56,88},{64,... | collective-permute-start | bytes 442376 | tf_op jit(solution)/shard_map/ppermute | solution.py:31
  156.6 26.7 %collective-permute-start.18 = (bf16[32,6144]{1,0:T(8,128)(2,1)S(1)}, bf16[32,6144]{1,0:T(8,128)(2,1)S(1)}, u32[]{:S(2)}, u32[]{:S(2)}) collective-permute-start(bf16[32,6144]{1,0:T(8,128)(2,1)S(1)} %add.149), channel_id=1, source_target_pairs={{0,4},{1,5},{2,6},{3,7},{4,0},{5,1},{6,2},{7,3},{8,12},{9,13},{10,... | collective-permute-start | bytes 1179656 | tf_op jit(solution)/shard_map/ppermute | solution.py:21
  162.1 14.2 %collective-permute-start.22 = (bf16[32,6144]{1,0:T(8,128)(2,1)S(1)}, bf16[32,6144]{1,0:T(8,128)(2,1)S(1)}, u32[]{:S(2)}, u32[]{:S(2)}) collective-permute-start(bf16[32,6144]{1,0:T(8,128)(2,1)S(1)} %add.153), channel_id=1, source_target_pairs={{0,4},{1,5},{2,6},{3,7},{4,0},{5,1},{6,2},{7,3},{8,12},{9,13},{10,... | collective-permute-start | bytes 1179656 | tf_op jit(solution)/shard_map/ppermute | solution.py:21
  162.8 19.9 %collective-permute-start.29 = (bf16[32,6144]{1,0:T(8,128)(2,1)S(1)}, bf16[32,6144]{1,0:T(8,128)(2,1)S(1)}, u32[]{:S(2)}, u32[]{:S(2)}) collective-permute-start(bf16[32,6144]{1,0:T(8,128)(2,1)S(1)} %add.160), channel_id=1, source_target_pairs={{0,4},{1,5},{2,6},{3,7},{4,0},{5,1},{6,2},{7,3},{8,12},{9,13},{10,... | collective-permute-start | bytes 1179656 | tf_op jit(solution)/shard_map/ppermute | solution.py:21
  165.9 20.7 %collective-permute-start.36 = (bf16[2,192,384]{2,1,0:T(8,128)(2,1)S(1)}, bf16[2,192,384]{2,1,0:T(8,128)(2,1)S(1)}, u32[]{:S(2)}, u32[]{:S(2)}) collective-permute-start(bf16[2,192,384]{2,1,0:T(8,128)(2,1)S(1)} %pad_maximum_fusion.4), channel_id=1, source_target_pairs={{0,32},{8,40},{16,48},{24,56},{32,64},{40,72},{48,80},{56,88},{64,... | collective-permute-start | bytes 884744 | tf_op jit(solution)/shard_map/ppermute | solution.py:31
  173.3 12.2 %collective-permute-start.39 = (bf16[1,192,384]{2,1,0:T(8,128)(2,1)S(1)}, bf16[1,192,384]{2,1,0:T(8,128)(2,1)S(1)}, u32[]{:S(2)}, u32[]{:S(2)}) collective-permute-start(bf16[1,192,384]{2,1,0:T(8,128)(2,1)S(1)} %get-tuple-element.67), channel_id=1, source_target_pairs={{0,224},{8,232},{16,240},{24,248},{32,0},{40,8},{48,16},{56,24},{6... | collective-permute-start | bytes 442376 | tf_op jit(solution)/shard_map/ppermute | solution.py:31
  176.3 10.4 %collective-permute-start.20 = (bf16[32,6144]{1,0:T(8,128)(2,1)S(1)}, bf16[32,6144]{1,0:T(8,128)(2,1)S(1)}, u32[]{:S(2)}, u32[]{:S(2)}) collective-permute-start(bf16[32,6144]{1,0:T(8,128)(2,1)S(1)} %add.151), channel_id=1, source_target_pairs={{0,1},{1,0},{2,3},{3,2},{4,5},{5,4},{6,7},{7,6},{8,9},{9,8},{10,11... | collective-permute-start | bytes 1179656 | tf_op jit(solution)/shard_map/ppermute | solution.py:21
  182.7 10.6 %collective-permute-start.25 = (bf16[32,6144]{1,0:T(8,128)(2,1)S(1)}, bf16[32,6144]{1,0:T(8,128)(2,1)S(1)}, u32[]{:S(2)}, u32[]{:S(2)}) collective-permute-start(bf16[32,6144]{1,0:T(8,128)(2,1)S(1)} %add.156), channel_id=1, source_target_pairs={{0,4},{1,5},{2,6},{3,7},{4,0},{5,1},{6,2},{7,3},{8,12},{9,13},{10,... | collective-permute-start | bytes 1179656 | tf_op jit(solution)/shard_map/ppermute | solution.py:21
  183.3 20.3 %collective-permute-start.27 = (bf16[32,6144]{1,0:T(8,128)(2,1)S(1)}, bf16[32,6144]{1,0:T(8,128)(2,1)S(1)}, u32[]{:S(2)}, u32[]{:S(2)}) collective-permute-start(bf16[32,6144]{1,0:T(8,128)(2,1)S(1)} %add.158), channel_id=1, source_target_pairs={{0,3},{1,2},{2,1},{3,0},{4,7},{5,6},{6,5},{7,4},{8,11},{9,10},{10,... | collective-permute-start | bytes 1179656 | tf_op jit(solution)/shard_map/ppermute | solution.py:21
  185.6 18.0 %collective-permute-start.23 = (bf16[32,6144]{1,0:T(8,128)(2,1)S(1)}, bf16[32,6144]{1,0:T(8,128)(2,1)S(1)}, u32[]{:S(2)}, u32[]{:S(2)}) collective-permute-start(bf16[32,6144]{1,0:T(8,128)(2,1)S(1)} %add.154), channel_id=1, source_target_pairs={{0,3},{1,2},{2,1},{3,0},{4,7},{5,6},{6,5},{7,4},{8,11},{9,10},{10,... | collective-permute-start | bytes 1179656 | tf_op jit(solution)/shard_map/ppermute | solution.py:21
  186.6 16.9 %collective-permute-start.30 = (bf16[32,6144]{1,0:T(8,128)(2,1)S(1)}, bf16[32,6144]{1,0:T(8,128)(2,1)S(1)}, u32[]{:S(2)}, u32[]{:S(2)}) collective-permute-start(bf16[32,6144]{1,0:T(8,128)(2,1)S(1)} %add.161), channel_id=1, source_target_pairs={{0,1},{1,0},{2,3},{3,2},{4,5},{5,4},{6,7},{7,6},{8,9},{9,8},{10,11... | collective-permute-start | bytes 1179656 | tf_op jit(solution)/shard_map/ppermute | solution.py:21
  186.8 18.9 %collective-permute-start.40 = (bf16[2,192,384]{2,1,0:T(8,128)(2,1)S(1)}, bf16[2,192,384]{2,1,0:T(8,128)(2,1)S(1)}, u32[]{:S(2)}, u32[]{:S(2)}) collective-permute-start(bf16[2,192,384]{2,1,0:T(8,128)(2,1)S(1)} %pad_maximum_fusion.5), channel_id=1, source_target_pairs={{0,224},{8,232},{16,240},{24,248},{32,0},{40,8},{48,16},{56,24},{6... | collective-permute-start | bytes 884744 | tf_op jit(solution)/shard_map/ppermute | solution.py:31
  193.3 30.8 %collective-permute-start.37 = (bf16[2,192,384]{2,1,0:T(8,128)(2,1)S(1)}, bf16[2,192,384]{2,1,0:T(8,128)(2,1)S(1)}, u32[]{:S(2)}, u32[]{:S(2)}) collective-permute-start(bf16[2,192,384]{2,1,0:T(8,128)(2,1)S(1)} %slice_add_fusion.2), channel_id=1, source_target_pairs={{0,32},{8,40},{16,48},{24,56},{32,64},{40,72},{48,80},{56,88},{64,... | collective-permute-start | bytes 884744 | tf_op jit(solution)/shard_map/ppermute | solution.py:31
  204.1 32.2 %collective-permute-start.31 = (bf16[32,6144]{1,0:T(8,128)(2,1)S(1)}, bf16[32,6144]{1,0:T(8,128)(2,1)S(1)}, u32[]{:S(2)}, u32[]{:S(2)}) collective-permute-start(bf16[32,6144]{1,0:T(8,128)(2,1)S(1)} %get-tuple-element.63), channel_id=1, source_target_pairs={{0,128},{8,136},{16,144},{24,152},{32,160},{40,168},{48,176},{56,1... | collective-permute-start | bytes 1179656 | tf_op jit(solution)/shard_map/ppermute | solution.py:31
  224.2 11.9 %collective-permute-start.41 = (bf16[2,192,384]{2,1,0:T(8,128)(2,1)S(1)}, bf16[2,192,384]{2,1,0:T(8,128)(2,1)S(1)}, u32[]{:S(2)}, u32[]{:S(2)}) collective-permute-start(bf16[2,192,384]{2,1,0:T(8,128)(2,1)S(1)} %get-tuple-element.65), channel_id=1, source_target_pairs={{0,224},{8,232},{16,240},{24,248},{32,0},{40,8},{48,16},{56,24},{6... | collective-permute-start | bytes 884744 | tf_op jit(solution)/shard_map/ppermute | solution.py:31
  224.9 11.4 %collective-permute-start.38 = (bf16[2,192,384]{2,1,0:T(8,128)(2,1)S(1)}, bf16[2,192,384]{2,1,0:T(8,128)(2,1)S(1)}, u32[]{:S(2)}, u32[]{:S(2)}) collective-permute-start(bf16[2,192,384]{2,1,0:T(8,128)(2,1)S(1)} %get-tuple-element.64), channel_id=1, source_target_pairs={{0,32},{8,40},{16,48},{24,56},{32,64},{40,72},{48,80},{56,88},{64,... | collective-permute-start | bytes 884744 | tf_op jit(solution)/shard_map/ppermute | solution.py:31
  236.1 8.0 %collective-permute-start.42 = (bf16[2,192,384]{2,1,0:T(8,128)(2,1)S(1)}, bf16[2,192,384]{2,1,0:T(8,128)(2,1)S(1)}, u32[]{:S(2)}, u32[]{:S(2)}) collective-permute-start(bf16[2,192,384]{2,1,0:T(8,128)(2,1)S(1)} %slice_add_fusion.1), channel_id=1, source_target_pairs={{0,224},{8,232},{16,240},{24,248},{32,0},{40,8},{48,16},{56,24},{6... | collective-permute-start | bytes 884744 | tf_op jit(solution)/shard_map/ppermute | solution.py:31
  244.3 5.2 %collective-permute-start.43 = (bf16[192,384]{1,0:T(8,128)(2,1)S(1)}, bf16[192,384]{1,0:T(8,128)(2,1)S(1)}, u32[]{:S(2)}, u32[]{:S(2)}) collective-permute-start(bf16[192,384]{1,0:T(8,128)(2,1)S(1)} %fusion), channel_id=1, source_target_pairs={{0,16},{8,24},{16,0},{24,8},{32,48},{40,56},{48,32},{56,40},{64,80... | collective-permute-start | bytes 442376 | tf_op jit(solution)/shard_map/ppermute | solution.py:31
  (23 other events, 177.3 us)

commit v2 on v1

v2 whole, which is shorter than its diff:
```python
import functools
import math

import jax
import jax.numpy as jnp
from jax import lax
from jax.experimental import pallas as pl
from jax.experimental.pallas import tpu as pltpu
from jax.sharding import PartitionSpec as P

HD = 128
N_TENSOR = 8
N_Z = 8
masked_score = -1e30
BF = jnp.bfloat16
F32 = jnp.float32
VMEM_LIMIT = 8 * 1024 * 1024
BLK = 1024
SMALL = pl.CostEstimate(flops=1, bytes_accessed=1, transcendentals=0)


def swap(x, d):
    return lax.ppermute(x, "tensor", [(i, i ^ d) for i in range(N_TENSOR)])


def dp_perm(x, move):
    pairs = []
    for z in range(N_Z):
        for xl in range(2):
            for c in range(2):
                z2, xl2, c2 = move(z, xl, c)
                pairs.append(((z * 2 + xl) * 2 + c, ((z2 % N_Z) * 2 + xl2 % 2) * 2 + c2 % 2))
    return lax.ppermute(x, "dp", pairs)


def to_partner(x):
    return dp_perm(x, lambda z, xl, c: (z + N_Z // 2, xl, c))


def along_z(x, by):
    return dp_perm(x, lambda z, xl, c: (z + by, xl, c))


def other_core(x):
    return dp_perm(x, lambda z, xl, c: (z, xl, c + 1))


def other_xl(x):
    return dp_perm(x, lambda z, xl, c: (z, xl + 1, c))


def gather_chunks(own, a, b):
    c = [None] * N_TENSOR
    c[0] = own
    c[4] = swap(own, 4)
    c[a] = swap(own, a)
    c[b] = swap(own, b)
    c[4 ^ b] = swap(c[b], 4)
    c[2] = swap(c[a], b)
    c[4 ^ a] = swap(c[4], a)
    c[6] = swap(c[4 ^ b], a)
    return c


def scatter_first(t, a, b, add_up):
    return (add_up(t[4 ^ b], swap(t[6], a)), add_up(t[a], swap(t[2], b)),
            add_up(t[4], swap(t[4 ^ a], a)))


def scatter_next(t, first, b):
    return t[b] + swap(first[0], 4)


def scatter_last(t, first, ub, a, b):
    _, ua, u4 = first
    parts = (t[0], swap(u4, 4), swap(ua, a), swap(ub, b))
    return sum(p.astype(F32) for p in parts).astype(BF)


VM = pl.BlockSpec(memory_space=pltpu.VMEM)
ANY = pl.BlockSpec(memory_space=pl.ANY)


def pack_kernel(n, *refs):
    for i in range(n):
        refs[-1][i] = refs[i][0]


def pack(homes, slot, after=()):
    _, t, cols = homes[0].shape
    n = len(homes)
    last = pl.BlockSpec((1, t, cols), lambda i: (slot, 0, 0))
    return pl.pallas_call(
        functools.partial(pack_kernel, n),
        grid=(1,),
        in_specs=[last] * n + [ANY] * len(after),
        out_specs=pl.BlockSpec((n, t, cols), lambda i: (0, 0, 0)),
        out_shape=jax.ShapeDtypeStruct((n, t, cols), BF),
        compiler_params=pltpu.CompilerParams(vmem_limit_bytes=VMEM_LIMIT),
        cost_estimate=SMALL,
        name="pack",
    )(*homes, *after)


def add_kernel(a_ref, b_ref, *refs):
    refs[-1][...] = a_ref[...] + b_ref[...]


def add(a, b, after):
    flat = a.ndim == 2
    blk = VM if flat else pl.BlockSpec((1,) + a.shape[1:], lambda i: (i, 0, 0))
    return pl.pallas_call(
        add_kernel,
        grid=() if flat else (a.shape[0],),
        in_specs=[blk, blk] + [ANY] * len(after),
        out_specs=blk,
        out_shape=jax.ShapeDtypeStruct(a.shape, a.dtype),
        compiler_params=pltpu.CompilerParams(vmem_limit_bytes=VMEM_LIMIT),
        cost_estimate=SMALL,
        name="add",
    )(a, b, *after)


def value_kernel(*refs):
    chunks, w_ref, out_ref = refs[:8], refs[8], refs[-1]
    d = w_ref.shape[0]
    acc = jnp.zeros(out_ref.shape, F32)
    for at in range(0, d, BLK):
        rows = jnp.concatenate([c[:, at:at + BLK] for c in chunks], axis=0)
        acc += jnp.dot(rows, w_ref[at:at + BLK, :], preferred_element_type=F32)
    out_ref[...] = acc.astype(BF)


def project_values(chunks, w, after=()):
    n, d = chunks[0].shape
    cols = w.shape[1]
    return pl.pallas_call(
        value_kernel,
        in_specs=[VM] * 9 + [ANY] * len(after),
        out_specs=VM,
        out_shape=jax.ShapeDtypeStruct((8 * n, cols), BF),
        compiler_params=pltpu.CompilerParams(vmem_limit_bytes=VMEM_LIMIT),
        cost_estimate=SMALL,
        name="project_values",
    )(*chunks, w, *after)


def attend_kernel(arrived, me_ref, *refs):
    q_ref, k_ref, v_ref, g_ref, bq_ref, bk_ref = refs[:6]
    got_ref = refs[6] if arrived else None
    att_ref, vg_ref, vgt_ref, dqk_ref, v_abs, vg_abs = refs[-6:]
    me, live, came = me_ref[0], me_ref[2] == 1, me_ref[3] == 1
    n = q_ref.shape[0] // N_TENSOR
    scale = 1.0 / math.sqrt(HD)
    for d in range(N_TENSOR):
        at = pl.multiple_of((me ^ d) * n, n)
        v_abs[pl.ds(at, n), :] = v_ref[d * n:(d + 1) * n, :]
    g, v = g_ref[...], v_abs[...]
    q = jnp.where(live, q_ref[...], 0).astype(BF)
    k = jnp.where(live, k_ref[...], 0).astype(BF)
    if arrived:
        q = jnp.where(came, got_ref[0], q)
        k = jnp.where(came, got_ref[1], k)
    nt = (((1,), (1,)), ((), ()))
    tn = (((0,), (0,)), ((), ()))
    s = lax.dot_general(q, k, nt, preferred_element_type=F32) * scale
    s = jnp.where(bq_ref[...] == bk_ref[...], s, masked_score)
    e = jnp.exp(s - jnp.max(s, axis=-1, keepdims=True))
    p = e / jnp.sum(e, axis=-1, keepdims=True)
    low = p.astype(BF)
    att_ref[...] = jnp.dot(low, v, preferred_element_type=F32).astype(BF)
    pg = lax.dot_general(g, v, nt, preferred_element_type=F32)
    vg_abs[...] = lax.dot_general(low, g, tn, preferred_element_type=F32).astype(BF)
    inner = jnp.sum(pg * p, axis=-1, keepdims=True)
    sg = (p * (pg - inner) * scale).astype(BF)
    dqk_ref[0] = jnp.dot(sg, k, preferred_element_type=F32).astype(BF)
    dqk_ref[1] = lax.dot_general(sg, q, tn, preferred_element_type=F32).astype(BF)
    vg = jnp.concatenate(
        [vg_abs[pl.ds(pl.multiple_of((me ^ d) * n, n), n), :] for d in range(N_TENSOR)], axis=0)
    vg_ref[...] = vg
    vgt_ref[...] = vg.T


def attend(info, q_home, k_home, v_rel, g, blocks, got=None, after=()):
    _, t, cols = q_home.shape
    row = pl.BlockSpec((None, t, HD), lambda h, m: (m[1], 0, h))
    flat = pl.BlockSpec((t, HD), lambda h, m: (0, h))
    two = pl.BlockSpec((2, t, HD), lambda h, m: (0, 0, h))
    arrived = got is not None
    shape = jax.ShapeDtypeStruct
    return pl.pallas_call(
        functools.partial(attend_kernel, arrived),
        grid_spec=pltpu.PrefetchScalarGridSpec(
            num_scalar_prefetch=1,
            grid=(cols // HD,),
            in_specs=[row, row, flat, row]
            + [
                pl.BlockSpec((None, t, 1), lambda h, m: (m[1], 0, 0)),
                pl.BlockSpec((None, 1, t), lambda h, m: (m[1], 0, 0)),
            ]
            + [two] * arrived + [ANY] * len(after),
            out_specs=[flat, flat, pl.BlockSpec((HD, t), lambda h, m: (h, 0)), two],
            scratch_shapes=[pltpu.VMEM((t, HD), BF)] * 2,
        ),
        out_shape=[shape((t, cols), BF), shape((t, cols), BF), shape((cols, t), BF),
                   shape((2, t, cols), BF)],
        compiler_params=pltpu.CompilerParams(vmem_limit_bytes=VMEM_LIMIT),
        cost_estimate=SMALL,
        name="attend",
    )(info, q_home, k_home, v_rel, g, blocks[:, :, None], blocks[:, None, :],
      *([got] if arrived else []), *after)


def terms_kernel(vg_ref, w_ref, *refs):
    outs = refs[-N_TENSOR:]
    n = outs[0].shape[0]
    for at in range(0, w_ref.shape[0], BLK):
        part = lax.dot_general(
            vg_ref[...], w_ref[at:at + BLK, :], (((1,), (1,)), ((), ())),
            preferred_element_type=F32,
        ).astype(BF)
        for d in range(N_TENSOR):
            outs[d][:, at:at + BLK] = part[d * n:(d + 1) * n]


def row_terms(vg_rel, w, after=()):
    t, cols = vg_rel.shape
    d = w.shape[0]
    n = t // N_TENSOR
    return pl.pallas_call(
        terms_kernel,
        in_specs=[VM, VM] + [ANY] * len(after),
        out_specs=[VM] * N_TENSOR,
        out_shape=[jax.ShapeDtypeStruct((n, d), BF)] * N_TENSOR,
        compiler_params=pltpu.CompilerParams(vmem_limit_bytes=VMEM_LIMIT),
        cost_estimate=SMALL,
        name="row_terms",
    )(vg_rel, w, *after)


def weight_kernel(core_ref, *refs):
    chunks, vgta_ref, vgtb_ref, keep_ref, send_ref = refs[:16], refs[16], refs[17], refs[-2], refs[-1]
    vgt = jnp.concatenate([vgta_ref[...], vgtb_ref[...]], axis=1)
    half, blk = keep_ref.shape[1], keep_ref.shape[2]
    first = core_ref[0] == 0
    for i in range(keep_ref.shape[0]):
        rows = jnp.concatenate([c[:, i * blk:(i + 1) * blk] for c in chunks], axis=0)
        part = jnp.dot(vgt, rows, preferred_element_type=F32).astype(BF)
        keep_ref[i] = jnp.where(first, part[:half], part[half:])
        send_ref[i] = jnp.where(first, part[half:], part[:half])


def weight_terms(core, chunks, vgt_a, vgt_b, after):
    n, d = chunks[0].shape
    cols, t = vgt_a.shape
    shape = jax.ShapeDtypeStruct((N_Z, cols // 2, d // N_Z), BF)
    return pl.pallas_call(
        weight_kernel,
        in_specs=[pl.BlockSpec(memory_space=pltpu.SMEM)] + [VM] * 18 + [ANY] * len(after),
        out_specs=[VM, VM],
        out_shape=[shape, shape],
        compiler_params=pltpu.CompilerParams(vmem_limit_bytes=VMEM_LIMIT),
        cost_estimate=SMALL,
        name="weight_terms",
    )(core, *chunks, vgt_a, vgt_b, *after)


def weight_sum(keep, sent, xl, core, after):
    u = add(keep, other_core(sent), after)
    groups = [[(z * 2 + x) * 2 + c for z in range(N_Z)] for x in range(2) for c in range(2)]
    u = lax.psum_scatter(u, "dp", scatter_dimension=0, axis_index_groups=groups)
    half, lanes = u.shape[0], u.shape[1] // 2
    mine = lax.dynamic_slice_in_dim(u, xl * lanes, lanes, 1).astype(F32)
    theirs = lax.dynamic_slice_in_dim(u, (1 - xl) * lanes, lanes, 1)
    total = (mine + other_xl(theirs).astype(F32)).T
    rows = lanes // 2
    mine = lax.dynamic_slice_in_dim(total, core * rows, rows, 0)
    theirs = other_core(lax.dynamic_slice_in_dim(total, (1 - core) * rows, rows, 0))
    first = core == 0
    return jnp.concatenate(
        [jnp.where(first, mine, theirs), jnp.where(first, theirs, mine)], axis=1)


def shards(tile_rows, queries, keys, w_value, ctx_grad, move, blocks):
    rank_count = lax.axis_size("dp")
    half_ranks = rank_count // 2
    my_rank = lax.axis_index("dp")
    partner = (my_rank + half_ranks) % rank_count
    me = lax.axis_index("tensor").astype(jnp.int32)
    xl, core = (my_rank // 2) % 2, my_rank % 2

    own_dest = move[my_rank]
    live = own_dest[:2] == my_rank * 2 + jnp.arange(2, dtype=jnp.int32)
    leaving = (own_dest[2] >= 0) & (own_dest[2] // 2 == partner)
    sender_dest = move[partner, 2]
    arriving = (sender_dest >= 0) & (sender_dest // 2 == my_rank)
    slot_b = jnp.where(arriving, sender_dest % 2, jnp.where(live[0], 1, 0)).astype(jnp.int32)
    slot_a = 1 - slot_b
    live_a, live_b = live[slot_a], live[slot_b]

    def own(home, slot):
        return lax.dynamic_index_in_dim(home, slot, 0, keepdims=False)

    def kept(home):
        row = own(home, slot_a)
        return jnp.where(live_a, row, jnp.zeros_like(row))

    def second(home, got):
        row = own(home, slot_b)
        return jnp.where(arriving, got, jnp.where(live_b, row, jnp.zeros_like(row)))

    got_rows = to_partner(pack([tile_rows], 2)[0])
    rows_a = gather_chunks(kept(tile_rows), 1, 3)
    rows_b = gather_chunks(second(tile_rows, got_rows), 3, 1)
    got_qk = to_partner(pack([queries, keys], 2, [rows_a[2]]))

    def info(slot, is_live, came):
        return jnp.stack([me, slot, is_live.astype(jnp.int32), came.astype(jnp.int32)])

    values_a = project_values(rows_a, w_value)
    att_a, vg_a, vgt_a, dqk_a = attend(
        info(slot_a, live_a, jnp.zeros((), bool)), queries, keys, values_a, ctx_grad, blocks)
    values_b = project_values(rows_b, w_value)
    terms_a = row_terms(vg_a, w_value, [values_b])
    arrived_a = [swap(terms_a[6], 1), swap(terms_a[2], 3), swap(terms_a[5], 1)]
    att_b, vg_b, vgt_b, dqk_b = attend(
        info(slot_b, live_b, arriving), queries, keys, values_b, ctx_grad, blocks, got_qk,
        [terms_a[0]])
    back_qk = to_partner(dqk_b)
    keep, sent = weight_terms(
        core.astype(jnp.int32).reshape(1), rows_a + rows_b, vgt_a, vgt_b, [])
    terms_b = row_terms(vg_b, w_value, [sent])
    weight_grad = weight_sum(keep, sent, xl, core, [terms_b[0]] + [])

    first_b = scatter_first(terms_b, 3, 1, lambda x, y: x + y)
    next_b = scatter_next(terms_b, first_b, 1)
    late = lambda x, y: add(x, y, [next_b])
    first_a = (late(terms_a[7], arrived_a[0]), late(terms_a[1], arrived_a[1]),
               late(terms_a[4], arrived_a[2]))
    next_a = scatter_next(terms_a, first_a, 3)
    grad_b = scatter_last(terms_b, first_b, next_b, 3, 1)
    grad_a = scatter_last(terms_a, first_a, next_a, 1, 3)

    def by_slot(of_a, of_b):
        first = slot_a == 0
        return [jnp.where(first, of_a, of_b), jnp.where(first, of_b, of_a)]

    def home(of_a, of_b, back):
        here = by_slot(of_a, of_b)
        rows = [jnp.where(live[0], here[0], 0), jnp.where(live[1], here[1], 0),
                jnp.where(leaving, back, 0)]
        return jnp.stack(rows).astype(BF)

    attended = jnp.stack(by_slot(att_a, att_b))
    tile_grad = home(grad_a, grad_b, to_partner(grad_b))
    query_grad = home(dqk_a[0], dqk_b[0], back_qk[0])
    key_grad = home(dqk_a[1], dqk_b[1], back_qk[1])
    return (attended, tile_grad, query_grad, key_grad, weight_grad)


def solution(mesh):
    placed = (
        P("dp", "tensor", None),
        P("dp", None, "tensor"),
        P("dp", None, "tensor"),
        P(None, "tensor"),
        P("dp", None, "tensor"),
        P(),
        P("dp", None),
    )
    return jax.shard_map(
        shards,
        mesh=mesh,
        in_specs=placed,
        out_specs=(
            P("dp", None, "tensor"),
            P("dp", "tensor", None),
            P("dp", None, "tensor"),
            P("dp", None, "tensor"),
            P("dp", "tensor"),
        ),
        check_vma=False,
    )
```

time: 252 us -> 204 us (0.81)
  the two profiles are of different devices: /device:TPU:96 before, /device:TPU:1 now
where the time goes in v2:
time: 204 us; the launch traced here: 203 us
  starting transfers between devices  70.4 us (35%)
  waiting for transfers between devices  57.6 us (28%)
  Pallas kernels  28.7 us (14%)
  between operations  22.4 us (11%)
  local copies, waits for them, and re-layouts  12.5 us (6%)
  other arithmetic  11.3 us (6%)
    ppermute x28, waiting for transfers between devices, swap(): return lax.ppermute(x, 'tensor', [(i, i ^ d) for i in range(N_TENSOR)])  45.3 us
    ppermute x28, starting transfers between devices, swap(): return lax.ppermute(x, 'tensor', [(i, i ^ d) for i in range(N_TENSOR)])  35.7 us
    ppermute x7, starting transfers between devices, dp_perm(): return lax.ppermute(x, 'dp', pairs)  34.6 us
    ppermute x7, waiting for transfers between devices, dp_perm(): return lax.ppermute(x, 'dp', pairs)  12.3 us
    unnamed x77, local copies, waits for them, and re-layouts  9.29 us
    pallas_call x2, Pallas kernels, attend(): pl.pallas_call(functools.partial(attend_kernel, arrived), grid_spec=pltpu...  8.54 us
    pallas_call x2, Pallas kernels, project_values(): pl.pallas_call(value_kernel, in_specs=[VM] * 9 + [ANY] * len(after), out_...  6.92 us
    pallas_call x1, Pallas kernels, weight_terms(): pl.pallas_call(weight_kernel, in_specs=[pl.BlockSpec(memory_space=pltpu.S...  4.75 us
  transfers between devices with their start and end apart: 36, of which 15 were waited for; matrix products, arithmetic and copies ran while one was open for 7% of the time, Pallas kernels for 8%

profile of v2, /device:TPU:1, one launch (start us, length us, event | category | flops | bytes accessed | tf_op | source)
XLA Modules:
  0.0 203.0 jit_solution(16787269448167005463)
XLA Ops:
  7.2 1.3 copy-done.5
  8.6 7.8 %collective-permute-start.7 = (bf16[32,6144]{1,0:T(8,128)(2,1)S(1)}, bf16[32,6144]{1,0:T(8,128)(2,1)}, u32[]{:S(2)}, u32[]{:S(2)}) collective-permute-start(bf16[32,6144]{1,0:T(8,128)(2,1)S(1)} %bitcast.38), channel_id=1, source_target_pairs={{0,128},{8,136},{16,144},{24,152},{32,160},{40,168},{48,176},{56,1... | collective-permute-start | bytes 1179656 | tf_op jit(solution)/shard_map/ppermute | solution.py:33
  21.8 2.8 %collective-permute-start.3 = (bf16[32,6144]{1,0:T(8,128)(2,1)S(1)}, bf16[32,6144]{1,0:T(8,128)(2,1)S(1)}, u32[]{:S(2)}, u32[]{:S(2)}) collective-permute-start(bf16[32,6144]{1,0:T(8,128)(2,1)S(1)} %select_bitcast_fusion.3.refs_0_), channel_id=1, source_target_pairs={{0,4},{1,5},{2,6},{3,7},{4,0},{5,1},{6,2},{7,3},{8,12},{9,13},{10,... | collective-permute-start | bytes 1179656 | tf_op jit(solution)/shard_map/ppermute | solution.py:23
  24.7 2.7 %collective-permute-start.2 = (bf16[32,6144]{1,0:T(8,128)(2,1)S(1)}, bf16[32,6144]{1,0:T(8,128)(2,1)}, u32[]{:S(2)}, u32[]{:S(2)}) collective-permute-start(bf16[32,6144]{1,0:T(8,128)(2,1)S(1)} %select_bitcast_fusion.3.refs_0_), channel_id=1, source_target_pairs={{0,3},{1,2},{2,1},{3,0},{4,7},{5,6},{6,5},{7,4},{8,11},{9,10},{10,... | collective-permute-start | bytes 1179656 | tf_op jit(solution)/shard_map/ppermute | solution.py:23
  28.1 1.5 collective-permute-start.8
  29.7 1.5 collective-permute-start.11
  31.2 4.3 %collective-permute-done.2.refs_3_ = bf16[32,6144]{1,0:T(8,128)(2,1)} collective-permute-done((bf16[32,6144]{1,0:T(8,128)(2,1)S(1)}, bf16[32,6144]{1,0:T(8,128)(2,1)}, u32[]{:S(2)}, u32[]{:S(2)}) %collective-permute-start.2) | collective-permute-done | bytes 393248 | tf_op jit(solution)/shard_map/ppermute | solution.py:23
  35.7 2.6 %collective-permute-start.9 = (bf16[32,6144]{1,0:T(8,128)(2,1)S(1)}, bf16[32,6144]{1,0:T(8,128)(2,1)}, u32[]{:S(2)}, u32[]{:S(2)}) collective-permute-start(bf16[32,6144]{1,0:T(8,128)(2,1)S(1)} %bitcast_select_fusion.refs_0_.refs_8_), channel_id=1, source_target_pairs={{0,3},{1,2},{2,1},{3,0},{4,7},{5,6},{6,5},{7,4},{8,11},{9,10},{10,... | collective-permute-start | bytes 1179656 | tf_op jit(solution)/shard_map/ppermute | solution.py:23
  38.4 6.6 %collective-permute-done.8.refs_1_.refs_9_ = bf16[32,6144]{1,0:T(8,128)(2,1)S(1)} collective-permute-done((bf16[32,6144]{1,0:T(8,128)(2,1)S(1)}, bf16[32,6144]{1,0:T(8,128)(2,1)S(1)}, u32[]{:S(2)}, u32[]{:S(2)}) %collective-permute-start.8) | collective-permute-done | bytes 393248 | tf_op jit(solution)/shard_map/ppermute | solution.py:23
  45.4 3.7 %collective-permute-done.5.refs_7_ = bf16[32,6144]{1,0:T(8,128)(2,1)} collective-permute-done((bf16[32,6144]{1,0:T(8,128)(2,1)}, bf16[32,6144]{1,0:T(8,128)(2,1)}, u32[]{:S(2)}, u32[]{:S(2)}) %collective-permute-start.5) | collective-permute-done | bytes 393248 | tf_op jit(solution)/shard_map/ppermute | solution.py:23
  49.1 2.3 %collective-permute-start.6 = (bf16[32,6144]{1,0:T(8,128)(2,1)}, bf16[32,6144]{1,0:T(8,128)(2,1)}, u32[]{:S(2)}, u32[]{:S(2)}) collective-permute-start(bf16[32,6144]{1,0:T(8,128)(2,1)} %collective-permute-done.5.refs_7_), channel_id=1, source_target_pairs={{0,1},{1,0},{2,3},{3,2},{4,5},{5,4},{6,7},{7,6},{8,9},{9,8},{10,11... | collective-permute-start | bytes 1179656 | tf_op jit(solution)/shard_map/ppermute | solution.py:23
  51.4 1.9 collective-permute-start.14
  53.7 4.1 %collective-permute-done.12.refs_5_.refs_13_ = bf16[32,6144]{1,0:T(8,128)(2,1)} collective-permute-done((bf16[32,6144]{1,0:T(8,128)(2,1)S(1)}, bf16[32,6144]{1,0:T(8,128)(2,1)}, u32[]{:S(2)}, u32[]{:S(2)}) %collective-permute-start.12) | collective-permute-done | bytes 393248 | tf_op jit(solution)/shard_map/ppermute | solution.py:23
  57.8 3.4 %collective-permute-start.13 = (bf16[32,6144]{1,0:T(8,128)(2,1)}, bf16[32,6144]{1,0:T(8,128)(2,1)}, u32[]{:S(2)}, u32[]{:S(2)}) collective-permute-start(bf16[32,6144]{1,0:T(8,128)(2,1)} %collective-permute-done.12.refs_5_.refs_13_), channel_id=1, source_target_pairs={{0,3},{1,2},{2,1},{3,0},{4,7},{5,6},{6,5},{7,4},{8,11},{9,10},{10,... | collective-permute-start | bytes 1179656 | tf_op jit(solution)/shard_map/ppermute | solution.py:23
  64.4 2.3 %copy-done.1 = bf16[6144,384]{1,0:T(8,128)(2,1)S(1)} copy-done((bf16[6144,384]{1,0:T(8,128)(2,1)S(1)}, bf16[6144,384]{1,0:T(8,128)(2,1)}, u32[]{:S(2)}) %copy-start.1) | copy-done | bytes 4718616
  66.7 1.0 copy-done.8
  67.7 3.3 %project_values.2.refs_2_ = bf16[256,384]{1,0:T(8,128)(2,1)S(1)} custom-call(bf16[32,6144]{1,0:T(8,128)(2,1)S(1)} %select_bitcast_fusion.3.refs_0_, bf16[32,6144]{1,0:T(8,128)(2,1)} %collective-permute-done.refs_1_, bf16[32,6144]{1,0:T(8,128)(2,1)S(1)} %collective-permute-done.1.refs_2_, bf16[32,6144]{1,0:T(8,128)(2,1)} %collective-permute-done.2.refs_3_, ...), custom_call_target="tpu_custom_call" | custom-call | flops 1 | bytes 1 | tf_op jit(solution)/shard_map/project_values/pallas_call | solution.py:137
  71.1 3.8 %attend.2 = (bf16[256,384]{1,0:T(8,128)(2,1)S(1)}, bf16[256,384]{1,0:T(8,128)(2,1)S(1)}, bf16[384,256]{1,0:T(8,128)(2,1)S(1)}, bf16[2,256,384]{2,1,0:T(8,128)(2,1)S(1)}) custom-call(s32[4]{0:T(128)S(1)} %pad_add_fusion.me_ref, bf16[3,256,384]{2,1,0:T(8,128)(2,1)S(1)} %copy-done.3, bf16[3,256,384]{2,1,0:T(8,128)(2,1)S(1)} %copy-done.4, ...), custom_call_target="tpu_custom_call" | custom-call | flops 1 | bytes 1 | tf_op jit(solution)/shard_map/attend/pallas_call | solution.py:191
  74.9 3.6 %project_values.3.refs_0_.refs_2_ = bf16[256,384]{1,0:T(8,128)(2,1)S(1)} custom-call(bf16[32,6144]{1,0:T(8,128)(2,1)S(1)} %bitcast_select_fusion.refs_0_.refs_8_, bf16[32,6144]{1,0:T(8,128)(2,1)S(1)} %collective-permute-done.8.refs_1_.refs_9_, bf16[32,6144]{1,0:T(8,128)(2,1)} %collective-permute-done.10.refs_2_.refs_10_, ...), custom_call_target="tpu_custom_call" | custom-call | flops 1 | bytes 1 | tf_op jit(solution)/shard_map/project_values/pallas_call | solution.py:137
  78.6 1.8 row_terms.2
  82.0 4.8 %attend.3 = (bf16[256,384]{1,0:T(8,128)(2,1)S(1)}, bf16[256,384]{1,0:T(8,128)(2,1)S(1)}, bf16[384,256]{1,0:T(8,128)(2,1)S(1)}, bf16[2,256,384]{2,1,0:T(8,128)(2,1)S(1)}) custom-call(s32[4]{0:T(128)S(1)} %pad_add_fusion.1.me_ref, bf16[3,256,384]{2,1,0:T(8,128)(2,1)S(1)} %copy-done.3, bf16[3,256,384]{2,1,0:T(8,128)(2,1)S(1)} %copy-done.4, ...), custom_call_target="tpu_custom_call" | custom-call | flops 1 | bytes 1 | tf_op jit(solution)/shard_map/attend/pallas_call | solution.py:191
  88.2 4.8 %weight_terms.1 = (bf16[8,192,768]{2,1,0:T(8,128)(2,1)S(1)}, bf16[8,192,768]{2,1,0:T(8,128)(2,1)S(1)}) custom-call(s32[1]{0:T(128)} %bitcast.14.core_ref, bf16[32,6144]{1,0:T(8,128)(2,1)S(1)} %select_bitcast_fusion.3.refs_0_, bf16[32,6144]{1,0:T(8,128)(2,1)} %collective-permute-done.refs_1_, bf16[32,6144]{1,0:T(8,128)(2,1)S(1)} %collective-permute-done.1.refs_2_, ...), custom_call_target="tpu_custom_call" | custom-call | flops 1 | bytes 1 | tf_op jit(solution)/shard_map/weight_terms/pallas_call | solution.py:257
  93.0 9.1 %collective-permute-start.32 = (bf16[8,192,768]{2,1,0:T(8,128)(2,1)S(1)}, bf16[8,192,768]{2,1,0:T(8,128)(2,1)S(1)}, u32[]{:S(2)}, u32[]{:S(2)}) collective-permute-start(bf16[8,192,768]{2,1,0:T(8,128)(2,1)S(1)} %get-tuple-element.40.refs_0_), channel_id=1, source_target_pairs={{0,8},{8,0},{16,24},{24,16},{32,40},{40,32},{48,56},{56,48},{64,72... | collective-permute-start | bytes 7077896 | tf_op jit(solution)/shard_map/ppermute | solution.py:33
  102.1 2.6 %row_terms.3 = (bf16[32,6144]{1,0:T(8,128)(2,1)S(1)}, bf16[32,6144]{1,0:T(8,128)(2,1)S(1)}, bf16[32,6144]{1,0:T(8,128)(2,1)S(1)}, bf16[32,6144]{1,0:T(8,128)(2,1...) custom-call(bf16[256,384]{1,0:T(8,128)(2,1)S(1)} %get-tuple-element., ...), custom_call_target="tpu_custom_call" | custom-call | flops 1 | bytes 1 | tf_op jit(solution)/shard_map/row_terms/pallas_call | solution.py:230
  104.7 1.6 collective-permute-done.32.b_ref
  106.3 3.1 %add.161 = bf16[8,192,768]{2,1,0:T(8,128)(2,1)} custom-call(bf16[8,192,768]{2,1,0:T(8,128)(2,1)S(1)} %get-tuple-element.56.a_ref, bf16[8,192,768]{2,1,0:T(8,128)(2,1)S(1)} %collective-permute-done.32.b_ref, bf16[32,6144]{1,0:T(8,128)(2,1)S(1)} %get-tuple-element.49.refs_0_), custom_call_target="tpu_custom_call" | custom-call | flops 1 | bytes 1 | tf_op jit(solution)/shard_map/add/pallas_call | solution.py:112
  109.5 1.1 collective-permute-start.17
  110.5 1.7 collective-permute-start.25
  112.2 8.9 %collective-permute-done.17 = bf16[32,6144]{1,0:T(8,128)(2,1)S(1)} collective-permute-done((bf16[32,6144]{1,0:T(8,128)(2,1)S(1)}, bf16[32,6144]{1,0:T(8,128)(2,1)S(1)}, u32[]{:S(2)}, u32[]{:S(2)}) %collective-permute-start.17) | collective-permute-done | bytes 393248 | tf_op jit(solution)/shard_map/ppermute | solution.py:23
  121.9 2.7 %collective-permute-start.18 = (bf16[32,6144]{1,0:T(8,128)(2,1)}, bf16[32,6144]{1,0:T(8,128)(2,1)}, u32[]{:S(2)}, u32[]{:S(2)}) collective-permute-start(bf16[32,6144]{1,0:T(8,128)(2,1)} %add.112), channel_id=1, source_target_pairs={{0,4},{1,5},{2,6},{3,7},{4,0},{5,1},{6,2},{7,3},{8,12},{9,13},{10,... | collective-permute-start | bytes 1179656 | tf_op jit(solution)/shard_map/ppermute | solution.py:23
  124.7 1.5 collective-permute-start.27
  130.2 1.2 add.118
  131.3 1.0 collective-permute-done.18
  133.4 1.2 add.113.refs_0_
  134.5 2.8 %collective-permute-start.26 = (bf16[32,6144]{1,0:T(8,128)(2,1)S(1)}, bf16[32,6144]{1,0:T(8,128)(2,1)S(1)}, u32[]{:S(2)}, u32[]{:S(2)}) collective-permute-start(bf16[32,6144]{1,0:T(8,128)(2,1)S(1)} %add.118), channel_id=1, source_target_pairs={{0,4},{1,5},{2,6},{3,7},{4,0},{5,1},{6,2},{7,3},{8,12},{9,13},{10,... | collective-permute-start | bytes 1179656 | tf_op jit(solution)/shard_map/ppermute | solution.py:23
  137.4 4.1 %collective-permute-done.27 = bf16[32,6144]{1,0:T(8,128)(2,1)} collective-permute-done((bf16[32,6144]{1,0:T(8,128)(2,1)}, bf16[32,6144]{1,0:T(8,128)(2,1)}, u32[]{:S(2)}, u32[]{:S(2)}) %collective-permute-start.27) | collective-permute-done | bytes 393248 | tf_op jit(solution)/shard_map/ppermute | solution.py:23
  142.7 1.2 add.120
  143.8 1.1 collective-permute-start.28
  145.0 5.0 %collective-permute-done.16.b_ref = bf16[32,6144]{1,0:T(8,128)(2,1)S(1)} collective-permute-done((bf16[32,6144]{1,0:T(8,128)(2,1)S(1)}, bf16[32,6144]{1,0:T(8,128)(2,1)S(1)}, u32[]{:S(2)}, u32[]{:S(2)}) %collective-permute-start.16) | collective-permute-done | bytes 393248 | tf_op jit(solution)/shard_map/ppermute | solution.py:23
  150.3 1.8 collective-permute-done.23
  152.1 2.7 %collective-permute-start.19 = (bf16[32,6144]{1,0:T(8,128)(2,1)S(1)}, bf16[32,6144]{1,0:T(8,128)(2,1)S(1)}, u32[]{:S(2)}, u32[]{:S(2)}) collective-permute-start(bf16[32,6144]{1,0:T(8,128)(2,1)S(1)} %add.158), channel_id=1, source_target_pairs={{0,4},{1,5},{2,6},{3,7},{4,0},{5,1},{6,2},{7,3},{8,12},{9,13},{10,... | collective-permute-start | bytes 1179656 | tf_op jit(solution)/shard_map/ppermute | solution.py:23
  154.9 2.1 %collective-permute-done.31 = bf16[2,256,384]{2,1,0:T(8,128)(2,1)S(1)} collective-permute-done((bf16[2,256,384]{2,1,0:T(8,128)(2,1)S(1)}, bf16[2,256,384]{2,1,0:T(8,128)(2,1)S(1)}, u32[]{:S(2)}, u32[]{:S(2)}) %collective-permute-start.31) | collective-permute-done | bytes 393248 | tf_op jit(solution)/shard_map/ppermute | solution.py:33
  157.1 1.0 collective-permute-start.24
  158.9 1.2 pad_maximum_fusion.1
  160.7 4.7 %collective-permute-done.21 = bf16[32,6144]{1,0:T(8,128)(2,1)S(1)} collective-permute-done((bf16[32,6144]{1,0:T(8,128)(2,1)S(1)}, bf16[32,6144]{1,0:T(8,128)(2,1)S(1)}, u32[]{:S(2)}, u32[]{:S(2)}) %collective-permute-start.21) | collective-permute-done | bytes 393248 | tf_op jit(solution)/shard_map/ppermute | solution.py:23
  167.9 8.6 %collective-permute-done.30 = bf16[32,6144]{1,0:T(8,128)(2,1)S(1)} collective-permute-done((bf16[32,6144]{1,0:T(8,128)(2,1)S(1)}, bf16[32,6144]{1,0:T(8,128)(2,1)S(1)}, u32[]{:S(2)}, u32[]{:S(2)}) %collective-permute-start.30) | collective-permute-done | bytes 393248 | tf_op jit(solution)/shard_map/ppermute | solution.py:33
  176.7 17.3 %collective-permute-start.34 = (f32[192,192]{0,1:T(8,128)S(1)}, f32[192,192]{0,1:T(8,128)S(1)}, u32[]{:S(2)}, u32[]{:S(2)}) collective-permute-start(f32[192,192]{0,1:T(8,128)S(1)} %dynamic-slice_bitcast_fusion), channel_id=1, source_target_pairs={{0,8},{8,0},{16,24},{24,16},{32,40},{40,32},{48,56},{56,48},{64,72... | collective-permute-start | bytes 442376 | tf_op jit(solution)/shard_map/ppermute | solution.py:33
  194.0 1.1 pad_maximum_fusion
  (146 shorter events, 18.3 us)
Async XLA Ops:
  7.2 9.2 %copy-start = (s32[32,3]{0,1:T(4,128)S(1)}, s32[32,3]{0,1:T(4,128)}, u32[]{:S(2)}) copy-start(s32[32,3]{0,1:T(4,128)} %param.12) | copy-start | bytes 1156
  7.2 159.5 %reduce-scatter.2.cloned.1.call-start = ((), (), s32[]{:S(2)}) async-start(), calls=%async_computation.1 | async-start | bytes 2654208 | tf_op jit(solution)/shard_map/reduce_scatter | solution.py:271
  8.5 12.7 %copy-start.6 = (bf16[3,32,6144]{2,1,0:T(8,128)(2,1)S(1)}, bf16[3,32,6144]{2,1,0:T(8,128)(2,1)}, u32[]{:S(2)}) copy-start(bf16[3,32,6144]{2,1,0:T(8,128)(2,1)} %refs_0_.5) | copy-start | bytes 3538948
  8.5 52.7 %copy-start.3 = (bf16[3,256,384]{2,1,0:T(8,128)(2,1)S(1)}, bf16[3,256,384]{2,1,0:T(8,128)(2,1)}, u32[]{:S(2)}) copy-start(bf16[3,256,384]{2,1,0:T(8,128)(2,1)} %refs_0_.7) | copy-start | bytes 1769476
  8.5 52.7 %copy-start.4 = (bf16[3,256,384]{2,1,0:T(8,128)(2,1)S(1)}, bf16[3,256,384]{2,1,0:T(8,128)(2,1)}, u32[]{:S(2)}) copy-start(bf16[3,256,384]{2,1,0:T(8,128)(2,1)} %refs_1_.5) | copy-start | bytes 1769476
  8.6 18.9 %collective-permute-start.7 = (bf16[32,6144]{1,0:T(8,128)(2,1)S(1)}, bf16[32,6144]{1,0:T(8,128)(2,1)}, u32[]{:S(2)}, u32[]{:S(2)}) collective-permute-start(bf16[32,6144]{1,0:T(8,128)(2,1)S(1)} %bitcast.38), channel_id=1, source_target_pairs={{0,128},{8,136},{16,144},{24,152},{32,160},{40,168},{48,176},{56,1... | collective-permute-start | bytes 1179656 | tf_op jit(solution)/shard_map/ppermute | solution.py:33
  21.8 13.9 %collective-permute-start.3 = (bf16[32,6144]{1,0:T(8,128)(2,1)S(1)}, bf16[32,6144]{1,0:T(8,128)(2,1)S(1)}, u32[]{:S(2)}, u32[]{:S(2)}) collective-permute-start(bf16[32,6144]{1,0:T(8,128)(2,1)S(1)} %select_bitcast_fusion.3.refs_0_), channel_id=1, source_target_pairs={{0,4},{1,5},{2,6},{3,7},{4,0},{5,1},{6,2},{7,3},{8,12},{9,13},{10,... | collective-permute-start | bytes 1179656 | tf_op jit(solution)/shard_map/ppermute | solution.py:23
  24.7 10.8 %collective-permute-start.2 = (bf16[32,6144]{1,0:T(8,128)(2,1)S(1)}, bf16[32,6144]{1,0:T(8,128)(2,1)}, u32[]{:S(2)}, u32[]{:S(2)}) collective-permute-start(bf16[32,6144]{1,0:T(8,128)(2,1)S(1)} %select_bitcast_fusion.3.refs_0_), channel_id=1, source_target_pairs={{0,3},{1,2},{2,1},{3,0},{4,7},{5,6},{6,5},{7,4},{8,11},{9,10},{10,... | collective-permute-start | bytes 1179656 | tf_op jit(solution)/shard_map/ppermute | solution.py:23
  27.4 10.9 %collective-permute-start = (bf16[32,6144]{1,0:T(8,128)(2,1)S(1)}, bf16[32,6144]{1,0:T(8,128)(2,1)}, u32[]{:S(2)}, u32[]{:S(2)}) collective-permute-start(bf16[32,6144]{1,0:T(8,128)(2,1)S(1)} %select_bitcast_fusion.3.refs_0_), channel_id=1, source_target_pairs={{0,1},{1,0},{2,3},{3,2},{4,5},{5,4},{6,7},{7,6},{8,9},{9,8},{10,11... | collective-permute-start | bytes 1179656 | tf_op jit(solution)/shard_map/ppermute | solution.py:23
  28.1 35.9 %copy-start.37 = (s32[2,256]{1,0:T(2,128)S(1)}, s32[2,256]{1,0:T(2,128)}, u32[]{:S(2)}) copy-start(s32[2,256]{1,0:T(2,128)} %param.13) | copy-start | bytes 6148
  28.1 16.9 %collective-permute-start.8 = (bf16[32,6144]{1,0:T(8,128)(2,1)S(1)}, bf16[32,6144]{1,0:T(8,128)(2,1)S(1)}, u32[]{:S(2)}, u32[]{:S(2)}) collective-permute-start(bf16[32,6144]{1,0:T(8,128)(2,1)S(1)} %bitcast_select_fusion.refs_0_.refs_8_), channel_id=1, source_target_pairs={{0,1},{1,0},{2,3},{3,2},{4,5},{5,4},{6,7},{7,6},{8,9},{9,8},{10,11... | collective-permute-start | bytes 1179656 | tf_op jit(solution)/shard_map/ppermute | solution.py:23
  29.7 15.6 %collective-permute-start.11 = (bf16[32,6144]{1,0:T(8,128)(2,1)S(1)}, bf16[32,6144]{1,0:T(8,128)(2,1)}, u32[]{:S(2)}, u32[]{:S(2)}) collective-permute-start(bf16[32,6144]{1,0:T(8,128)(2,1)S(1)} %bitcast_select_fusion.refs_0_.refs_8_), channel_id=1, source_target_pairs={{0,4},{1,5},{2,6},{3,7},{4,0},{5,1},{6,2},{7,3},{8,12},{9,13},{10,... | collective-permute-start | bytes 1179656 | tf_op jit(solution)/shard_map/ppermute | solution.py:23
  35.5 13.6 %collective-permute-start.5 = (bf16[32,6144]{1,0:T(8,128)(2,1)}, bf16[32,6144]{1,0:T(8,128)(2,1)}, u32[]{:S(2)}, u32[]{:S(2)}) collective-permute-start(bf16[32,6144]{1,0:T(8,128)(2,1)} %collective-permute-done.2.refs_3_), channel_id=1, source_target_pairs={{0,4},{1,5},{2,6},{3,7},{4,0},{5,1},{6,2},{7,3},{8,12},{9,13},{10,... | collective-permute-start | bytes 1179656 | tf_op jit(solution)/shard_map/ppermute | solution.py:23
  35.7 15.6 %collective-permute-start.9 = (bf16[32,6144]{1,0:T(8,128)(2,1)S(1)}, bf16[32,6144]{1,0:T(8,128)(2,1)}, u32[]{:S(2)}, u32[]{:S(2)}) collective-permute-start(bf16[32,6144]{1,0:T(8,128)(2,1)S(1)} %bitcast_select_fusion.refs_0_.refs_8_), channel_id=1, source_target_pairs={{0,3},{1,2},{2,1},{3,0},{4,7},{5,6},{6,5},{7,4},{8,11},{9,10},{10,... | collective-permute-start | bytes 1179656 | tf_op jit(solution)/shard_map/ppermute | solution.py:23
  38.3 15.4 %collective-permute-start.1 = (bf16[32,6144]{1,0:T(8,128)(2,1)}, bf16[32,6144]{1,0:T(8,128)(2,1)S(1)}, u32[]{:S(2)}, u32[]{:S(2)}) collective-permute-start(bf16[32,6144]{1,0:T(8,128)(2,1)} %collective-permute-done.refs_1_), channel_id=1, source_target_pairs={{0,3},{1,2},{2,1},{3,0},{4,7},{5,6},{6,5},{7,4},{8,11},{9,10},{10,... | collective-permute-start | bytes 1179656 | tf_op jit(solution)/shard_map/ppermute | solution.py:23
  45.0 12.8 %collective-permute-start.12 = (bf16[32,6144]{1,0:T(8,128)(2,1)S(1)}, bf16[32,6144]{1,0:T(8,128)(2,1)}, u32[]{:S(2)}, u32[]{:S(2)}) collective-permute-start(bf16[32,6144]{1,0:T(8,128)(2,1)S(1)} %collective-permute-done.8.refs_1_.refs_9_), channel_id=1, source_target_pairs={{0,4},{1,5},{2,6},{3,7},{4,0},{5,1},{6,2},{7,3},{8,12},{9,13},{10,... | collective-permute-start | bytes 1179656 | tf_op jit(solution)/shard_map/ppermute | solution.py:23
  45.3 16.7 %collective-permute-start.4 = (bf16[32,6144]{1,0:T(8,128)(2,1)S(1)}, bf16[32,6144]{1,0:T(8,128)(2,1)S(1)}, u32[]{:S(2)}, u32[]{:S(2)}) collective-permute-start(bf16[32,6144]{1,0:T(8,128)(2,1)S(1)} %collective-permute-done.3.refs_4_), channel_id=1, source_target_pairs={{0,1},{1,0},{2,3},{3,2},{4,5},{5,4},{6,7},{7,6},{8,9},{9,8},{10,11... | collective-permute-start | bytes 1179656 | tf_op jit(solution)/shard_map/ppermute | solution.py:23
  49.1 15.3 %collective-permute-start.6 = (bf16[32,6144]{1,0:T(8,128)(2,1)}, bf16[32,6144]{1,0:T(8,128)(2,1)}, u32[]{:S(2)}, u32[]{:S(2)}) collective-permute-start(bf16[32,6144]{1,0:T(8,128)(2,1)} %collective-permute-done.5.refs_7_), channel_id=1, source_target_pairs={{0,1},{1,0},{2,3},{3,2},{4,5},{5,4},{6,7},{7,6},{8,9},{9,8},{10,11... | collective-permute-start | bytes 1179656 | tf_op jit(solution)/shard_map/ppermute | solution.py:23
  51.4 23.5 %collective-permute-start.14 = (bf16[32,6144]{1,0:T(8,128)(2,1)}, bf16[32,6144]{1,0:T(8,128)(2,1)}, u32[]{:S(2)}, u32[]{:S(2)}) collective-permute-start(bf16[32,6144]{1,0:T(8,128)(2,1)} %collective-permute-done.11.refs_4_.refs_12_), channel_id=1, source_target_pairs={{0,3},{1,2},{2,1},{3,0},{4,7},{5,6},{6,5},{7,4},{8,11},{9,10},{10,... | collective-permute-start | bytes 1179656 | tf_op jit(solution)/shard_map/ppermute | solution.py:23
  53.7 21.2 %collective-permute-start.10 = (bf16[32,6144]{1,0:T(8,128)(2,1)}, bf16[32,6144]{1,0:T(8,128)(2,1)}, u32[]{:S(2)}, u32[]{:S(2)}) collective-permute-start(bf16[32,6144]{1,0:T(8,128)(2,1)} %collective-permute-done.9.refs_3_.refs_11_), channel_id=1, source_target_pairs={{0,1},{1,0},{2,3},{3,2},{4,5},{5,4},{6,7},{7,6},{8,9},{9,8},{10,11... | collective-permute-start | bytes 1179656 | tf_op jit(solution)/shard_map/ppermute | solution.py:23
  57.8 17.1 %collective-permute-start.13 = (bf16[32,6144]{1,0:T(8,128)(2,1)}, bf16[32,6144]{1,0:T(8,128)(2,1)}, u32[]{:S(2)}, u32[]{:S(2)}) collective-permute-start(bf16[32,6144]{1,0:T(8,128)(2,1)} %collective-permute-done.12.refs_5_.refs_13_), channel_id=1, source_target_pairs={{0,3},{1,2},{2,1},{3,0},{4,7},{5,6},{6,5},{7,4},{8,11},{9,10},{10,... | collective-permute-start | bytes 1179656 | tf_op jit(solution)/shard_map/ppermute | solution.py:23
  62.8 19.2 %collective-permute-start.15 = (bf16[2,256,384]{2,1,0:T(8,128)(2,1)}, bf16[2,256,384]{2,1,0:T(8,128)(2,1)}, u32[]{:S(2)}, u32[]{:S(2)}) collective-permute-start(bf16[2,256,384]{2,1,0:T(8,128)(2,1)} %pack.3), channel_id=1, source_target_pairs={{0,128},{8,136},{16,144},{24,152},{32,160},{40,168},{48,176},{56,1... | collective-permute-start | bytes 1179656 | tf_op jit(solution)/shard_map/ppermute | solution.py:33
  93.0 13.3 %collective-permute-start.32 = (bf16[8,192,768]{2,1,0:T(8,128)(2,1)S(1)}, bf16[8,192,768]{2,1,0:T(8,128)(2,1)S(1)}, u32[]{:S(2)}, u32[]{:S(2)}) collective-permute-start(bf16[8,192,768]{2,1,0:T(8,128)(2,1)S(1)} %get-tuple-element.40.refs_0_), channel_id=1, source_target_pairs={{0,8},{8,0},{16,24},{24,16},{32,40},{40,32},{48,56},{56,48},{64,72... | collective-permute-start | bytes 7077896 | tf_op jit(solution)/shard_map/ppermute | solution.py:33
  109.4 15.2 %copy-start.34 = (bf16[32,6144]{1,0:T(8,128)(2,1)S(1)}, bf16[32,6144]{1,0:T(8,128)(2,1)}, u32[]{:S(2)}) copy-start(bf16[32,6144]{1,0:T(8,128)(2,1)} %copy-done.33) | copy-start | bytes 1179652
  109.5 20.4 %copy-start.16 = (bf16[2,256,384]{2,1,0:T(8,128)(2,1)S(1)}, bf16[2,256,384]{2,1,0:T(8,128)(2,1)}, u32[]{:S(2)}) copy-start(bf16[2,256,384]{2,1,0:T(8,128)(2,1)} %copy-done.15) | copy-start | bytes 1179652
  109.5 20.6 %copy-start.30 = (bf16[32,6144]{1,0:T(8,128)(2,1)S(1)}, bf16[32,6144]{1,0:T(8,128)(2,1)}, u32[]{:S(2)}) copy-start(bf16[32,6144]{1,0:T(8,128)(2,1)} %copy-done.29) | copy-start | bytes 1179652
  109.5 11.6 %collective-permute-start.17 = (bf16[32,6144]{1,0:T(8,128)(2,1)S(1)}, bf16[32,6144]{1,0:T(8,128)(2,1)S(1)}, u32[]{:S(2)}, u32[]{:S(2)}) collective-permute-start(bf16[32,6144]{1,0:T(8,128)(2,1)S(1)} %get-tuple-element.43), channel_id=1, source_target_pairs={{0,3},{1,2},{2,1},{3,0},{4,7},{5,6},{6,5},{7,4},{8,11},{9,10},{10,... | collective-permute-start | bytes 1179656 | tf_op jit(solution)/shard_map/ppermute | solution.py:23
  110.5 19.5 %collective-permute-start.25 = (bf16[32,6144]{1,0:T(8,128)(2,1)}, bf16[32,6144]{1,0:T(8,128)(2,1)}, u32[]{:S(2)}, u32[]{:S(2)}) collective-permute-start(bf16[32,6144]{1,0:T(8,128)(2,1)} %get-tuple-element.51), channel_id=1, source_target_pairs={{0,3},{1,2},{2,1},{3,0},{4,7},{5,6},{6,5},{7,4},{8,11},{9,10},{10,... | collective-permute-start | bytes 1179656 | tf_op jit(solution)/shard_map/ppermute | solution.py:23
  121.1 11.3 %copy-start.32 = (bf16[32,6144]{1,0:T(8,128)(2,1)S(1)}, bf16[32,6144]{1,0:T(8,128)(2,1)}, u32[]{:S(2)}) copy-start(bf16[32,6144]{1,0:T(8,128)(2,1)} %copy-done.31) | copy-start | bytes 1179652
  121.9 10.4 %collective-permute-start.18 = (bf16[32,6144]{1,0:T(8,128)(2,1)}, bf16[32,6144]{1,0:T(8,128)(2,1)}, u32[]{:S(2)}, u32[]{:S(2)}) collective-permute-start(bf16[32,6144]{1,0:T(8,128)(2,1)} %add.112), channel_id=1, source_target_pairs={{0,4},{1,5},{2,6},{3,7},{4,0},{5,1},{6,2},{7,3},{8,12},{9,13},{10,... | collective-permute-start | bytes 1179656 | tf_op jit(solution)/shard_map/ppermute | solution.py:23
  124.7 9.8 %collective-permute-start.22 = (bf16[32,6144]{1,0:T(8,128)(2,1)S(1)}, bf16[32,6144]{1,0:T(8,128)(2,1)S(1)}, u32[]{:S(2)}, u32[]{:S(2)}) collective-permute-start(bf16[32,6144]{1,0:T(8,128)(2,1)S(1)} %copy-done.34), channel_id=1, source_target_pairs={{0,1},{1,0},{2,3},{3,2},{4,5},{5,4},{6,7},{7,6},{8,9},{9,8},{10,11... | collective-permute-start | bytes 1179656 | tf_op jit(solution)/shard_map/ppermute | solution.py:23
  124.7 16.9 %collective-permute-start.27 = (bf16[32,6144]{1,0:T(8,128)(2,1)}, bf16[32,6144]{1,0:T(8,128)(2,1)}, u32[]{:S(2)}, u32[]{:S(2)}) collective-permute-start(bf16[32,6144]{1,0:T(8,128)(2,1)} %copy-done.35), channel_id=1, source_target_pairs={{0,1},{1,0},{2,3},{3,2},{4,5},{5,4},{6,7},{7,6},{8,9},{9,8},{10,11... | collective-permute-start | bytes 1179656 | tf_op jit(solution)/shard_map/ppermute | solution.py:23
  129.9 27.1 %collective-permute-start.31 = (bf16[2,256,384]{2,1,0:T(8,128)(2,1)S(1)}, bf16[2,256,384]{2,1,0:T(8,128)(2,1)S(1)}, u32[]{:S(2)}, u32[]{:S(2)}) collective-permute-start(bf16[2,256,384]{2,1,0:T(8,128)(2,1)S(1)} %copy-done.16), channel_id=1, source_target_pairs={{0,128},{8,136},{16,144},{24,152},{32,160},{40,168},{48,176},{56,1... | collective-permute-start | bytes 1179656 | tf_op jit(solution)/shard_map/ppermute | solution.py:33
  130.0 19.9 %collective-permute-start.16 = (bf16[32,6144]{1,0:T(8,128)(2,1)S(1)}, bf16[32,6144]{1,0:T(8,128)(2,1)S(1)}, u32[]{:S(2)}, u32[]{:S(2)}) collective-permute-start(bf16[32,6144]{1,0:T(8,128)(2,1)S(1)} %copy-done.30), channel_id=1, source_target_pairs={{0,1},{1,0},{2,3},{3,2},{4,5},{5,4},{6,7},{7,6},{8,9},{9,8},{10,11... | collective-permute-start | bytes 1179656 | tf_op jit(solution)/shard_map/ppermute | solution.py:23
  132.4 11.5 %collective-permute-start.20 = (bf16[32,6144]{1,0:T(8,128)(2,1)S(1)}, bf16[32,6144]{1,0:T(8,128)(2,1)S(1)}, u32[]{:S(2)}, u32[]{:S(2)}) collective-permute-start(bf16[32,6144]{1,0:T(8,128)(2,1)S(1)} %copy-done.32), channel_id=1, source_target_pairs={{0,3},{1,2},{2,1},{3,0},{4,7},{5,6},{6,5},{7,4},{8,11},{9,10},{10,... | collective-permute-start | bytes 1179656 | tf_op jit(solution)/shard_map/ppermute | solution.py:23
  133.4 8.4 %copy-start.28 = (bf16[256,384]{1,0:T(8,128)(2,1)S(1)}, bf16[256,384]{1,0:T(8,128)(2,1)}, u32[]{:S(2)}) copy-start(bf16[256,384]{1,0:T(8,128)(2,1)} %copy-done.27) | copy-start | bytes 589828
  134.5 22.6 %collective-permute-start.26 = (bf16[32,6144]{1,0:T(8,128)(2,1)S(1)}, bf16[32,6144]{1,0:T(8,128)(2,1)S(1)}, u32[]{:S(2)}, u32[]{:S(2)}) collective-permute-start(bf16[32,6144]{1,0:T(8,128)(2,1)S(1)} %add.118), channel_id=1, source_target_pairs={{0,4},{1,5},{2,6},{3,7},{4,0},{5,1},{6,2},{7,3},{8,12},{9,13},{10,... | collective-permute-start | bytes 1179656 | tf_op jit(solution)/shard_map/ppermute | solution.py:23
  141.5 10.6 %collective-permute-start.23 = (bf16[32,6144]{1,0:T(8,128)(2,1)S(1)}, bf16[32,6144]{1,0:T(8,128)(2,1)S(1)}, u32[]{:S(2)}, u32[]{:S(2)}) collective-permute-start(bf16[32,6144]{1,0:T(8,128)(2,1)S(1)} %add.160), channel_id=1, source_target_pairs={{0,4},{1,5},{2,6},{3,7},{4,0},{5,1},{6,2},{7,3},{8,12},{9,13},{10,... | collective-permute-start | bytes 1179656 | tf_op jit(solution)/shard_map/ppermute | solution.py:23
  143.8 16.3 %collective-permute-start.28 = (bf16[32,6144]{1,0:T(8,128)(2,1)S(1)}, bf16[32,6144]{1,0:T(8,128)(2,1)S(1)}, u32[]{:S(2)}, u32[]{:S(2)}) collective-permute-start(bf16[32,6144]{1,0:T(8,128)(2,1)S(1)} %add.120), channel_id=1, source_target_pairs={{0,3},{1,2},{2,1},{3,0},{4,7},{5,6},{6,5},{7,4},{8,11},{9,10},{10,... | collective-permute-start | bytes 1179656 | tf_op jit(solution)/shard_map/ppermute | solution.py:23
  145.0 9.8 %copy-start.14 = (bf16[32,6144]{1,0:T(8,128)(2,1)S(1)}, bf16[32,6144]{1,0:T(8,128)(2,1)}, u32[]{:S(2)}) copy-start(bf16[32,6144]{1,0:T(8,128)(2,1)} %copy-done.13) | copy-start | bytes 1179652
  150.0 15.4 %collective-permute-start.29 = (bf16[32,6144]{1,0:T(8,128)(2,1)S(1)}, bf16[32,6144]{1,0:T(8,128)(2,1)S(1)}, u32[]{:S(2)}, u32[]{:S(2)}) collective-permute-start(bf16[32,6144]{1,0:T(8,128)(2,1)S(1)} %add.113.refs_0_), channel_id=1, source_target_pairs={{0,1},{1,0},{2,3},{3,2},{4,5},{5,4},{6,7},{7,6},{8,9},{9,8},{10,11... | collective-permute-start | bytes 1179656 | tf_op jit(solution)/shard_map/ppermute | solution.py:23
  152.1 8.5 %collective-permute-start.19 = (bf16[32,6144]{1,0:T(8,128)(2,1)S(1)}, bf16[32,6144]{1,0:T(8,128)(2,1)S(1)}, u32[]{:S(2)}, u32[]{:S(2)}) collective-permute-start(bf16[32,6144]{1,0:T(8,128)(2,1)S(1)} %add.158), channel_id=1, source_target_pairs={{0,4},{1,5},{2,6},{3,7},{4,0},{5,1},{6,2},{7,3},{8,12},{9,13},{10,... | collective-permute-start | bytes 1179656 | tf_op jit(solution)/shard_map/ppermute | solution.py:23
  157.0 8.4 %collective-permute-start.21 = (bf16[32,6144]{1,0:T(8,128)(2,1)S(1)}, bf16[32,6144]{1,0:T(8,128)(2,1)S(1)}, u32[]{:S(2)}, u32[]{:S(2)}) collective-permute-start(bf16[32,6144]{1,0:T(8,128)(2,1)S(1)} %add.159), channel_id=1, source_target_pairs={{0,1},{1,0},{2,3},{3,2},{4,5},{5,4},{6,7},{7,6},{8,9},{9,8},{10,11... | collective-permute-start | bytes 1179656 | tf_op jit(solution)/shard_map/ppermute | solution.py:23
  157.1 8.3 %collective-permute-start.24 = (bf16[32,6144]{1,0:T(8,128)(2,1)S(1)}, bf16[32,6144]{1,0:T(8,128)(2,1)S(1)}, u32[]{:S(2)}, u32[]{:S(2)}) collective-permute-start(bf16[32,6144]{1,0:T(8,128)(2,1)S(1)} %add.116), channel_id=1, source_target_pairs={{0,3},{1,2},{2,1},{3,0},{4,7},{5,6},{6,5},{7,4},{8,11},{9,10},{10,... | collective-permute-start | bytes 1179656 | tf_op jit(solution)/shard_map/ppermute | solution.py:23
  165.9 10.6 %collective-permute-start.30 = (bf16[32,6144]{1,0:T(8,128)(2,1)S(1)}, bf16[32,6144]{1,0:T(8,128)(2,1)S(1)}, u32[]{:S(2)}, u32[]{:S(2)}) collective-permute-start(bf16[32,6144]{1,0:T(8,128)(2,1)S(1)} %get-tuple-element.69), channel_id=1, source_target_pairs={{0,128},{8,136},{16,144},{24,152},{32,160},{40,168},{48,176},{56,1... | collective-permute-start | bytes 1179656 | tf_op jit(solution)/shard_map/ppermute | solution.py:33
  166.7 9.9 %copy-start.36 = (bf16[1,192,768]{2,1,0:T(8,128)(2,1)S(1)}, bf16[1,192,768]{2,1,0:T(8,128)(2,1)}, u32[]{:S(2)}) copy-start(bf16[1,192,768]{2,1,0:T(8,128)(2,1)} %reduce-scatter.2.cloned.1.call-done) | copy-start | bytes 884740
  167.7 8.9 %collective-permute-start.33 = (bf16[192,384]{1,0:T(8,128)(2,1)S(1)}, bf16[192,384]{1,0:T(8,128)(2,1)S(1)}, u32[]{:S(2)}, u32[]{:S(2)}) collective-permute-start(bf16[192,384]{1,0:T(8,128)(2,1)S(1)} %dynamic-slice_bitcast_fusion.1), channel_id=1, source_target_pairs={{0,16},{8,24},{16,0},{24,8},{32,48},{40,56},{48,32},{56,40},{64,80... | collective-permute-start | bytes 442376 | tf_op jit(solution)/shard_map/ppermute | solution.py:33
  176.7 18.4 %collective-permute-start.34 = (f32[192,192]{0,1:T(8,128)S(1)}, f32[192,192]{0,1:T(8,128)S(1)}, u32[]{:S(2)}, u32[]{:S(2)}) collective-permute-start(f32[192,192]{0,1:T(8,128)S(1)} %dynamic-slice_bitcast_fusion), channel_id=1, source_target_pairs={{0,8},{8,0},{16,24},{24,16},{32,40},{40,32},{48,56},{56,48},{64,72... | collective-permute-start | bytes 442376 | tf_op jit(solution)/shard_map/ppermute | solution.py:33
  (26 other events, 103.5 us)
Sparse Core Ops, SparseCore 0:
  109.6 54.4 reduce-scatter.1

commit v3 on v2

--- a/solution.py
+++ b/solution.py
@@ -14,7 +14,7 @@
 masked_score = -1e30
 BF = jnp.bfloat16
 F32 = jnp.float32
-VMEM_LIMIT = 8 * 1024 * 1024
+VMEM_LIMIT = 10 * 1024 * 1024
 BLK = 1024
 SMALL = pl.CostEstimate(flops=1, bytes_accessed=1, transcendentals=0)
 
@@ -119,6 +119,23 @@
         cost_estimate=SMALL,
         name="add",
     )(a, b, *after)
+
+
+def sum_kernel(a_ref, b_ref, c_ref, d_ref, *refs):
+    parts = (a_ref[...], b_ref[...], c_ref[...], d_ref[...])
+    refs[-1][...] = sum(p.astype(F32) for p in parts).astype(BF)
+
+
+def sum_last(parts, after):
+    return pl.pallas_call(
+        sum_kernel,
+        in_specs=[VM] * 4 + [ANY] * len(after),
+        out_specs=VM,
+        out_shape=jax.ShapeDtypeStruct(parts[0].shape, BF),
+        compiler_params=pltpu.CompilerParams(vmem_limit_bytes=VMEM_LIMIT),
+        cost_estimate=SMALL,
+        name="sum_last",
+    )(*parts, *after)
 
 
 def value_kernel(*refs):
@@ -259,16 +276,18 @@
         in_specs=[pl.BlockSpec(memory_space=pltpu.SMEM)] + [VM] * 18 + [ANY] * len(after),
         out_specs=[VM, VM],
         out_shape=[shape, shape],
-        compiler_params=pltpu.CompilerParams(vmem_limit_bytes=VMEM_LIMIT),
+        compiler_params=pltpu.CompilerParams(vmem_limit_bytes=2 * VMEM_LIMIT),
         cost_estimate=SMALL,
         name="weight_terms",
     )(core, *chunks, vgt_a, vgt_b, *after)
 
 
-def weight_sum(keep, sent, xl, core, after):
-    u = add(keep, other_core(sent), after)
+def over_z(u):
     groups = [[(z * 2 + x) * 2 + c for z in range(N_Z)] for x in range(2) for c in range(2)]
-    u = lax.psum_scatter(u, "dp", scatter_dimension=0, axis_index_groups=groups)
+    return lax.psum_scatter(u, "dp", scatter_dimension=0, axis_index_groups=groups)
+
+
+def weight_sum(u, xl, core):
     half, lanes = u.shape[0], u.shape[1] // 2
     mine = lax.dynamic_slice_in_dim(u, xl * lanes, lanes, 1).astype(F32)
     theirs = lax.dynamic_slice_in_dim(u, (1 - xl) * lanes, lanes, 1)
@@ -330,16 +349,20 @@
     keep, sent = weight_terms(
         core.astype(jnp.int32).reshape(1), rows_a + rows_b, vgt_a, vgt_b, [])
     terms_b = row_terms(vg_b, w_value, [sent])
-    weight_grad = weight_sum(keep, sent, xl, core, [terms_b[0]] + [])
-
-    first_b = scatter_first(terms_b, 3, 1, lambda x, y: x + y)
+    both_cores = add(keep, other_core(sent), [terms_b[0]])
+    z_sum = over_z(both_cores)
+    weight_grad = weight_sum(z_sum, xl, core)
+
+    first_b = scatter_first(terms_b, 3, 1, lambda x, y: add(x, y, [both_cores]))
     next_b = scatter_next(terms_b, first_b, 1)
-    late = lambda x, y: add(x, y, [next_b])
+    grad_b = scatter_last(terms_b, first_b, next_b, 3, 1)
+    back_rows = to_partner(grad_b)
+    late = lambda x, y: add(x, y, [grad_b])
     first_a = (late(terms_a[7], arrived_a[0]), late(terms_a[1], arrived_a[1]),
                late(terms_a[4], arrived_a[2]))
     next_a = scatter_next(terms_a, first_a, 3)
-    grad_b = scatter_last(terms_b, first_b, next_b, 3, 1)
-    grad_a = scatter_last(terms_a, first_a, next_a, 1, 3)
+    last_a = [terms_a[0], swap(first_a[2], 4), swap(first_a[1], 1), swap(next_a, 3)]
+    grad_a = sum_last(last_a, [z_sum])
 
     def by_slot(of_a, of_b):
         first = slot_a == 0
@@ -352,7 +375,7 @@
         return jnp.stack(rows).astype(BF)
 
     attended = jnp.stack(by_slot(att_a, att_b))
-    tile_grad = home(grad_a, grad_b, to_partner(grad_b))
+    tile_grad = home(grad_a, grad_b, back_rows)
     query_grad = home(dqk_a[0], dqk_b[0], back_qk[0])
     key_grad = home(dqk_a[1], dqk_b[1], back_qk[1])
     return (attended, tile_grad, query_grad, key_grad, weight_grad)

time: 204 us -> 198 us (0.971)
  starting transfers between devices: 70.4 us -> 60.9 us
  waiting for transfers between devices: 57.6 us -> 63.6 us
  other arithmetic: 11.3 us -> 6.78 us
    ppermute x7, starting transfers between devices: 34.6 us -> 25.7 us  [dp_perm(): return lax.ppermute(x, 'dp', pairs)]
    ppermute x7, waiting for transfers between devices: 12.3 us -> 16.5 us  [dp_perm(): return lax.ppermute(x, 'dp', pairs)]
    add x3 -> x0, other arithmetic: 3.17 us -> none  [shards(): first_b = scatter_first(terms_b, 3, 1, lambda x, y: x + y)]
    unnamed x77 -> x75, local copies, waits for them, and re-layouts: 9.29 us -> 10.9 us
  transfers between devices with their start and end apart: 36 -> 36, of which waited for: 15 -> 15; matrix products, arithmetic and copies ran while one was open for 7% -> 5% of each run, Pallas kernels for 8% -> 8%
where the time goes in v3:
time: 198 us; the launch traced here: 197 us
  waiting for transfers between devices  63.6 us (32%)
  starting transfers between devices  60.9 us (31%)
  Pallas kernels  29.1 us (15%)
  between operations  22.6 us (11%)
  local copies, waits for them, and re-layouts  14 us (7%)
  other arithmetic  6.78 us (3%)
    ppermute x28, waiting for transfers between devices, swap(): return lax.ppermute(x, 'tensor', [(i, i ^ d) for i in range(N_TENSOR)])  47 us
    ppermute x28, starting transfers between devices, swap(): return lax.ppermute(x, 'tensor', [(i, i ^ d) for i in range(N_TENSOR)])  35.2 us
    ppermute x7, starting transfers between devices, dp_perm(): return lax.ppermute(x, 'dp', pairs)  25.7 us
    ppermute x7, waiting for transfers between devices, dp_perm(): return lax.ppermute(x, 'dp', pairs)  16.5 us
    unnamed x75, local copies, waits for them, and re-layouts  10.9 us
    pallas_call x2, Pallas kernels, attend(): pl.pallas_call(functools.partial(attend_kernel, arrived), grid_spec=pltpu...  8.56 us
    pallas_call x2, Pallas kernels, project_values(): pl.pallas_call(value_kernel, in_specs=[VM] * 9 + [ANY] * len(after), out_...  6.77 us
    pallas_call x1, Pallas kernels, weight_terms(): pl.pallas_call(weight_kernel, in_specs=[pl.BlockSpec(memory_space=pltpu.S...  4.76 us
  transfers between devices with their start and end apart: 36, of which 15 were waited for; matrix products, arithmetic and copies ran while one was open for 5% of the time, Pallas kernels for 8%

profile of v3, /device:TPU:1, one launch (start us, length us, event | category | flops | bytes accessed | tf_op | source)
XLA Modules:
  0.0 196.9 jit_solution(9606414671974239418)
XLA Ops:
  7.2 1.3 copy-done.5
  8.6 7.8 %collective-permute-start.7 = (bf16[32,6144]{1,0:T(8,128)(2,1)S(1)}, bf16[32,6144]{1,0:T(8,128)(2,1)}, u32[]{:S(2)}, u32[]{:S(2)}) collective-permute-start(bf16[32,6144]{1,0:T(8,128)(2,1)S(1)} %bitcast.40), channel_id=1, source_target_pairs={{0,128},{8,136},{16,144},{24,152},{32,160},{40,168},{48,176},{56,1... | collective-permute-start | bytes 1179656 | tf_op jit(solution)/shard_map/ppermute | solution.py:33
  21.8 2.8 %collective-permute-start.3 = (bf16[32,6144]{1,0:T(8,128)(2,1)S(1)}, bf16[32,6144]{1,0:T(8,128)(2,1)S(1)}, u32[]{:S(2)}, u32[]{:S(2)}) collective-permute-start(bf16[32,6144]{1,0:T(8,128)(2,1)S(1)} %select_bitcast_fusion.3.refs_0_), channel_id=1, source_target_pairs={{0,4},{1,5},{2,6},{3,7},{4,0},{5,1},{6,2},{7,3},{8,12},{9,13},{10,... | collective-permute-start | bytes 1179656 | tf_op jit(solution)/shard_map/ppermute | solution.py:23
  24.6 2.7 %collective-permute-start.2 = (bf16[32,6144]{1,0:T(8,128)(2,1)S(1)}, bf16[32,6144]{1,0:T(8,128)(2,1)}, u32[]{:S(2)}, u32[]{:S(2)}) collective-permute-start(bf16[32,6144]{1,0:T(8,128)(2,1)S(1)} %select_bitcast_fusion.3.refs_0_), channel_id=1, source_target_pairs={{0,3},{1,2},{2,1},{3,0},{4,7},{5,6},{6,5},{7,4},{8,11},{9,10},{10,... | collective-permute-start | bytes 1179656 | tf_op jit(solution)/shard_map/ppermute | solution.py:23
  28.1 1.5 collective-permute-start.8
  29.6 1.6 collective-permute-start.11
  31.2 4.2 %collective-permute-done.2.refs_3_ = bf16[32,6144]{1,0:T(8,128)(2,1)} collective-permute-done((bf16[32,6144]{1,0:T(8,128)(2,1)S(1)}, bf16[32,6144]{1,0:T(8,128)(2,1)}, u32[]{:S(2)}, u32[]{:S(2)}) %collective-permute-start.2) | collective-permute-done | bytes 393248 | tf_op jit(solution)/shard_map/ppermute | solution.py:23
  35.7 2.6 %collective-permute-start.9 = (bf16[32,6144]{1,0:T(8,128)(2,1)S(1)}, bf16[32,6144]{1,0:T(8,128)(2,1)}, u32[]{:S(2)}, u32[]{:S(2)}) collective-permute-start(bf16[32,6144]{1,0:T(8,128)(2,1)S(1)} %bitcast_select_fusion.refs_0_.refs_8_), channel_id=1, source_target_pairs={{0,3},{1,2},{2,1},{3,0},{4,7},{5,6},{6,5},{7,4},{8,11},{9,10},{10,... | collective-permute-start | bytes 1179656 | tf_op jit(solution)/shard_map/ppermute | solution.py:23
  38.4 6.6 %collective-permute-done.8.refs_1_.refs_9_ = bf16[32,6144]{1,0:T(8,128)(2,1)S(1)} collective-permute-done((bf16[32,6144]{1,0:T(8,128)(2,1)S(1)}, bf16[32,6144]{1,0:T(8,128)(2,1)S(1)}, u32[]{:S(2)}, u32[]{:S(2)}) %collective-permute-start.8) | collective-permute-done | bytes 393248 | tf_op jit(solution)/shard_map/ppermute | solution.py:23
  45.4 3.7 %collective-permute-done.5.refs_7_ = bf16[32,6144]{1,0:T(8,128)(2,1)} collective-permute-done((bf16[32,6144]{1,0:T(8,128)(2,1)}, bf16[32,6144]{1,0:T(8,128)(2,1)}, u32[]{:S(2)}, u32[]{:S(2)}) %collective-permute-start.5) | collective-permute-done | bytes 393248 | tf_op jit(solution)/shard_map/ppermute | solution.py:23
  49.0 2.3 %collective-permute-start.6 = (bf16[32,6144]{1,0:T(8,128)(2,1)}, bf16[32,6144]{1,0:T(8,128)(2,1)}, u32[]{:S(2)}, u32[]{:S(2)}) collective-permute-start(bf16[32,6144]{1,0:T(8,128)(2,1)} %collective-permute-done.5.refs_7_), channel_id=1, source_target_pairs={{0,1},{1,0},{2,3},{3,2},{4,5},{5,4},{6,7},{7,6},{8,9},{9,8},{10,11... | collective-permute-start | bytes 1179656 | tf_op jit(solution)/shard_map/ppermute | solution.py:23
  51.3 1.9 collective-permute-start.14
  53.6 4.1 %collective-permute-done.12.refs_5_.refs_13_ = bf16[32,6144]{1,0:T(8,128)(2,1)} collective-permute-done((bf16[32,6144]{1,0:T(8,128)(2,1)S(1)}, bf16[32,6144]{1,0:T(8,128)(2,1)}, u32[]{:S(2)}, u32[]{:S(2)}) %collective-permute-start.12) | collective-permute-done | bytes 393248 | tf_op jit(solution)/shard_map/ppermute | solution.py:23
  57.8 3.4 %collective-permute-start.13 = (bf16[32,6144]{1,0:T(8,128)(2,1)}, bf16[32,6144]{1,0:T(8,128)(2,1)}, u32[]{:S(2)}, u32[]{:S(2)}) collective-permute-start(bf16[32,6144]{1,0:T(8,128)(2,1)} %collective-permute-done.12.refs_5_.refs_13_), channel_id=1, source_target_pairs={{0,3},{1,2},{2,1},{3,0},{4,7},{5,6},{6,5},{7,4},{8,11},{9,10},{10,... | collective-permute-start | bytes 1179656 | tf_op jit(solution)/shard_map/ppermute | solution.py:23
  64.3 2.3 %copy-done.1 = bf16[6144,384]{1,0:T(8,128)(2,1)S(1)} copy-done((bf16[6144,384]{1,0:T(8,128)(2,1)S(1)}, bf16[6144,384]{1,0:T(8,128)(2,1)}, u32[]{:S(2)}) %copy-start.1) | copy-done | bytes 4718616
  66.7 1.0 copy-done.8
  67.7 3.3 %project_values.2.refs_2_ = bf16[256,384]{1,0:T(8,128)(2,1)S(1)} custom-call(bf16[32,6144]{1,0:T(8,128)(2,1)S(1)} %select_bitcast_fusion.3.refs_0_, bf16[32,6144]{1,0:T(8,128)(2,1)} %collective-permute-done.refs_1_, bf16[32,6144]{1,0:T(8,128)(2,1)S(1)} %collective-permute-done.1.refs_2_, bf16[32,6144]{1,0:T(8,128)(2,1)} %collective-permute-done.2.refs_3_, ...), custom_call_target="tpu_custom_call" | custom-call | flops 1 | bytes 1 | tf_op jit(solution)/shard_map/project_values/pallas_call | solution.py:154
  71.0 3.8 %attend.2 = (bf16[256,384]{1,0:T(8,128)(2,1)S(1)}, bf16[256,384]{1,0:T(8,128)(2,1)S(1)}, bf16[384,256]{1,0:T(8,128)(2,1)S(1)}, bf16[2,256,384]{2,1,0:T(8,128)(2,1)S(1)}) custom-call(s32[4]{0:T(128)S(1)} %pad_add_fusion.me_ref, bf16[3,256,384]{2,1,0:T(8,128)(2,1)S(1)} %copy-done.3, bf16[3,256,384]{2,1,0:T(8,128)(2,1)S(1)} %copy-done.4, ...), custom_call_target="tpu_custom_call" | custom-call | flops 1 | bytes 1 | tf_op jit(solution)/shard_map/attend/pallas_call | solution.py:208
  76.3 3.4 %project_values.3.refs_0_.refs_2_ = bf16[256,384]{1,0:T(8,128)(2,1)S(1)} custom-call(bf16[32,6144]{1,0:T(8,128)(2,1)S(1)} %bitcast_select_fusion.refs_0_.refs_8_, bf16[32,6144]{1,0:T(8,128)(2,1)S(1)} %collective-permute-done.8.refs_1_.refs_9_, bf16[32,6144]{1,0:T(8,128)(2,1)} %collective-permute-done.10.refs_2_.refs_10_, ...), custom_call_target="tpu_custom_call" | custom-call | flops 1 | bytes 1 | tf_op jit(solution)/shard_map/project_values/pallas_call | solution.py:154
  79.7 1.8 row_terms.2
  82.4 4.8 %attend.3 = (bf16[256,384]{1,0:T(8,128)(2,1)S(1)}, bf16[256,384]{1,0:T(8,128)(2,1)S(1)}, bf16[384,256]{1,0:T(8,128)(2,1)S(1)}, bf16[2,256,384]{2,1,0:T(8,128)(2,1)S(1)}) custom-call(s32[4]{0:T(128)S(1)} %pad_add_fusion.1.me_ref, bf16[3,256,384]{2,1,0:T(8,128)(2,1)S(1)} %copy-done.3, bf16[3,256,384]{2,1,0:T(8,128)(2,1)S(1)} %copy-done.4, ...), custom_call_target="tpu_custom_call" | custom-call | flops 1 | bytes 1 | tf_op jit(solution)/shard_map/attend/pallas_call | solution.py:208
  88.7 4.8 %weight_terms.1 = (bf16[8,192,768]{2,1,0:T(8,128)(2,1)S(1)}, bf16[8,192,768]{2,1,0:T(8,128)(2,1)S(1)}) custom-call(s32[1]{0:T(128)} %bitcast.14.core_ref, bf16[32,6144]{1,0:T(8,128)(2,1)S(1)} %select_bitcast_fusion.3.refs_0_, bf16[32,6144]{1,0:T(8,128)(2,1)} %collective-permute-done.refs_1_, bf16[32,6144]{1,0:T(8,128)(2,1)S(1)} %collective-permute-done.1.refs_2_, ...), custom_call_target="tpu_custom_call" | custom-call | flops 1 | bytes 1 | tf_op jit(solution)/shard_map/weight_terms/pallas_call | solution.py:274
  93.5 9.2 %collective-permute-start.18 = (bf16[8,192,768]{2,1,0:T(8,128)(2,1)S(1)}, bf16[8,192,768]{2,1,0:T(8,128)(2,1)S(1)}, u32[]{:S(2)}, u32[]{:S(2)}) collective-permute-start(bf16[8,192,768]{2,1,0:T(8,128)(2,1)S(1)} %get-tuple-element.40.refs_0_), channel_id=1, source_target_pairs={{0,8},{8,0},{16,24},{24,16},{32,40},{40,32},{48,56},{56,48},{64,72... | collective-permute-start | bytes 7077896 | tf_op jit(solution)/shard_map/ppermute | solution.py:33
  102.7 2.8 %row_terms.3 = (bf16[32,6144]{1,0:T(8,128)(2,1)S(1)}, bf16[32,6144]{1,0:T(8,128)(2,1)S(1)}, bf16[32,6144]{1,0:T(8,128)(2,1)}, bf16[32,6144]{1,0:T(8,128)(2,1)S(1...) custom-call(bf16[256,384]{1,0:T(8,128)(2,1)S(1)} %get-tuple-element., ...), custom_call_target="tpu_custom_call" | custom-call | flops 1 | bytes 1 | tf_op jit(solution)/shard_map/row_terms/pallas_call | solution.py:247
  105.5 1.4 collective-permute-done.18.b_ref
  106.8 3.1 %add.128.refs_0_ = bf16[8,192,768]{2,1,0:T(8,128)(2,1)} custom-call(bf16[8,192,768]{2,1,0:T(8,128)(2,1)S(1)} %get-tuple-element.44.a_ref, bf16[8,192,768]{2,1,0:T(8,128)(2,1)S(1)} %collective-permute-done.18.b_ref, bf16[32,6144]{1,0:T(8,128)(2,1)S(1)} %get-tuple-element.41.refs_0_), custom_call_target="tpu_custom_call" | custom-call | flops 1 | bytes 1 | tf_op jit(solution)/shard_map/add/pallas_call | solution.py:112
  110.0 1.1 collective-permute-start.22
  111.0 1.7 collective-permute-start.17
  112.7 9.1 %collective-permute-done.22.b_ref = bf16[32,6144]{1,0:T(8,128)(2,1)S(1)} collective-permute-done((bf16[32,6144]{1,0:T(8,128)(2,1)}, bf16[32,6144]{1,0:T(8,128)(2,1)S(1)}, u32[]{:S(2)}, u32[]{:S(2)}) %collective-permute-start.22) | collective-permute-done | bytes 393248 | tf_op jit(solution)/shard_map/ppermute | solution.py:23
  121.8 2.8 %collective-permute-start.23 = (bf16[32,6144]{1,0:T(8,128)(2,1)S(1)}, bf16[32,6144]{1,0:T(8,128)(2,1)S(1)}, u32[]{:S(2)}, u32[]{:S(2)}) collective-permute-start(bf16[32,6144]{1,0:T(8,128)(2,1)S(1)} %add.131), channel_id=1, source_target_pairs={{0,4},{1,5},{2,6},{3,7},{4,0},{5,1},{6,2},{7,3},{8,12},{9,13},{10,... | collective-permute-start | bytes 1179656 | tf_op jit(solution)/shard_map/ppermute | solution.py:23
  128.7 1.5 collective-permute-done.17.b_ref
  130.3 2.8 %collective-permute-start.19 = (bf16[32,6144]{1,0:T(8,128)(2,1)S(1)}, bf16[32,6144]{1,0:T(8,128)(2,1)S(1)}, u32[]{:S(2)}, u32[]{:S(2)}) collective-permute-start(bf16[32,6144]{1,0:T(8,128)(2,1)S(1)} %add.129), channel_id=1, source_target_pairs={{0,4},{1,5},{2,6},{3,7},{4,0},{5,1},{6,2},{7,3},{8,12},{9,13},{10,... | collective-permute-start | bytes 1179656 | tf_op jit(solution)/shard_map/ppermute | solution.py:23
  133.2 1.2 collective-permute-start.21
  135.4 5.8 %collective-permute-done.19 = bf16[32,6144]{1,0:T(8,128)(2,1)S(1)} collective-permute-done((bf16[32,6144]{1,0:T(8,128)(2,1)S(1)}, bf16[32,6144]{1,0:T(8,128)(2,1)S(1)}, u32[]{:S(2)}, u32[]{:S(2)}) %collective-permute-start.19) | collective-permute-done | bytes 393248 | tf_op jit(solution)/shard_map/ppermute | solution.py:23
  141.3 1.2 collective-permute-start.26
  142.4 1.3 collective-permute-done.21
  143.7 2.1 %collective-permute-done.24 = bf16[32,6144]{1,0:T(8,128)(2,1)S(1)} collective-permute-done((bf16[32,6144]{1,0:T(8,128)(2,1)S(1)}, bf16[32,6144]{1,0:T(8,128)(2,1)S(1)}, u32[]{:S(2)}, u32[]{:S(2)}) %collective-permute-start.24) | collective-permute-done | bytes 393248 | tf_op jit(solution)/shard_map/ppermute | solution.py:23
  146.0 5.0 %collective-permute-start.31 = (bf16[32,6144]{1,0:T(8,128)(2,1)S(1)}, bf16[32,6144]{1,0:T(8,128)(2,1)S(1)}, u32[]{:S(2)}, u32[]{:S(2)}) collective-permute-start(bf16[32,6144]{1,0:T(8,128)(2,1)S(1)} %add_convert_fusion.refs_0_), channel_id=1, source_target_pairs={{0,128},{8,136},{16,144},{24,152},{32,160},{40,168},{48,176},{56,1... | collective-permute-start | bytes 1179656 | tf_op jit(solution)/shard_map/ppermute | solution.py:33
  151.0 4.0 %collective-permute-done.28.b_ref = bf16[32,6144]{1,0:T(8,128)(2,1)S(1)} collective-permute-done((bf16[32,6144]{1,0:T(8,128)(2,1)S(1)}, bf16[32,6144]{1,0:T(8,128)(2,1)S(1)}, u32[]{:S(2)}, u32[]{:S(2)}) %collective-permute-start.28) | collective-permute-done | bytes 393248 | tf_op jit(solution)/shard_map/ppermute | solution.py:23
  156.1 1.2 pad_maximum_fusion.1
  157.4 2.9 %collective-permute-start.25 = (bf16[32,6144]{1,0:T(8,128)(2,1)S(1)}, bf16[32,6144]{1,0:T(8,128)(2,1)S(1)}, u32[]{:S(2)}, u32[]{:S(2)}) collective-permute-start(bf16[32,6144]{1,0:T(8,128)(2,1)S(1)} %add.132), channel_id=1, source_target_pairs={{0,4},{1,5},{2,6},{3,7},{4,0},{5,1},{6,2},{7,3},{8,12},{9,13},{10,... | collective-permute-start | bytes 1179656 | tf_op jit(solution)/shard_map/ppermute | solution.py:23
  160.5 4.0 %collective-permute-done.29 = bf16[32,6144]{1,0:T(8,128)(2,1)S(1)} collective-permute-done((bf16[32,6144]{1,0:T(8,128)(2,1)S(1)}, bf16[32,6144]{1,0:T(8,128)(2,1)S(1)}, u32[]{:S(2)}, u32[]{:S(2)}) %collective-permute-start.29) | collective-permute-done | bytes 393248 | tf_op jit(solution)/shard_map/ppermute | solution.py:23
  164.6 1.5 collective-permute-start.30
  166.1 13.1 %collective-permute-done.31 = bf16[32,6144]{1,0:T(8,128)(2,1)S(1)} collective-permute-done((bf16[32,6144]{1,0:T(8,128)(2,1)S(1)}, bf16[32,6144]{1,0:T(8,128)(2,1)S(1)}, u32[]{:S(2)}, u32[]{:S(2)}) %collective-permute-start.31) | collective-permute-done | bytes 393248 | tf_op jit(solution)/shard_map/ppermute | solution.py:33
  180.3 1.0 copy-done.13
  182.2 2.1 %collective-permute-done.33 = bf16[192,384]{1,0:T(8,128)(2,1)S(1)} collective-permute-done((bf16[192,384]{1,0:T(8,128)(2,1)S(1)}, bf16[192,384]{1,0:T(8,128)(2,1)S(1)}, u32[]{:S(2)}, u32[]{:S(2)}) %collective-permute-start.33) | collective-permute-done | bytes 147488 | tf_op jit(solution)/shard_map/ppermute | solution.py:33
  184.4 3.5 %collective-permute-start.34 = (f32[192,192]{0,1:T(8,128)S(1)}, f32[192,192]{0,1:T(8,128)S(1)}, u32[]{:S(2)}, u32[]{:S(2)}) collective-permute-start(f32[192,192]{0,1:T(8,128)S(1)} %dynamic-slice_bitcast_fusion), channel_id=1, source_target_pairs={{0,8},{8,0},{16,24},{24,16},{32,40},{40,32},{48,56},{56,48},{64,72... | collective-permute-start | bytes 442376 | tf_op jit(solution)/shard_map/ppermute | solution.py:33
  187.9 1.1 pad_maximum_fusion
  (145 shorter events, 16.1 us)
Async XLA Ops:
  7.2 9.2 %copy-start = (s32[32,3]{0,1:T(4,128)S(1)}, s32[32,3]{0,1:T(4,128)}, u32[]{:S(2)}) copy-start(s32[32,3]{0,1:T(4,128)} %param.12) | copy-start | bytes 1156
  7.2 172.0 %reduce-scatter.2.cloned.1.call-start = ((), (), s32[]{:S(2)}) async-start(), calls=%async_computation.1 | async-start | bytes 2654208 | tf_op jit(solution)/shard_map/reduce_scatter | solution.py:287
  8.5 12.6 %copy-start.6 = (bf16[3,32,6144]{2,1,0:T(8,128)(2,1)S(1)}, bf16[3,32,6144]{2,1,0:T(8,128)(2,1)}, u32[]{:S(2)}) copy-start(bf16[3,32,6144]{2,1,0:T(8,128)(2,1)} %refs_0_.5) | copy-start | bytes 3538948
  8.5 52.6 %copy-start.3 = (bf16[3,256,384]{2,1,0:T(8,128)(2,1)S(1)}, bf16[3,256,384]{2,1,0:T(8,128)(2,1)}, u32[]{:S(2)}) copy-start(bf16[3,256,384]{2,1,0:T(8,128)(2,1)} %refs_0_.7) | copy-start | bytes 1769476
  8.5 52.6 %copy-start.4 = (bf16[3,256,384]{2,1,0:T(8,128)(2,1)S(1)}, bf16[3,256,384]{2,1,0:T(8,128)(2,1)}, u32[]{:S(2)}) copy-start(bf16[3,256,384]{2,1,0:T(8,128)(2,1)} %refs_1_.5) | copy-start | bytes 1769476
  8.6 18.8 %collective-permute-start.7 = (bf16[32,6144]{1,0:T(8,128)(2,1)S(1)}, bf16[32,6144]{1,0:T(8,128)(2,1)}, u32[]{:S(2)}, u32[]{:S(2)}) collective-permute-start(bf16[32,6144]{1,0:T(8,128)(2,1)S(1)} %bitcast.40), channel_id=1, source_target_pairs={{0,128},{8,136},{16,144},{24,152},{32,160},{40,168},{48,176},{56,1... | collective-permute-start | bytes 1179656 | tf_op jit(solution)/shard_map/ppermute | solution.py:33
  21.8 13.9 %collective-permute-start.3 = (bf16[32,6144]{1,0:T(8,128)(2,1)S(1)}, bf16[32,6144]{1,0:T(8,128)(2,1)S(1)}, u32[]{:S(2)}, u32[]{:S(2)}) collective-permute-start(bf16[32,6144]{1,0:T(8,128)(2,1)S(1)} %select_bitcast_fusion.3.refs_0_), channel_id=1, source_target_pairs={{0,4},{1,5},{2,6},{3,7},{4,0},{5,1},{6,2},{7,3},{8,12},{9,13},{10,... | collective-permute-start | bytes 1179656 | tf_op jit(solution)/shard_map/ppermute | solution.py:23
  24.6 10.8 %collective-permute-start.2 = (bf16[32,6144]{1,0:T(8,128)(2,1)S(1)}, bf16[32,6144]{1,0:T(8,128)(2,1)}, u32[]{:S(2)}, u32[]{:S(2)}) collective-permute-start(bf16[32,6144]{1,0:T(8,128)(2,1)S(1)} %select_bitcast_fusion.3.refs_0_), channel_id=1, source_target_pairs={{0,3},{1,2},{2,1},{3,0},{4,7},{5,6},{6,5},{7,4},{8,11},{9,10},{10,... | collective-permute-start | bytes 1179656 | tf_op jit(solution)/shard_map/ppermute | solution.py:23
  27.4 10.9 %collective-permute-start = (bf16[32,6144]{1,0:T(8,128)(2,1)S(1)}, bf16[32,6144]{1,0:T(8,128)(2,1)}, u32[]{:S(2)}, u32[]{:S(2)}) collective-permute-start(bf16[32,6144]{1,0:T(8,128)(2,1)S(1)} %select_bitcast_fusion.3.refs_0_), channel_id=1, source_target_pairs={{0,1},{1,0},{2,3},{3,2},{4,5},{5,4},{6,7},{7,6},{8,9},{9,8},{10,11... | collective-permute-start | bytes 1179656 | tf_op jit(solution)/shard_map/ppermute | solution.py:23
  28.1 35.9 %copy-start.36 = (s32[2,256]{1,0:T(2,128)S(1)}, s32[2,256]{1,0:T(2,128)}, u32[]{:S(2)}) copy-start(s32[2,256]{1,0:T(2,128)} %param.13) | copy-start | bytes 6148
  28.1 16.9 %collective-permute-start.8 = (bf16[32,6144]{1,0:T(8,128)(2,1)S(1)}, bf16[32,6144]{1,0:T(8,128)(2,1)S(1)}, u32[]{:S(2)}, u32[]{:S(2)}) collective-permute-start(bf16[32,6144]{1,0:T(8,128)(2,1)S(1)} %bitcast_select_fusion.refs_0_.refs_8_), channel_id=1, source_target_pairs={{0,1},{1,0},{2,3},{3,2},{4,5},{5,4},{6,7},{7,6},{8,9},{9,8},{10,11... | collective-permute-start | bytes 1179656 | tf_op jit(solution)/shard_map/ppermute | solution.py:23
  29.6 15.6 %collective-permute-start.11 = (bf16[32,6144]{1,0:T(8,128)(2,1)S(1)}, bf16[32,6144]{1,0:T(8,128)(2,1)}, u32[]{:S(2)}, u32[]{:S(2)}) collective-permute-start(bf16[32,6144]{1,0:T(8,128)(2,1)S(1)} %bitcast_select_fusion.refs_0_.refs_8_), channel_id=1, source_target_pairs={{0,4},{1,5},{2,6},{3,7},{4,0},{5,1},{6,2},{7,3},{8,12},{9,13},{10,... | collective-permute-start | bytes 1179656 | tf_op jit(solution)/shard_map/ppermute | solution.py:23
  35.4 13.6 %collective-permute-start.5 = (bf16[32,6144]{1,0:T(8,128)(2,1)}, bf16[32,6144]{1,0:T(8,128)(2,1)}, u32[]{:S(2)}, u32[]{:S(2)}) collective-permute-start(bf16[32,6144]{1,0:T(8,128)(2,1)} %collective-permute-done.2.refs_3_), channel_id=1, source_target_pairs={{0,4},{1,5},{2,6},{3,7},{4,0},{5,1},{6,2},{7,3},{8,12},{9,13},{10,... | collective-permute-start | bytes 1179656 | tf_op jit(solution)/shard_map/ppermute | solution.py:23
  35.7 15.6 %collective-permute-start.9 = (bf16[32,6144]{1,0:T(8,128)(2,1)S(1)}, bf16[32,6144]{1,0:T(8,128)(2,1)}, u32[]{:S(2)}, u32[]{:S(2)}) collective-permute-start(bf16[32,6144]{1,0:T(8,128)(2,1)S(1)} %bitcast_select_fusion.refs_0_.refs_8_), channel_id=1, source_target_pairs={{0,3},{1,2},{2,1},{3,0},{4,7},{5,6},{6,5},{7,4},{8,11},{9,10},{10,... | collective-permute-start | bytes 1179656 | tf_op jit(solution)/shard_map/ppermute | solution.py:23
  38.3 15.4 %collective-permute-start.1 = (bf16[32,6144]{1,0:T(8,128)(2,1)}, bf16[32,6144]{1,0:T(8,128)(2,1)S(1)}, u32[]{:S(2)}, u32[]{:S(2)}) collective-permute-start(bf16[32,6144]{1,0:T(8,128)(2,1)} %collective-permute-done.refs_1_), channel_id=1, source_target_pairs={{0,3},{1,2},{2,1},{3,0},{4,7},{5,6},{6,5},{7,4},{8,11},{9,10},{10,... | collective-permute-start | bytes 1179656 | tf_op jit(solution)/shard_map/ppermute | solution.py:23
  45.0 12.8 %collective-permute-start.12 = (bf16[32,6144]{1,0:T(8,128)(2,1)S(1)}, bf16[32,6144]{1,0:T(8,128)(2,1)}, u32[]{:S(2)}, u32[]{:S(2)}) collective-permute-start(bf16[32,6144]{1,0:T(8,128)(2,1)S(1)} %collective-permute-done.8.refs_1_.refs_9_), channel_id=1, source_target_pairs={{0,4},{1,5},{2,6},{3,7},{4,0},{5,1},{6,2},{7,3},{8,12},{9,13},{10,... | collective-permute-start | bytes 1179656 | tf_op jit(solution)/shard_map/ppermute | solution.py:23
  45.2 16.7 %collective-permute-start.4 = (bf16[32,6144]{1,0:T(8,128)(2,1)S(1)}, bf16[32,6144]{1,0:T(8,128)(2,1)S(1)}, u32[]{:S(2)}, u32[]{:S(2)}) collective-permute-start(bf16[32,6144]{1,0:T(8,128)(2,1)S(1)} %collective-permute-done.3.refs_4_), channel_id=1, source_target_pairs={{0,1},{1,0},{2,3},{3,2},{4,5},{5,4},{6,7},{7,6},{8,9},{9,8},{10,11... | collective-permute-start | bytes 1179656 | tf_op jit(solution)/shard_map/ppermute | solution.py:23
  49.0 15.3 %collective-permute-start.6 = (bf16[32,6144]{1,0:T(8,128)(2,1)}, bf16[32,6144]{1,0:T(8,128)(2,1)}, u32[]{:S(2)}, u32[]{:S(2)}) collective-permute-start(bf16[32,6144]{1,0:T(8,128)(2,1)} %collective-permute-done.5.refs_7_), channel_id=1, source_target_pairs={{0,1},{1,0},{2,3},{3,2},{4,5},{5,4},{6,7},{7,6},{8,9},{9,8},{10,11... | collective-permute-start | bytes 1179656 | tf_op jit(solution)/shard_map/ppermute | solution.py:23
  51.3 25.0 %collective-permute-start.14 = (bf16[32,6144]{1,0:T(8,128)(2,1)}, bf16[32,6144]{1,0:T(8,128)(2,1)}, u32[]{:S(2)}, u32[]{:S(2)}) collective-permute-start(bf16[32,6144]{1,0:T(8,128)(2,1)} %collective-permute-done.11.refs_4_.refs_12_), channel_id=1, source_target_pairs={{0,3},{1,2},{2,1},{3,0},{4,7},{5,6},{6,5},{7,4},{8,11},{9,10},{10,... | collective-permute-start | bytes 1179656 | tf_op jit(solution)/shard_map/ppermute | solution.py:23
  53.6 22.6 %collective-permute-start.10 = (bf16[32,6144]{1,0:T(8,128)(2,1)}, bf16[32,6144]{1,0:T(8,128)(2,1)}, u32[]{:S(2)}, u32[]{:S(2)}) collective-permute-start(bf16[32,6144]{1,0:T(8,128)(2,1)} %collective-permute-done.9.refs_3_.refs_11_), channel_id=1, source_target_pairs={{0,1},{1,0},{2,3},{3,2},{4,5},{5,4},{6,7},{7,6},{8,9},{9,8},{10,11... | collective-permute-start | bytes 1179656 | tf_op jit(solution)/shard_map/ppermute | solution.py:23
  57.8 18.5 %collective-permute-start.13 = (bf16[32,6144]{1,0:T(8,128)(2,1)}, bf16[32,6144]{1,0:T(8,128)(2,1)}, u32[]{:S(2)}, u32[]{:S(2)}) collective-permute-start(bf16[32,6144]{1,0:T(8,128)(2,1)} %collective-permute-done.12.refs_5_.refs_13_), channel_id=1, source_target_pairs={{0,3},{1,2},{2,1},{3,0},{4,7},{5,6},{6,5},{7,4},{8,11},{9,10},{10,... | collective-permute-start | bytes 1179656 | tf_op jit(solution)/shard_map/ppermute | solution.py:23
  62.7 19.7 %collective-permute-start.15 = (bf16[2,256,384]{2,1,0:T(8,128)(2,1)}, bf16[2,256,384]{2,1,0:T(8,128)(2,1)}, u32[]{:S(2)}, u32[]{:S(2)}) collective-permute-start(bf16[2,256,384]{2,1,0:T(8,128)(2,1)} %pack.3), channel_id=1, source_target_pairs={{0,128},{8,136},{16,144},{24,152},{32,160},{40,168},{48,176},{56,1... | collective-permute-start | bytes 1179656 | tf_op jit(solution)/shard_map/ppermute | solution.py:33
  67.7 8.6 %copy-start.2 = (bf16[6144,384]{1,0:T(8,128)(2,1)S(1)}, bf16[6144,384]{1,0:T(8,128)(2,1)}, u32[]{:S(2)}) copy-start(bf16[6144,384]{1,0:T(8,128)(2,1)} %w_ref.3) | copy-start | bytes 14155780
  93.5 13.3 %collective-permute-start.18 = (bf16[8,192,768]{2,1,0:T(8,128)(2,1)S(1)}, bf16[8,192,768]{2,1,0:T(8,128)(2,1)S(1)}, u32[]{:S(2)}, u32[]{:S(2)}) collective-permute-start(bf16[8,192,768]{2,1,0:T(8,128)(2,1)S(1)} %get-tuple-element.40.refs_0_), channel_id=1, source_target_pairs={{0,8},{8,0},{16,24},{24,16},{32,40},{40,32},{48,56},{56,48},{64,72... | collective-permute-start | bytes 7077896 | tf_op jit(solution)/shard_map/ppermute | solution.py:33
  110.0 11.8 %collective-permute-start.22 = (bf16[32,6144]{1,0:T(8,128)(2,1)}, bf16[32,6144]{1,0:T(8,128)(2,1)S(1)}, u32[]{:S(2)}, u32[]{:S(2)}) collective-permute-start(bf16[32,6144]{1,0:T(8,128)(2,1)} %get-tuple-element.49), channel_id=1, source_target_pairs={{0,3},{1,2},{2,1},{3,0},{4,7},{5,6},{6,5},{7,4},{8,11},{9,10},{10,... | collective-permute-start | bytes 1179656 | tf_op jit(solution)/shard_map/ppermute | solution.py:23
  111.0 19.2 %collective-permute-start.17 = (bf16[32,6144]{1,0:T(8,128)(2,1)}, bf16[32,6144]{1,0:T(8,128)(2,1)S(1)}, u32[]{:S(2)}, u32[]{:S(2)}) collective-permute-start(bf16[32,6144]{1,0:T(8,128)(2,1)} %get-tuple-element.43), channel_id=1, source_target_pairs={{0,3},{1,2},{2,1},{3,0},{4,7},{5,6},{6,5},{7,4},{8,11},{9,10},{10,... | collective-permute-start | bytes 1179656 | tf_op jit(solution)/shard_map/ppermute | solution.py:23
  112.7 20.4 %collective-permute-start.20 = (bf16[32,6144]{1,0:T(8,128)(2,1)}, bf16[32,6144]{1,0:T(8,128)(2,1)S(1)}, u32[]{:S(2)}, u32[]{:S(2)}) collective-permute-start(bf16[32,6144]{1,0:T(8,128)(2,1)} %get-tuple-element.46), channel_id=1, source_target_pairs={{0,1},{1,0},{2,3},{3,2},{4,5},{5,4},{6,7},{7,6},{8,9},{9,8},{10,11... | collective-permute-start | bytes 1179656 | tf_op jit(solution)/shard_map/ppermute | solution.py:23
  121.8 6.7 %copy-start.24 = (bf16[2,256,384]{2,1,0:T(8,128)(2,1)S(1)}, bf16[2,256,384]{2,1,0:T(8,128)(2,1)}, u32[]{:S(2)}) copy-start(bf16[2,256,384]{2,1,0:T(8,128)(2,1)} %copy-done.23) | copy-start | bytes 1179652
  121.8 12.5 %collective-permute-start.23 = (bf16[32,6144]{1,0:T(8,128)(2,1)S(1)}, bf16[32,6144]{1,0:T(8,128)(2,1)S(1)}, u32[]{:S(2)}, u32[]{:S(2)}) collective-permute-start(bf16[32,6144]{1,0:T(8,128)(2,1)S(1)} %add.131), channel_id=1, source_target_pairs={{0,4},{1,5},{2,6},{3,7},{4,0},{5,1},{6,2},{7,3},{8,12},{9,13},{10,... | collective-permute-start | bytes 1179656 | tf_op jit(solution)/shard_map/ppermute | solution.py:23
  128.5 27.6 %collective-permute-start.32 = (bf16[2,256,384]{2,1,0:T(8,128)(2,1)S(1)}, bf16[2,256,384]{2,1,0:T(8,128)(2,1)S(1)}, u32[]{:S(2)}, u32[]{:S(2)}) collective-permute-start(bf16[2,256,384]{2,1,0:T(8,128)(2,1)S(1)} %copy-done.24), channel_id=1, source_target_pairs={{0,128},{8,136},{16,144},{24,152},{32,160},{40,168},{48,176},{56,1... | collective-permute-start | bytes 1179656 | tf_op jit(solution)/shard_map/ppermute | solution.py:33
  128.6 28.7 %collective-permute-start.16 = (bf16[32,6144]{1,0:T(8,128)(2,1)}, bf16[32,6144]{1,0:T(8,128)(2,1)S(1)}, u32[]{:S(2)}, u32[]{:S(2)}) collective-permute-start(bf16[32,6144]{1,0:T(8,128)(2,1)} %copy-done.33), channel_id=1, source_target_pairs={{0,1},{1,0},{2,3},{3,2},{4,5},{5,4},{6,7},{7,6},{8,9},{9,8},{10,11... | collective-permute-start | bytes 1179656 | tf_op jit(solution)/shard_map/ppermute | solution.py:23
  130.3 11.0 %collective-permute-start.19 = (bf16[32,6144]{1,0:T(8,128)(2,1)S(1)}, bf16[32,6144]{1,0:T(8,128)(2,1)S(1)}, u32[]{:S(2)}, u32[]{:S(2)}) collective-permute-start(bf16[32,6144]{1,0:T(8,128)(2,1)S(1)} %add.129), channel_id=1, source_target_pairs={{0,4},{1,5},{2,6},{3,7},{4,0},{5,1},{6,2},{7,3},{8,12},{9,13},{10,... | collective-permute-start | bytes 1179656 | tf_op jit(solution)/shard_map/ppermute | solution.py:23
  133.2 10.5 %collective-permute-start.21 = (bf16[32,6144]{1,0:T(8,128)(2,1)S(1)}, bf16[32,6144]{1,0:T(8,128)(2,1)S(1)}, u32[]{:S(2)}, u32[]{:S(2)}) collective-permute-start(bf16[32,6144]{1,0:T(8,128)(2,1)S(1)} %add.130), channel_id=1, source_target_pairs={{0,3},{1,2},{2,1},{3,0},{4,7},{5,6},{6,5},{7,4},{8,11},{9,10},{10,... | collective-permute-start | bytes 1179656 | tf_op jit(solution)/shard_map/ppermute | solution.py:23
  134.4 11.4 %collective-permute-start.24 = (bf16[32,6144]{1,0:T(8,128)(2,1)S(1)}, bf16[32,6144]{1,0:T(8,128)(2,1)S(1)}, u32[]{:S(2)}, u32[]{:S(2)}) collective-permute-start(bf16[32,6144]{1,0:T(8,128)(2,1)S(1)} %add.99), channel_id=1, source_target_pairs={{0,1},{1,0},{2,3},{3,2},{4,5},{5,4},{6,7},{7,6},{8,9},{9,8},{10,11... | collective-permute-start | bytes 1179656 | tf_op jit(solution)/shard_map/ppermute | solution.py:23
  134.6 6.7 %copy-start.32 = (bf16[32,6144]{1,0:T(8,128)(2,1)S(1)}, bf16[32,6144]{1,0:T(8,128)(2,1)}, u32[]{:S(2)}) copy-start(bf16[32,6144]{1,0:T(8,128)(2,1)} %copy-done.31) | copy-start | bytes 1179652
  134.6 9.1 %copy-start.35 = (bf16[32,6144]{1,0:T(8,128)(2,1)S(1)}, bf16[32,6144]{1,0:T(8,128)(2,1)}, u32[]{:S(2)}) copy-start(bf16[32,6144]{1,0:T(8,128)(2,1)} %copy-done.34) | copy-start | bytes 1179652
  135.4 19.6 %copy-start.22 = (bf16[32,6144]{1,0:T(8,128)(2,1)S(1)}, bf16[32,6144]{1,0:T(8,128)(2,1)}, u32[]{:S(2)}) copy-start(bf16[32,6144]{1,0:T(8,128)(2,1)} %copy-done.21) | copy-start | bytes 1179652
  141.3 19.0 %collective-permute-start.26 = (bf16[32,6144]{1,0:T(8,128)(2,1)S(1)}, bf16[32,6144]{1,0:T(8,128)(2,1)S(1)}, u32[]{:S(2)}, u32[]{:S(2)}) collective-permute-start(bf16[32,6144]{1,0:T(8,128)(2,1)S(1)} %copy-done.32), channel_id=1, source_target_pairs={{0,3},{1,2},{2,1},{3,0},{4,7},{5,6},{6,5},{7,4},{8,11},{9,10},{10,... | collective-permute-start | bytes 1179656 | tf_op jit(solution)/shard_map/ppermute | solution.py:23
  143.7 11.3 %collective-permute-start.28 = (bf16[32,6144]{1,0:T(8,128)(2,1)S(1)}, bf16[32,6144]{1,0:T(8,128)(2,1)S(1)}, u32[]{:S(2)}, u32[]{:S(2)}) collective-permute-start(bf16[32,6144]{1,0:T(8,128)(2,1)S(1)} %copy-done.35), channel_id=1, source_target_pairs={{0,1},{1,0},{2,3},{3,2},{4,5},{5,4},{6,7},{7,6},{8,9},{9,8},{10,11... | collective-permute-start | bytes 1179656 | tf_op jit(solution)/shard_map/ppermute | solution.py:23
  146.0 33.1 %collective-permute-start.31 = (bf16[32,6144]{1,0:T(8,128)(2,1)S(1)}, bf16[32,6144]{1,0:T(8,128)(2,1)S(1)}, u32[]{:S(2)}, u32[]{:S(2)}) collective-permute-start(bf16[32,6144]{1,0:T(8,128)(2,1)S(1)} %add_convert_fusion.refs_0_), channel_id=1, source_target_pairs={{0,128},{8,136},{16,144},{24,152},{32,160},{40,168},{48,176},{56,1... | collective-permute-start | bytes 1179656 | tf_op jit(solution)/shard_map/ppermute | solution.py:33
  155.1 9.4 %collective-permute-start.29 = (bf16[32,6144]{1,0:T(8,128)(2,1)S(1)}, bf16[32,6144]{1,0:T(8,128)(2,1)S(1)}, u32[]{:S(2)}, u32[]{:S(2)}) collective-permute-start(bf16[32,6144]{1,0:T(8,128)(2,1)S(1)} %add.134), channel_id=1, source_target_pairs={{0,4},{1,5},{2,6},{3,7},{4,0},{5,1},{6,2},{7,3},{8,12},{9,13},{10,... | collective-permute-start | bytes 1179656 | tf_op jit(solution)/shard_map/ppermute | solution.py:23
  157.3 7.2 %copy-start.16 = (bf16[32,6144]{1,0:T(8,128)(2,1)S(1)}, bf16[32,6144]{1,0:T(8,128)(2,1)}, u32[]{:S(2)}) copy-start(bf16[32,6144]{1,0:T(8,128)(2,1)} %copy-done.15) | copy-start | bytes 1179652
  157.4 22.9 %collective-permute-start.25 = (bf16[32,6144]{1,0:T(8,128)(2,1)S(1)}, bf16[32,6144]{1,0:T(8,128)(2,1)S(1)}, u32[]{:S(2)}, u32[]{:S(2)}) collective-permute-start(bf16[32,6144]{1,0:T(8,128)(2,1)S(1)} %add.132), channel_id=1, source_target_pairs={{0,4},{1,5},{2,6},{3,7},{4,0},{5,1},{6,2},{7,3},{8,12},{9,13},{10,... | collective-permute-start | bytes 1179656 | tf_op jit(solution)/shard_map/ppermute | solution.py:23
  160.3 19.9 %copy-start.12 = (bf16[32,6144]{1,0:T(8,128)(2,1)S(1)}, bf16[32,6144]{1,0:T(8,128)(2,1)}, u32[]{:S(2)}) copy-start(bf16[32,6144]{1,0:T(8,128)(2,1)} %copy-done.11) | copy-start | bytes 1179652
  160.4 19.9 %collective-permute-start.27 = (bf16[32,6144]{1,0:T(8,128)(2,1)S(1)}, bf16[32,6144]{1,0:T(8,128)(2,1)S(1)}, u32[]{:S(2)}, u32[]{:S(2)}) collective-permute-start(bf16[32,6144]{1,0:T(8,128)(2,1)S(1)} %add.133), channel_id=1, source_target_pairs={{0,1},{1,0},{2,3},{3,2},{4,5},{5,4},{6,7},{7,6},{8,9},{9,8},{10,11... | collective-permute-start | bytes 1179656 | tf_op jit(solution)/shard_map/ppermute | solution.py:23
  164.6 15.7 %collective-permute-start.30 = (bf16[32,6144]{1,0:T(8,128)(2,1)S(1)}, bf16[32,6144]{1,0:T(8,128)(2,1)S(1)}, u32[]{:S(2)}, u32[]{:S(2)}) collective-permute-start(bf16[32,6144]{1,0:T(8,128)(2,1)S(1)} %add.101), channel_id=1, source_target_pairs={{0,3},{1,2},{2,1},{3,0},{4,7},{5,6},{6,5},{7,4},{8,11},{9,10},{10,... | collective-permute-start | bytes 1179656 | tf_op jit(solution)/shard_map/ppermute | solution.py:23
  180.2 4.1 %collective-permute-start.33 = (bf16[192,384]{1,0:T(8,128)(2,1)S(1)}, bf16[192,384]{1,0:T(8,128)(2,1)S(1)}, u32[]{:S(2)}, u32[]{:S(2)}) collective-permute-start(bf16[192,384]{1,0:T(8,128)(2,1)S(1)} %dynamic-slice_bitcast_fusion.1), channel_id=1, source_target_pairs={{0,16},{8,24},{16,0},{24,8},{32,48},{40,56},{48,32},{56,40},{64,80... | collective-permute-start | bytes 442376 | tf_op jit(solution)/shard_map/ppermute | solution.py:33
  184.4 4.6 %collective-permute-start.34 = (f32[192,192]{0,1:T(8,128)S(1)}, f32[192,192]{0,1:T(8,128)S(1)}, u32[]{:S(2)}, u32[]{:S(2)}) collective-permute-start(f32[192,192]{0,1:T(8,128)S(1)} %dynamic-slice_bitcast_fusion), channel_id=1, source_target_pairs={{0,8},{8,0},{16,24},{24,16},{32,40},{40,32},{48,56},{56,48},{64,72... | collective-permute-start | bytes 442376 | tf_op jit(solution)/shard_map/ppermute | solution.py:33
  (25 other events, 65.0 us)
Sparse Core Ops, SparseCore 0:
  110.1 60.2 reduce-scatter.1

commit v4 on v3

--- a/solution.py
+++ b/solution.py
@@ -362,7 +362,7 @@
                late(terms_a[4], arrived_a[2]))
     next_a = scatter_next(terms_a, first_a, 3)
     last_a = [terms_a[0], swap(first_a[2], 4), swap(first_a[1], 1), swap(next_a, 3)]
-    grad_a = sum_last(last_a, [z_sum])
+    grad_a = sum_last(last_a, [z_sum, back_rows])
 
     def by_slot(of_a, of_b):
         first = slot_a == 0

time: 198 us -> 198 us (level)
  transfers between devices with their start and end apart: 36 -> 36, of which waited for: 15 -> 14; matrix products, arithmetic and copies ran while one was open for 5% -> 6% of each run, Pallas kernels for 8% -> 8%
where the time goes in v4:
time: 198 us; the launch traced here: 197 us
  waiting for transfers between devices  61.9 us (31%)
  starting transfers between devices  61.2 us (31%)
  Pallas kernels  29.1 us (15%)
  between operations  22.6 us (11%)
  local copies, waits for them, and re-layouts  14 us (7%)
  other arithmetic  8.52 us (4%)
    ppermute x28, waiting for transfers between devices, swap(): return lax.ppermute(x, 'tensor', [(i, i ^ d) for i in range(N_TENSOR)])  46.1 us
    ppermute x28, starting transfers between devices, swap(): return lax.ppermute(x, 'tensor', [(i, i ^ d) for i in range(N_TENSOR)])  35 us
    ppermute x7, starting transfers between devices, dp_perm(): return lax.ppermute(x, 'dp', pairs)  26.1 us
    ppermute x7, waiting for transfers between devices, dp_perm(): return lax.ppermute(x, 'dp', pairs)  15.8 us
    unnamed x75, local copies, waits for them, and re-layouts  10.9 us
    pallas_call x2, Pallas kernels, attend(): pl.pallas_call(functools.partial(attend_kernel, arrived), grid_spec=pltpu...  8.56 us
    pallas_call x2, Pallas kernels, project_values(): pl.pallas_call(value_kernel, in_specs=[VM] * 9 + [ANY] * len(after), out_...  6.77 us
    pallas_call x1, Pallas kernels, weight_terms(): pl.pallas_call(weight_kernel, in_specs=[pl.BlockSpec(memory_space=pltpu.S...  4.76 us
  transfers between devices with their start and end apart: 36, of which 14 were waited for; matrix products, arithmetic and copies ran while one was open for 6% of the time, Pallas kernels for 8%

profile of v4, /device:TPU:1, one launch (start us, length us, event | category | flops | bytes accessed | tf_op | source)
XLA Modules:
  0.0 197.2 jit_solution(16064939148728805549)
XLA Ops:
  7.2 1.3 copy-done.5
  8.6 7.8 %collective-permute-start.7 = (bf16[32,6144]{1,0:T(8,128)(2,1)S(1)}, bf16[32,6144]{1,0:T(8,128)(2,1)}, u32[]{:S(2)}, u32[]{:S(2)}) collective-permute-start(bf16[32,6144]{1,0:T(8,128)(2,1)S(1)} %bitcast.40), channel_id=1, source_target_pairs={{0,128},{8,136},{16,144},{24,152},{32,160},{40,168},{48,176},{56,1... | collective-permute-start | bytes 1179656 | tf_op jit(solution)/shard_map/ppermute | solution.py:33
  21.8 2.8 %collective-permute-start.3 = (bf16[32,6144]{1,0:T(8,128)(2,1)S(1)}, bf16[32,6144]{1,0:T(8,128)(2,1)S(1)}, u32[]{:S(2)}, u32[]{:S(2)}) collective-permute-start(bf16[32,6144]{1,0:T(8,128)(2,1)S(1)} %select_bitcast_fusion.3.refs_0_), channel_id=1, source_target_pairs={{0,4},{1,5},{2,6},{3,7},{4,0},{5,1},{6,2},{7,3},{8,12},{9,13},{10,... | collective-permute-start | bytes 1179656 | tf_op jit(solution)/shard_map/ppermute | solution.py:23
  24.6 2.7 %collective-permute-start.2 = (bf16[32,6144]{1,0:T(8,128)(2,1)S(1)}, bf16[32,6144]{1,0:T(8,128)(2,1)}, u32[]{:S(2)}, u32[]{:S(2)}) collective-permute-start(bf16[32,6144]{1,0:T(8,128)(2,1)S(1)} %select_bitcast_fusion.3.refs_0_), channel_id=1, source_target_pairs={{0,3},{1,2},{2,1},{3,0},{4,7},{5,6},{6,5},{7,4},{8,11},{9,10},{10,... | collective-permute-start | bytes 1179656 | tf_op jit(solution)/shard_map/ppermute | solution.py:23
  27.4 1.7 bitcast_select_fusion.refs_0_.refs_8_
  29.1 1.5 collective-permute-start.8
  30.6 1.6 collective-permute-start.11
  32.2 3.2 %collective-permute-done.2.refs_3_ = bf16[32,6144]{1,0:T(8,128)(2,1)} collective-permute-done((bf16[32,6144]{1,0:T(8,128)(2,1)S(1)}, bf16[32,6144]{1,0:T(8,128)(2,1)}, u32[]{:S(2)}, u32[]{:S(2)}) %collective-permute-start.2) | collective-permute-done | bytes 393248 | tf_op jit(solution)/shard_map/ppermute | solution.py:23
  35.7 2.6 %collective-permute-start.9 = (bf16[32,6144]{1,0:T(8,128)(2,1)S(1)}, bf16[32,6144]{1,0:T(8,128)(2,1)}, u32[]{:S(2)}, u32[]{:S(2)}) collective-permute-start(bf16[32,6144]{1,0:T(8,128)(2,1)S(1)} %bitcast_select_fusion.refs_0_.refs_8_), channel_id=1, source_target_pairs={{0,3},{1,2},{2,1},{3,0},{4,7},{5,6},{6,5},{7,4},{8,11},{9,10},{10,... | collective-permute-start | bytes 1179656 | tf_op jit(solution)/shard_map/ppermute | solution.py:23
  38.4 6.6 %collective-permute-done.8.refs_1_.refs_9_ = bf16[32,6144]{1,0:T(8,128)(2,1)S(1)} collective-permute-done((bf16[32,6144]{1,0:T(8,128)(2,1)S(1)}, bf16[32,6144]{1,0:T(8,128)(2,1)S(1)}, u32[]{:S(2)}, u32[]{:S(2)}) %collective-permute-start.8) | collective-permute-done | bytes 393248 | tf_op jit(solution)/shard_map/ppermute | solution.py:23
  45.4 3.9 %collective-permute-done.5.refs_7_ = bf16[32,6144]{1,0:T(8,128)(2,1)} collective-permute-done((bf16[32,6144]{1,0:T(8,128)(2,1)}, bf16[32,6144]{1,0:T(8,128)(2,1)}, u32[]{:S(2)}, u32[]{:S(2)}) %collective-permute-start.5) | collective-permute-done | bytes 393248 | tf_op jit(solution)/shard_map/ppermute | solution.py:23
  49.2 2.1 %collective-permute-start.6 = (bf16[32,6144]{1,0:T(8,128)(2,1)}, bf16[32,6144]{1,0:T(8,128)(2,1)}, u32[]{:S(2)}, u32[]{:S(2)}) collective-permute-start(bf16[32,6144]{1,0:T(8,128)(2,1)} %collective-permute-done.5.refs_7_), channel_id=1, source_target_pairs={{0,1},{1,0},{2,3},{3,2},{4,5},{5,4},{6,7},{7,6},{8,9},{9,8},{10,11... | collective-permute-start | bytes 1179656 | tf_op jit(solution)/shard_map/ppermute | solution.py:23
  51.3 2.3 %collective-permute-start.14 = (bf16[32,6144]{1,0:T(8,128)(2,1)}, bf16[32,6144]{1,0:T(8,128)(2,1)}, u32[]{:S(2)}, u32[]{:S(2)}) collective-permute-start(bf16[32,6144]{1,0:T(8,128)(2,1)} %collective-permute-done.11.refs_4_.refs_12_), channel_id=1, source_target_pairs={{0,3},{1,2},{2,1},{3,0},{4,7},{5,6},{6,5},{7,4},{8,11},{9,10},{10,... | collective-permute-start | bytes 1179656 | tf_op jit(solution)/shard_map/ppermute | solution.py:23
  53.6 4.1 %collective-permute-done.12.refs_5_.refs_13_ = bf16[32,6144]{1,0:T(8,128)(2,1)} collective-permute-done((bf16[32,6144]{1,0:T(8,128)(2,1)S(1)}, bf16[32,6144]{1,0:T(8,128)(2,1)}, u32[]{:S(2)}, u32[]{:S(2)}) %collective-permute-start.12) | collective-permute-done | bytes 393248 | tf_op jit(solution)/shard_map/ppermute | solution.py:23
  57.8 3.4 %collective-permute-start.13 = (bf16[32,6144]{1,0:T(8,128)(2,1)}, bf16[32,6144]{1,0:T(8,128)(2,1)}, u32[]{:S(2)}, u32[]{:S(2)}) collective-permute-start(bf16[32,6144]{1,0:T(8,128)(2,1)} %collective-permute-done.12.refs_5_.refs_13_), channel_id=1, source_target_pairs={{0,3},{1,2},{2,1},{3,0},{4,7},{5,6},{6,5},{7,4},{8,11},{9,10},{10,... | collective-permute-start | bytes 1179656 | tf_op jit(solution)/shard_map/ppermute | solution.py:23
  64.3 2.3 %copy-done.1 = bf16[6144,384]{1,0:T(8,128)(2,1)S(1)} copy-done((bf16[6144,384]{1,0:T(8,128)(2,1)S(1)}, bf16[6144,384]{1,0:T(8,128)(2,1)}, u32[]{:S(2)}) %copy-start.1) | copy-done | bytes 4718616
  66.7 1.0 copy-done.8
  67.7 3.3 %project_values.2.refs_2_ = bf16[256,384]{1,0:T(8,128)(2,1)S(1)} custom-call(bf16[32,6144]{1,0:T(8,128)(2,1)S(1)} %select_bitcast_fusion.3.refs_0_, bf16[32,6144]{1,0:T(8,128)(2,1)} %collective-permute-done.refs_1_, bf16[32,6144]{1,0:T(8,128)(2,1)S(1)} %collective-permute-done.1.refs_2_, bf16[32,6144]{1,0:T(8,128)(2,1)} %collective-permute-done.2.refs_3_, ...), custom_call_target="tpu_custom_call" | custom-call | flops 1 | bytes 1 | tf_op jit(solution)/shard_map/project_values/pallas_call | solution.py:154
  71.0 3.8 %attend.2 = (bf16[256,384]{1,0:T(8,128)(2,1)S(1)}, bf16[256,384]{1,0:T(8,128)(2,1)S(1)}, bf16[384,256]{1,0:T(8,128)(2,1)S(1)}, bf16[2,256,384]{2,1,0:T(8,128)(2,1)S(1)}) custom-call(s32[4]{0:T(128)S(1)} %pad_add_fusion.me_ref, bf16[3,256,384]{2,1,0:T(8,128)(2,1)S(1)} %copy-done.3, bf16[3,256,384]{2,1,0:T(8,128)(2,1)S(1)} %copy-done.4, ...), custom_call_target="tpu_custom_call" | custom-call | flops 1 | bytes 1 | tf_op jit(solution)/shard_map/attend/pallas_call | solution.py:208
  76.3 3.4 %project_values.3.refs_0_.refs_2_ = bf16[256,384]{1,0:T(8,128)(2,1)S(1)} custom-call(bf16[32,6144]{1,0:T(8,128)(2,1)S(1)} %bitcast_select_fusion.refs_0_.refs_8_, bf16[32,6144]{1,0:T(8,128)(2,1)S(1)} %collective-permute-done.8.refs_1_.refs_9_, bf16[32,6144]{1,0:T(8,128)(2,1)} %collective-permute-done.10.refs_2_.refs_10_, ...), custom_call_target="tpu_custom_call" | custom-call | flops 1 | bytes 1 | tf_op jit(solution)/shard_map/project_values/pallas_call | solution.py:154
  79.7 1.8 row_terms.2
  82.4 4.8 %attend.3 = (bf16[256,384]{1,0:T(8,128)(2,1)S(1)}, bf16[256,384]{1,0:T(8,128)(2,1)S(1)}, bf16[384,256]{1,0:T(8,128)(2,1)S(1)}, bf16[2,256,384]{2,1,0:T(8,128)(2,1)S(1)}) custom-call(s32[4]{0:T(128)S(1)} %pad_add_fusion.1.me_ref, bf16[3,256,384]{2,1,0:T(8,128)(2,1)S(1)} %copy-done.3, bf16[3,256,384]{2,1,0:T(8,128)(2,1)S(1)} %copy-done.4, ...), custom_call_target="tpu_custom_call" | custom-call | flops 1 | bytes 1 | tf_op jit(solution)/shard_map/attend/pallas_call | solution.py:208
  88.7 4.8 %weight_terms.1 = (bf16[8,192,768]{2,1,0:T(8,128)(2,1)S(1)}, bf16[8,192,768]{2,1,0:T(8,128)(2,1)S(1)}) custom-call(s32[1]{0:T(128)} %bitcast.14.core_ref, bf16[32,6144]{1,0:T(8,128)(2,1)S(1)} %select_bitcast_fusion.3.refs_0_, bf16[32,6144]{1,0:T(8,128)(2,1)} %collective-permute-done.refs_1_, bf16[32,6144]{1,0:T(8,128)(2,1)S(1)} %collective-permute-done.1.refs_2_, ...), custom_call_target="tpu_custom_call" | custom-call | flops 1 | bytes 1 | tf_op jit(solution)/shard_map/weight_terms/pallas_call | solution.py:274
  93.5 9.2 %collective-permute-start.18 = (bf16[8,192,768]{2,1,0:T(8,128)(2,1)S(1)}, bf16[8,192,768]{2,1,0:T(8,128)(2,1)S(1)}, u32[]{:S(2)}, u32[]{:S(2)}) collective-permute-start(bf16[8,192,768]{2,1,0:T(8,128)(2,1)S(1)} %get-tuple-element.40.refs_0_), channel_id=1, source_target_pairs={{0,8},{8,0},{16,24},{24,16},{32,40},{40,32},{48,56},{56,48},{64,72... | collective-permute-start | bytes 7077896 | tf_op jit(solution)/shard_map/ppermute | solution.py:33
  102.7 2.8 %row_terms.3 = (bf16[32,6144]{1,0:T(8,128)(2,1)S(1)}, bf16[32,6144]{1,0:T(8,128)(2,1)S(1)}, bf16[32,6144]{1,0:T(8,128)(2,1)}, bf16[32,6144]{1,0:T(8,128)(2,1)S(1...) custom-call(bf16[256,384]{1,0:T(8,128)(2,1)S(1)} %get-tuple-element., ...), custom_call_target="tpu_custom_call" | custom-call | flops 1 | bytes 1 | tf_op jit(solution)/shard_map/row_terms/pallas_call | solution.py:247
  105.5 1.4 collective-permute-done.18.b_ref
  106.8 3.1 %add.128.refs_0_ = bf16[8,192,768]{2,1,0:T(8,128)(2,1)} custom-call(bf16[8,192,768]{2,1,0:T(8,128)(2,1)S(1)} %get-tuple-element.44.a_ref, bf16[8,192,768]{2,1,0:T(8,128)(2,1)S(1)} %collective-permute-done.18.b_ref, bf16[32,6144]{1,0:T(8,128)(2,1)S(1)} %get-tuple-element.41.refs_0_), custom_call_target="tpu_custom_call" | custom-call | flops 1 | bytes 1 | tf_op jit(solution)/shard_map/add/pallas_call | solution.py:112
  110.0 1.1 collective-permute-start.22
  111.0 1.7 collective-permute-start.17
  112.7 9.1 %collective-permute-done.22.b_ref = bf16[32,6144]{1,0:T(8,128)(2,1)S(1)} collective-permute-done((bf16[32,6144]{1,0:T(8,128)(2,1)}, bf16[32,6144]{1,0:T(8,128)(2,1)S(1)}, u32[]{:S(2)}, u32[]{:S(2)}) %collective-permute-start.22) | collective-permute-done | bytes 393248 | tf_op jit(solution)/shard_map/ppermute | solution.py:23
  121.8 2.8 %collective-permute-start.23 = (bf16[32,6144]{1,0:T(8,128)(2,1)S(1)}, bf16[32,6144]{1,0:T(8,128)(2,1)S(1)}, u32[]{:S(2)}, u32[]{:S(2)}) collective-permute-start(bf16[32,6144]{1,0:T(8,128)(2,1)S(1)} %add.131), channel_id=1, source_target_pairs={{0,4},{1,5},{2,6},{3,7},{4,0},{5,1},{6,2},{7,3},{8,12},{9,13},{10,... | collective-permute-start | bytes 1179656 | tf_op jit(solution)/shard_map/ppermute | solution.py:23
  128.7 1.5 collective-permute-done.17.b_ref
  130.3 2.8 %collective-permute-start.19 = (bf16[32,6144]{1,0:T(8,128)(2,1)S(1)}, bf16[32,6144]{1,0:T(8,128)(2,1)S(1)}, u32[]{:S(2)}, u32[]{:S(2)}) collective-permute-start(bf16[32,6144]{1,0:T(8,128)(2,1)S(1)} %add.129), channel_id=1, source_target_pairs={{0,4},{1,5},{2,6},{3,7},{4,0},{5,1},{6,2},{7,3},{8,12},{9,13},{10,... | collective-permute-start | bytes 1179656 | tf_op jit(solution)/shard_map/ppermute | solution.py:23
  133.2 1.2 collective-permute-start.21
  135.4 5.8 %collective-permute-done.19 = bf16[32,6144]{1,0:T(8,128)(2,1)S(1)} collective-permute-done((bf16[32,6144]{1,0:T(8,128)(2,1)S(1)}, bf16[32,6144]{1,0:T(8,128)(2,1)S(1)}, u32[]{:S(2)}, u32[]{:S(2)}) %collective-permute-start.19) | collective-permute-done | bytes 393248 | tf_op jit(solution)/shard_map/ppermute | solution.py:23
  142.2 1.5 collective-permute-done.21
  143.7 2.1 %collective-permute-done.24 = bf16[32,6144]{1,0:T(8,128)(2,1)S(1)} collective-permute-done((bf16[32,6144]{1,0:T(8,128)(2,1)S(1)}, bf16[32,6144]{1,0:T(8,128)(2,1)S(1)}, u32[]{:S(2)}, u32[]{:S(2)}) %collective-permute-start.24) | collective-permute-done | bytes 393248 | tf_op jit(solution)/shard_map/ppermute | solution.py:23
  146.0 5.0 %collective-permute-start.31 = (bf16[32,6144]{1,0:T(8,128)(2,1)S(1)}, bf16[32,6144]{1,0:T(8,128)(2,1)S(1)}, u32[]{:S(2)}, u32[]{:S(2)}) collective-permute-start(bf16[32,6144]{1,0:T(8,128)(2,1)S(1)} %add_convert_fusion.refs_0_), channel_id=1, source_target_pairs={{0,128},{8,136},{16,144},{24,152},{32,160},{40,168},{48,176},{56,1... | collective-permute-start | bytes 1179656 | tf_op jit(solution)/shard_map/ppermute | solution.py:33
  151.0 4.0 %collective-permute-done.28.b_ref = bf16[32,6144]{1,0:T(8,128)(2,1)S(1)} collective-permute-done((bf16[32,6144]{1,0:T(8,128)(2,1)S(1)}, bf16[32,6144]{1,0:T(8,128)(2,1)S(1)}, u32[]{:S(2)}, u32[]{:S(2)}) %collective-permute-start.28) | collective-permute-done | bytes 393248 | tf_op jit(solution)/shard_map/ppermute | solution.py:23
  156.1 1.2 pad_maximum_fusion.1
  157.4 2.9 %collective-permute-start.25 = (bf16[32,6144]{1,0:T(8,128)(2,1)S(1)}, bf16[32,6144]{1,0:T(8,128)(2,1)S(1)}, u32[]{:S(2)}, u32[]{:S(2)}) collective-permute-start(bf16[32,6144]{1,0:T(8,128)(2,1)S(1)} %add.132), channel_id=1, source_target_pairs={{0,4},{1,5},{2,6},{3,7},{4,0},{5,1},{6,2},{7,3},{8,12},{9,13},{10,... | collective-permute-start | bytes 1179656 | tf_op jit(solution)/shard_map/ppermute | solution.py:23
  160.5 4.0 %collective-permute-done.29 = bf16[32,6144]{1,0:T(8,128)(2,1)S(1)} collective-permute-done((bf16[32,6144]{1,0:T(8,128)(2,1)S(1)}, bf16[32,6144]{1,0:T(8,128)(2,1)S(1)}, u32[]{:S(2)}, u32[]{:S(2)}) %collective-permute-start.29) | collective-permute-done | bytes 393248 | tf_op jit(solution)/shard_map/ppermute | solution.py:23
  165.4 1.4 collective-permute-start.30
  166.7 12.5 %collective-permute-done.31.refs_1_ = bf16[32,6144]{1,0:T(8,128)(2,1)S(1)} collective-permute-done((bf16[32,6144]{1,0:T(8,128)(2,1)S(1)}, bf16[32,6144]{1,0:T(8,128)(2,1)S(1)}, u32[]{:S(2)}, u32[]{:S(2)}) %collective-permute-start.31) | collective-permute-done | bytes 393248 | tf_op jit(solution)/shard_map/ppermute | solution.py:33
  180.6 1.0 copy-done.13
  182.5 1.9 collective-permute-done.33
  184.5 3.7 %collective-permute-start.34 = (f32[192,192]{0,1:T(8,128)S(1)}, f32[192,192]{0,1:T(8,128)S(1)}, u32[]{:S(2)}, u32[]{:S(2)}) collective-permute-start(f32[192,192]{0,1:T(8,128)S(1)} %dynamic-slice_bitcast_fusion), channel_id=1, source_target_pairs={{0,8},{8,0},{16,24},{24,16},{32,40},{40,32},{48,56},{56,48},{64,72... | collective-permute-start | bytes 442376 | tf_op jit(solution)/shard_map/ppermute | solution.py:33
  188.2 1.1 pad_maximum_fusion
  (145 shorter events, 16.9 us)
Async XLA Ops:
  7.2 9.2 %copy-start = (s32[32,3]{0,1:T(4,128)S(1)}, s32[32,3]{0,1:T(4,128)}, u32[]{:S(2)}) copy-start(s32[32,3]{0,1:T(4,128)} %param.12) | copy-start | bytes 1156
  7.2 172.1 %reduce-scatter.2.cloned.1.call-start = ((), (), s32[]{:S(2)}) async-start(), calls=%async_computation.1 | async-start | bytes 2654208 | tf_op jit(solution)/shard_map/reduce_scatter | solution.py:287
  8.5 12.6 %copy-start.6 = (bf16[3,32,6144]{2,1,0:T(8,128)(2,1)S(1)}, bf16[3,32,6144]{2,1,0:T(8,128)(2,1)}, u32[]{:S(2)}) copy-start(bf16[3,32,6144]{2,1,0:T(8,128)(2,1)} %refs_0_.5) | copy-start | bytes 3538948
  8.5 52.6 %copy-start.3 = (bf16[3,256,384]{2,1,0:T(8,128)(2,1)S(1)}, bf16[3,256,384]{2,1,0:T(8,128)(2,1)}, u32[]{:S(2)}) copy-start(bf16[3,256,384]{2,1,0:T(8,128)(2,1)} %refs_0_.7) | copy-start | bytes 1769476
  8.5 52.6 %copy-start.4 = (bf16[3,256,384]{2,1,0:T(8,128)(2,1)S(1)}, bf16[3,256,384]{2,1,0:T(8,128)(2,1)}, u32[]{:S(2)}) copy-start(bf16[3,256,384]{2,1,0:T(8,128)(2,1)} %refs_1_.5) | copy-start | bytes 1769476
  8.6 18.8 %collective-permute-start.7 = (bf16[32,6144]{1,0:T(8,128)(2,1)S(1)}, bf16[32,6144]{1,0:T(8,128)(2,1)}, u32[]{:S(2)}, u32[]{:S(2)}) collective-permute-start(bf16[32,6144]{1,0:T(8,128)(2,1)S(1)} %bitcast.40), channel_id=1, source_target_pairs={{0,128},{8,136},{16,144},{24,152},{32,160},{40,168},{48,176},{56,1... | collective-permute-start | bytes 1179656 | tf_op jit(solution)/shard_map/ppermute | solution.py:33
  21.8 13.9 %collective-permute-start.3 = (bf16[32,6144]{1,0:T(8,128)(2,1)S(1)}, bf16[32,6144]{1,0:T(8,128)(2,1)S(1)}, u32[]{:S(2)}, u32[]{:S(2)}) collective-permute-start(bf16[32,6144]{1,0:T(8,128)(2,1)S(1)} %select_bitcast_fusion.3.refs_0_), channel_id=1, source_target_pairs={{0,4},{1,5},{2,6},{3,7},{4,0},{5,1},{6,2},{7,3},{8,12},{9,13},{10,... | collective-permute-start | bytes 1179656 | tf_op jit(solution)/shard_map/ppermute | solution.py:23
  24.6 10.8 %collective-permute-start.2 = (bf16[32,6144]{1,0:T(8,128)(2,1)S(1)}, bf16[32,6144]{1,0:T(8,128)(2,1)}, u32[]{:S(2)}, u32[]{:S(2)}) collective-permute-start(bf16[32,6144]{1,0:T(8,128)(2,1)S(1)} %select_bitcast_fusion.3.refs_0_), channel_id=1, source_target_pairs={{0,3},{1,2},{2,1},{3,0},{4,7},{5,6},{6,5},{7,4},{8,11},{9,10},{10,... | collective-permute-start | bytes 1179656 | tf_op jit(solution)/shard_map/ppermute | solution.py:23
  27.4 10.9 %collective-permute-start = (bf16[32,6144]{1,0:T(8,128)(2,1)S(1)}, bf16[32,6144]{1,0:T(8,128)(2,1)}, u32[]{:S(2)}, u32[]{:S(2)}) collective-permute-start(bf16[32,6144]{1,0:T(8,128)(2,1)S(1)} %select_bitcast_fusion.3.refs_0_), channel_id=1, source_target_pairs={{0,1},{1,0},{2,3},{3,2},{4,5},{5,4},{6,7},{7,6},{8,9},{9,8},{10,11... | collective-permute-start | bytes 1179656 | tf_op jit(solution)/shard_map/ppermute | solution.py:23
  29.1 34.9 %copy-start.36 = (s32[2,256]{1,0:T(2,128)S(1)}, s32[2,256]{1,0:T(2,128)}, u32[]{:S(2)}) copy-start(s32[2,256]{1,0:T(2,128)} %param.13) | copy-start | bytes 6148
  29.1 15.9 %collective-permute-start.8 = (bf16[32,6144]{1,0:T(8,128)(2,1)S(1)}, bf16[32,6144]{1,0:T(8,128)(2,1)S(1)}, u32[]{:S(2)}, u32[]{:S(2)}) collective-permute-start(bf16[32,6144]{1,0:T(8,128)(2,1)S(1)} %bitcast_select_fusion.refs_0_.refs_8_), channel_id=1, source_target_pairs={{0,1},{1,0},{2,3},{3,2},{4,5},{5,4},{6,7},{7,6},{8,9},{9,8},{10,11... | collective-permute-start | bytes 1179656 | tf_op jit(solution)/shard_map/ppermute | solution.py:23
  30.6 14.6 %collective-permute-start.11 = (bf16[32,6144]{1,0:T(8,128)(2,1)S(1)}, bf16[32,6144]{1,0:T(8,128)(2,1)}, u32[]{:S(2)}, u32[]{:S(2)}) collective-permute-start(bf16[32,6144]{1,0:T(8,128)(2,1)S(1)} %bitcast_select_fusion.refs_0_.refs_8_), channel_id=1, source_target_pairs={{0,4},{1,5},{2,6},{3,7},{4,0},{5,1},{6,2},{7,3},{8,12},{9,13},{10,... | collective-permute-start | bytes 1179656 | tf_op jit(solution)/shard_map/ppermute | solution.py:23
  35.4 13.8 %collective-permute-start.5 = (bf16[32,6144]{1,0:T(8,128)(2,1)}, bf16[32,6144]{1,0:T(8,128)(2,1)}, u32[]{:S(2)}, u32[]{:S(2)}) collective-permute-start(bf16[32,6144]{1,0:T(8,128)(2,1)} %collective-permute-done.2.refs_3_), channel_id=1, source_target_pairs={{0,4},{1,5},{2,6},{3,7},{4,0},{5,1},{6,2},{7,3},{8,12},{9,13},{10,... | collective-permute-start | bytes 1179656 | tf_op jit(solution)/shard_map/ppermute | solution.py:23
  35.7 15.6 %collective-permute-start.9 = (bf16[32,6144]{1,0:T(8,128)(2,1)S(1)}, bf16[32,6144]{1,0:T(8,128)(2,1)}, u32[]{:S(2)}, u32[]{:S(2)}) collective-permute-start(bf16[32,6144]{1,0:T(8,128)(2,1)S(1)} %bitcast_select_fusion.refs_0_.refs_8_), channel_id=1, source_target_pairs={{0,3},{1,2},{2,1},{3,0},{4,7},{5,6},{6,5},{7,4},{8,11},{9,10},{10,... | collective-permute-start | bytes 1179656 | tf_op jit(solution)/shard_map/ppermute | solution.py:23
  38.3 15.4 %collective-permute-start.1 = (bf16[32,6144]{1,0:T(8,128)(2,1)}, bf16[32,6144]{1,0:T(8,128)(2,1)S(1)}, u32[]{:S(2)}, u32[]{:S(2)}) collective-permute-start(bf16[32,6144]{1,0:T(8,128)(2,1)} %collective-permute-done.refs_1_), channel_id=1, source_target_pairs={{0,3},{1,2},{2,1},{3,0},{4,7},{5,6},{6,5},{7,4},{8,11},{9,10},{10,... | collective-permute-start | bytes 1179656 | tf_op jit(solution)/shard_map/ppermute | solution.py:23
  45.0 12.8 %collective-permute-start.12 = (bf16[32,6144]{1,0:T(8,128)(2,1)S(1)}, bf16[32,6144]{1,0:T(8,128)(2,1)}, u32[]{:S(2)}, u32[]{:S(2)}) collective-permute-start(bf16[32,6144]{1,0:T(8,128)(2,1)S(1)} %collective-permute-done.8.refs_1_.refs_9_), channel_id=1, source_target_pairs={{0,4},{1,5},{2,6},{3,7},{4,0},{5,1},{6,2},{7,3},{8,12},{9,13},{10,... | collective-permute-start | bytes 1179656 | tf_op jit(solution)/shard_map/ppermute | solution.py:23
  45.2 16.7 %collective-permute-start.4 = (bf16[32,6144]{1,0:T(8,128)(2,1)S(1)}, bf16[32,6144]{1,0:T(8,128)(2,1)S(1)}, u32[]{:S(2)}, u32[]{:S(2)}) collective-permute-start(bf16[32,6144]{1,0:T(8,128)(2,1)S(1)} %collective-permute-done.3.refs_4_), channel_id=1, source_target_pairs={{0,1},{1,0},{2,3},{3,2},{4,5},{5,4},{6,7},{7,6},{8,9},{9,8},{10,11... | collective-permute-start | bytes 1179656 | tf_op jit(solution)/shard_map/ppermute | solution.py:23
  49.2 15.1 %collective-permute-start.6 = (bf16[32,6144]{1,0:T(8,128)(2,1)}, bf16[32,6144]{1,0:T(8,128)(2,1)}, u32[]{:S(2)}, u32[]{:S(2)}) collective-permute-start(bf16[32,6144]{1,0:T(8,128)(2,1)} %collective-permute-done.5.refs_7_), channel_id=1, source_target_pairs={{0,1},{1,0},{2,3},{3,2},{4,5},{5,4},{6,7},{7,6},{8,9},{9,8},{10,11... | collective-permute-start | bytes 1179656 | tf_op jit(solution)/shard_map/ppermute | solution.py:23
  51.3 25.0 %collective-permute-start.14 = (bf16[32,6144]{1,0:T(8,128)(2,1)}, bf16[32,6144]{1,0:T(8,128)(2,1)}, u32[]{:S(2)}, u32[]{:S(2)}) collective-permute-start(bf16[32,6144]{1,0:T(8,128)(2,1)} %collective-permute-done.11.refs_4_.refs_12_), channel_id=1, source_target_pairs={{0,3},{1,2},{2,1},{3,0},{4,7},{5,6},{6,5},{7,4},{8,11},{9,10},{10,... | collective-permute-start | bytes 1179656 | tf_op jit(solution)/shard_map/ppermute | solution.py:23
  53.6 22.6 %collective-permute-start.10 = (bf16[32,6144]{1,0:T(8,128)(2,1)}, bf16[32,6144]{1,0:T(8,128)(2,1)}, u32[]{:S(2)}, u32[]{:S(2)}) collective-permute-start(bf16[32,6144]{1,0:T(8,128)(2,1)} %collective-permute-done.9.refs_3_.refs_11_), channel_id=1, source_target_pairs={{0,1},{1,0},{2,3},{3,2},{4,5},{5,4},{6,7},{7,6},{8,9},{9,8},{10,11... | collective-permute-start | bytes 1179656 | tf_op jit(solution)/shard_map/ppermute | solution.py:23
  57.8 18.5 %collective-permute-start.13 = (bf16[32,6144]{1,0:T(8,128)(2,1)}, bf16[32,6144]{1,0:T(8,128)(2,1)}, u32[]{:S(2)}, u32[]{:S(2)}) collective-permute-start(bf16[32,6144]{1,0:T(8,128)(2,1)} %collective-permute-done.12.refs_5_.refs_13_), channel_id=1, source_target_pairs={{0,3},{1,2},{2,1},{3,0},{4,7},{5,6},{6,5},{7,4},{8,11},{9,10},{10,... | collective-permute-start | bytes 1179656 | tf_op jit(solution)/shard_map/ppermute | solution.py:23
  62.7 19.7 %collective-permute-start.15 = (bf16[2,256,384]{2,1,0:T(8,128)(2,1)}, bf16[2,256,384]{2,1,0:T(8,128)(2,1)}, u32[]{:S(2)}, u32[]{:S(2)}) collective-permute-start(bf16[2,256,384]{2,1,0:T(8,128)(2,1)} %pack.3), channel_id=1, source_target_pairs={{0,128},{8,136},{16,144},{24,152},{32,160},{40,168},{48,176},{56,1... | collective-permute-start | bytes 1179656 | tf_op jit(solution)/shard_map/ppermute | solution.py:33
  67.7 8.6 %copy-start.2 = (bf16[6144,384]{1,0:T(8,128)(2,1)S(1)}, bf16[6144,384]{1,0:T(8,128)(2,1)}, u32[]{:S(2)}) copy-start(bf16[6144,384]{1,0:T(8,128)(2,1)} %w_ref.3) | copy-start | bytes 14155780
  93.5 13.3 %collective-permute-start.18 = (bf16[8,192,768]{2,1,0:T(8,128)(2,1)S(1)}, bf16[8,192,768]{2,1,0:T(8,128)(2,1)S(1)}, u32[]{:S(2)}, u32[]{:S(2)}) collective-permute-start(bf16[8,192,768]{2,1,0:T(8,128)(2,1)S(1)} %get-tuple-element.40.refs_0_), channel_id=1, source_target_pairs={{0,8},{8,0},{16,24},{24,16},{32,40},{40,32},{48,56},{56,48},{64,72... | collective-permute-start | bytes 7077896 | tf_op jit(solution)/shard_map/ppermute | solution.py:33
  110.0 11.8 %collective-permute-start.22 = (bf16[32,6144]{1,0:T(8,128)(2,1)}, bf16[32,6144]{1,0:T(8,128)(2,1)S(1)}, u32[]{:S(2)}, u32[]{:S(2)}) collective-permute-start(bf16[32,6144]{1,0:T(8,128)(2,1)} %get-tuple-element.49), channel_id=1, source_target_pairs={{0,3},{1,2},{2,1},{3,0},{4,7},{5,6},{6,5},{7,4},{8,11},{9,10},{10,... | collective-permute-start | bytes 1179656 | tf_op jit(solution)/shard_map/ppermute | solution.py:23
  111.0 19.2 %collective-permute-start.17 = (bf16[32,6144]{1,0:T(8,128)(2,1)}, bf16[32,6144]{1,0:T(8,128)(2,1)S(1)}, u32[]{:S(2)}, u32[]{:S(2)}) collective-permute-start(bf16[32,6144]{1,0:T(8,128)(2,1)} %get-tuple-element.43), channel_id=1, source_target_pairs={{0,3},{1,2},{2,1},{3,0},{4,7},{5,6},{6,5},{7,4},{8,11},{9,10},{10,... | collective-permute-start | bytes 1179656 | tf_op jit(solution)/shard_map/ppermute | solution.py:23
  112.7 20.4 %collective-permute-start.20 = (bf16[32,6144]{1,0:T(8,128)(2,1)}, bf16[32,6144]{1,0:T(8,128)(2,1)S(1)}, u32[]{:S(2)}, u32[]{:S(2)}) collective-permute-start(bf16[32,6144]{1,0:T(8,128)(2,1)} %get-tuple-element.46), channel_id=1, source_target_pairs={{0,1},{1,0},{2,3},{3,2},{4,5},{5,4},{6,7},{7,6},{8,9},{9,8},{10,11... | collective-permute-start | bytes 1179656 | tf_op jit(solution)/shard_map/ppermute | solution.py:23
  121.8 6.7 %copy-start.24 = (bf16[2,256,384]{2,1,0:T(8,128)(2,1)S(1)}, bf16[2,256,384]{2,1,0:T(8,128)(2,1)}, u32[]{:S(2)}) copy-start(bf16[2,256,384]{2,1,0:T(8,128)(2,1)} %copy-done.23) | copy-start | bytes 1179652
  121.8 12.5 %collective-permute-start.23 = (bf16[32,6144]{1,0:T(8,128)(2,1)S(1)}, bf16[32,6144]{1,0:T(8,128)(2,1)S(1)}, u32[]{:S(2)}, u32[]{:S(2)}) collective-permute-start(bf16[32,6144]{1,0:T(8,128)(2,1)S(1)} %add.131), channel_id=1, source_target_pairs={{0,4},{1,5},{2,6},{3,7},{4,0},{5,1},{6,2},{7,3},{8,12},{9,13},{10,... | collective-permute-start | bytes 1179656 | tf_op jit(solution)/shard_map/ppermute | solution.py:23
  128.5 27.6 %collective-permute-start.32 = (bf16[2,256,384]{2,1,0:T(8,128)(2,1)S(1)}, bf16[2,256,384]{2,1,0:T(8,128)(2,1)S(1)}, u32[]{:S(2)}, u32[]{:S(2)}) collective-permute-start(bf16[2,256,384]{2,1,0:T(8,128)(2,1)S(1)} %copy-done.24), channel_id=1, source_target_pairs={{0,128},{8,136},{16,144},{24,152},{32,160},{40,168},{48,176},{56,1... | collective-permute-start | bytes 1179656 | tf_op jit(solution)/shard_map/ppermute | solution.py:33
  128.6 28.7 %collective-permute-start.16 = (bf16[32,6144]{1,0:T(8,128)(2,1)}, bf16[32,6144]{1,0:T(8,128)(2,1)S(1)}, u32[]{:S(2)}, u32[]{:S(2)}) collective-permute-start(bf16[32,6144]{1,0:T(8,128)(2,1)} %copy-done.33), channel_id=1, source_target_pairs={{0,1},{1,0},{2,3},{3,2},{4,5},{5,4},{6,7},{7,6},{8,9},{9,8},{10,11... | collective-permute-start | bytes 1179656 | tf_op jit(solution)/shard_map/ppermute | solution.py:23
  130.3 11.0 %collective-permute-start.19 = (bf16[32,6144]{1,0:T(8,128)(2,1)S(1)}, bf16[32,6144]{1,0:T(8,128)(2,1)S(1)}, u32[]{:S(2)}, u32[]{:S(2)}) collective-permute-start(bf16[32,6144]{1,0:T(8,128)(2,1)S(1)} %add.129), channel_id=1, source_target_pairs={{0,4},{1,5},{2,6},{3,7},{4,0},{5,1},{6,2},{7,3},{8,12},{9,13},{10,... | collective-permute-start | bytes 1179656 | tf_op jit(solution)/shard_map/ppermute | solution.py:23
  133.2 10.5 %collective-permute-start.21 = (bf16[32,6144]{1,0:T(8,128)(2,1)S(1)}, bf16[32,6144]{1,0:T(8,128)(2,1)S(1)}, u32[]{:S(2)}, u32[]{:S(2)}) collective-permute-start(bf16[32,6144]{1,0:T(8,128)(2,1)S(1)} %add.130), channel_id=1, source_target_pairs={{0,3},{1,2},{2,1},{3,0},{4,7},{5,6},{6,5},{7,4},{8,11},{9,10},{10,... | collective-permute-start | bytes 1179656 | tf_op jit(solution)/shard_map/ppermute | solution.py:23
  134.4 11.4 %collective-permute-start.24 = (bf16[32,6144]{1,0:T(8,128)(2,1)S(1)}, bf16[32,6144]{1,0:T(8,128)(2,1)S(1)}, u32[]{:S(2)}, u32[]{:S(2)}) collective-permute-start(bf16[32,6144]{1,0:T(8,128)(2,1)S(1)} %add.99), channel_id=1, source_target_pairs={{0,1},{1,0},{2,3},{3,2},{4,5},{5,4},{6,7},{7,6},{8,9},{9,8},{10,11... | collective-permute-start | bytes 1179656 | tf_op jit(solution)/shard_map/ppermute | solution.py:23
  134.6 6.7 %copy-start.32 = (bf16[32,6144]{1,0:T(8,128)(2,1)S(1)}, bf16[32,6144]{1,0:T(8,128)(2,1)}, u32[]{:S(2)}) copy-start(bf16[32,6144]{1,0:T(8,128)(2,1)} %copy-done.31) | copy-start | bytes 1179652
  134.6 9.1 %copy-start.35 = (bf16[32,6144]{1,0:T(8,128)(2,1)S(1)}, bf16[32,6144]{1,0:T(8,128)(2,1)}, u32[]{:S(2)}) copy-start(bf16[32,6144]{1,0:T(8,128)(2,1)} %copy-done.34) | copy-start | bytes 1179652
  135.4 19.6 %copy-start.22 = (bf16[32,6144]{1,0:T(8,128)(2,1)S(1)}, bf16[32,6144]{1,0:T(8,128)(2,1)}, u32[]{:S(2)}) copy-start(bf16[32,6144]{1,0:T(8,128)(2,1)} %copy-done.21) | copy-start | bytes 1179652
  141.3 19.0 %collective-permute-start.26 = (bf16[32,6144]{1,0:T(8,128)(2,1)S(1)}, bf16[32,6144]{1,0:T(8,128)(2,1)S(1)}, u32[]{:S(2)}, u32[]{:S(2)}) collective-permute-start(bf16[32,6144]{1,0:T(8,128)(2,1)S(1)} %copy-done.32), channel_id=1, source_target_pairs={{0,3},{1,2},{2,1},{3,0},{4,7},{5,6},{6,5},{7,4},{8,11},{9,10},{10,... | collective-permute-start | bytes 1179656 | tf_op jit(solution)/shard_map/ppermute | solution.py:23
  143.7 11.3 %collective-permute-start.28 = (bf16[32,6144]{1,0:T(8,128)(2,1)S(1)}, bf16[32,6144]{1,0:T(8,128)(2,1)S(1)}, u32[]{:S(2)}, u32[]{:S(2)}) collective-permute-start(bf16[32,6144]{1,0:T(8,128)(2,1)S(1)} %copy-done.35), channel_id=1, source_target_pairs={{0,1},{1,0},{2,3},{3,2},{4,5},{5,4},{6,7},{7,6},{8,9},{9,8},{10,11... | collective-permute-start | bytes 1179656 | tf_op jit(solution)/shard_map/ppermute | solution.py:23
  146.0 33.2 %collective-permute-start.31 = (bf16[32,6144]{1,0:T(8,128)(2,1)S(1)}, bf16[32,6144]{1,0:T(8,128)(2,1)S(1)}, u32[]{:S(2)}, u32[]{:S(2)}) collective-permute-start(bf16[32,6144]{1,0:T(8,128)(2,1)S(1)} %add_convert_fusion.refs_0_), channel_id=1, source_target_pairs={{0,128},{8,136},{16,144},{24,152},{32,160},{40,168},{48,176},{56,1... | collective-permute-start | bytes 1179656 | tf_op jit(solution)/shard_map/ppermute | solution.py:33
  155.1 9.4 %collective-permute-start.29 = (bf16[32,6144]{1,0:T(8,128)(2,1)S(1)}, bf16[32,6144]{1,0:T(8,128)(2,1)S(1)}, u32[]{:S(2)}, u32[]{:S(2)}) collective-permute-start(bf16[32,6144]{1,0:T(8,128)(2,1)S(1)} %add.134), channel_id=1, source_target_pairs={{0,4},{1,5},{2,6},{3,7},{4,0},{5,1},{6,2},{7,3},{8,12},{9,13},{10,... | collective-permute-start | bytes 1179656 | tf_op jit(solution)/shard_map/ppermute | solution.py:23
  157.3 7.2 %copy-start.16 = (bf16[32,6144]{1,0:T(8,128)(2,1)S(1)}, bf16[32,6144]{1,0:T(8,128)(2,1)}, u32[]{:S(2)}) copy-start(bf16[32,6144]{1,0:T(8,128)(2,1)} %copy-done.15) | copy-start | bytes 1179652
  157.4 23.2 %collective-permute-start.25 = (bf16[32,6144]{1,0:T(8,128)(2,1)S(1)}, bf16[32,6144]{1,0:T(8,128)(2,1)S(1)}, u32[]{:S(2)}, u32[]{:S(2)}) collective-permute-start(bf16[32,6144]{1,0:T(8,128)(2,1)S(1)} %add.132), channel_id=1, source_target_pairs={{0,4},{1,5},{2,6},{3,7},{4,0},{5,1},{6,2},{7,3},{8,12},{9,13},{10,... | collective-permute-start | bytes 1179656 | tf_op jit(solution)/shard_map/ppermute | solution.py:23
  160.3 20.3 %copy-start.12 = (bf16[32,6144]{1,0:T(8,128)(2,1)S(1)}, bf16[32,6144]{1,0:T(8,128)(2,1)}, u32[]{:S(2)}) copy-start(bf16[32,6144]{1,0:T(8,128)(2,1)} %copy-done.11) | copy-start | bytes 1179652
  160.4 20.3 %collective-permute-start.27 = (bf16[32,6144]{1,0:T(8,128)(2,1)S(1)}, bf16[32,6144]{1,0:T(8,128)(2,1)S(1)}, u32[]{:S(2)}, u32[]{:S(2)}) collective-permute-start(bf16[32,6144]{1,0:T(8,128)(2,1)S(1)} %add.133), channel_id=1, source_target_pairs={{0,1},{1,0},{2,3},{3,2},{4,5},{5,4},{6,7},{7,6},{8,9},{9,8},{10,11... | collective-permute-start | bytes 1179656 | tf_op jit(solution)/shard_map/ppermute | solution.py:23
  165.4 15.3 %collective-permute-start.30 = (bf16[32,6144]{1,0:T(8,128)(2,1)}, bf16[32,6144]{1,0:T(8,128)(2,1)S(1)}, u32[]{:S(2)}, u32[]{:S(2)}) collective-permute-start(bf16[32,6144]{1,0:T(8,128)(2,1)} %add.101), channel_id=1, source_target_pairs={{0,3},{1,2},{2,1},{3,0},{4,7},{5,6},{6,5},{7,4},{8,11},{9,10},{10,... | collective-permute-start | bytes 1179656 | tf_op jit(solution)/shard_map/ppermute | solution.py:23
  180.3 4.1 %collective-permute-start.33 = (bf16[192,384]{1,0:T(8,128)(2,1)S(1)}, bf16[192,384]{1,0:T(8,128)(2,1)S(1)}, u32[]{:S(2)}, u32[]{:S(2)}) collective-permute-start(bf16[192,384]{1,0:T(8,128)(2,1)S(1)} %dynamic-slice_bitcast_fusion.1), channel_id=1, source_target_pairs={{0,16},{8,24},{16,0},{24,8},{32,48},{40,56},{48,32},{56,40},{64,80... | collective-permute-start | bytes 442376 | tf_op jit(solution)/shard_map/ppermute | solution.py:33
  184.5 4.8 %collective-permute-start.34 = (f32[192,192]{0,1:T(8,128)S(1)}, f32[192,192]{0,1:T(8,128)S(1)}, u32[]{:S(2)}, u32[]{:S(2)}) collective-permute-start(f32[192,192]{0,1:T(8,128)S(1)} %dynamic-slice_bitcast_fusion), channel_id=1, source_target_pairs={{0,8},{8,0},{16,24},{24,16},{32,40},{40,32},{48,56},{56,48},{64,72... | collective-permute-start | bytes 442376 | tf_op jit(solution)/shard_map/ppermute | solution.py:33
  (25 other events, 64.8 us)
Sparse Core Ops, SparseCore 0:
  110.1 60.1 reduce-scatter.1
